TPU v7x, 32 devices: a whole 2x2x4 slice. The times are simulated.
32 devices in a mesh: groups: 2 (over x), seq: 16 (over z, y, core).
Axes of the slice: x: 2, y: 2, z: 4, core: 2. Of those that a mesh axis runs over, the one named last changes fastest.
Arguments:
- hidden_states: bfloat16 [37, 512, 2560], P(None, ('groups', 'seq')), parts along dimension 1, may hold values from -80 to 80
- layer_mix: float32 [37], replicated, may hold values from 0.05 to 1
- norm_gain: float32 [2560], replicated, may hold values from 0.1 to 1.9
- norm_bias: float32 [2560], replicated, may hold values from -3 to 3
- proj_in: bfloat16 [2560, 1024], replicated, may hold values from -0.125 to 0.125
- proj_in_bias: float32 [1024], replicated, may hold values from -3 to 3
- proj_out: bfloat16 [1024, 1024], replicated, may hold values from -0.1875 to 0.1875
- proj_out_bias: float32 [1024], replicated, may hold values from -3 to 3
- residue_tokens: int32 [512], P(('groups', 'seq')), parts along dimension 0, may hold values from 0 to 22
- residue_table: float32 [23, 1024], replicated, may hold values from -5 to 5
- pair_norm_gain: float32 [1024], replicated, may hold values from 0.1 to 1.9
- pair_norm_bias: float32 [1024], replicated, may hold values from -3 to 3
- qk_weight: bfloat16 [1024, 128], replicated, may hold values from -0.1875 to 0.1875
- qk_bias: float32 [128], replicated, may hold values from -3 to 3
- pair_weight: bfloat16 [128, 128], replicated, may hold values from -0.75 to 0.75
- relpos_bins: int32 [512, 256], P(('groups', 'seq')), parts along dimension 0, may hold values from 0 to 65
- relpos_table: float32 [66, 128], replicated, may hold values from -5 to 5
- chain_ids: int32 [512], P(('groups', 'seq')), parts along dimension 0, may hold values from 0 to 7, never falling along the last dimension, each value on 1 to 64 neighbouring positions
- chain_table: float32 [2, 128], replicated, may hold values from -5 to 5
Outputs:
- single: bfloat16 [512, 1024], P(('groups', 'seq')), parts along dimension 0
- pair: bfloat16 [512, 256, 128], P(('groups', 'seq')), parts along dimension 0
There are 2 independent parts, one for each index of `groups`. A program takes and returns all parts, laid end to end along the dimension named above; an argument that names none is the same for every part. Nothing has to cross between parts.
Inputs may be any that keep to these rules, and one draw needn't show every extreme that they name: `chain_ids`: chain numbers never fall along the residues; each chain has at most 64 residues.
All inputs are finite; a program needn't handle non-finite values.
Results may differ from a plain program's by a relative error of at most 0.0067.
Values may be sent and summed in bfloat16 or wider, within the bound.
No kernel may reach another device: no remote copies, remote signals or barrier semaphores. Data moves between devices by JAX's collectives and lax.ppermute only.
A program may use at most 64 MiB of HBM per device.

v0:
```python
import jax
import jax.numpy as jnp
from jax import lax
from jax.sharding import PartitionSpec as P

epsilon = 1e-05


def layer_norm(values, weight_gain, weight_bias):
    center = values - jnp.mean(values, axis=-1, keepdims=True)
    spread = jnp.mean(center * center, axis=-1, keepdims=True)
    return center * lax.rsqrt(spread + epsilon) * weight_gain + weight_bias


def single_path(
    mixture,
    norm_gain,
    norm_bias,
    proj_in,
    proj_in_bias,
    proj_out,
    proj_out_bias,
    residue_tokens,
    residue_table,
    pair_norm_gain,
    pair_norm_bias,
    qk_weight,
    qk_bias,
    pair_weight,
):
    normed = layer_norm(mixture, norm_gain, norm_bias).astype(jnp.bfloat16)
    hidden = jax.nn.relu(
        jnp.dot(normed, proj_in, preferred_element_type=jnp.float32) + proj_in_bias
    ).astype(jnp.bfloat16)
    onehot = (
        residue_tokens[:, None] == jnp.arange(residue_table.shape[0], dtype=jnp.int32)[None, :]
    ).astype(jnp.float32)
    residue_term = jnp.dot(onehot, residue_table, precision=lax.Precision.HIGHEST)
    single_f = (
        jnp.dot(hidden, proj_out, preferred_element_type=jnp.float32) + proj_out_bias + residue_term
    )
    pair_in = layer_norm(single_f, pair_norm_gain, pair_norm_bias).astype(jnp.bfloat16)
    query_key = jnp.dot(pair_in, qk_weight, preferred_element_type=jnp.float32) + qk_bias
    inner_dim = pair_weight.shape[0] // 2
    queries = query_key[:, :inner_dim].astype(jnp.bfloat16)
    key_rows = query_key[:, inner_dim:].astype(jnp.bfloat16)
    row_diff = jnp.dot(queries, pair_weight[inner_dim:], preferred_element_type=jnp.float32)
    return (single_f, queries, key_rows, row_diff)


def pair_tile(
    queries,
    row_diff,
    row_chain,
    key_rows,
    col_diff,
    col_chain,
    bin_block,
    pair_weight,
    relpos_table,
    chain_table,
):
    inner_dim = queries.shape[1]
    row_count = queries.shape[0]
    col_count = key_rows.shape[0]
    products = (
        queries[:, None, :].astype(jnp.float32) * key_rows[None, :, :].astype(jnp.float32)
    ).astype(jnp.bfloat16)
    product_term = jnp.dot(
        products.reshape(row_count * col_count, inner_dim),
        pair_weight[:inner_dim],
        preferred_element_type=jnp.float32,
    )
    product_term = product_term.reshape(row_count, col_count, -1)
    onehot = (
        bin_block[:, :, None] == jnp.arange(relpos_table.shape[0], dtype=jnp.int32)[None, None, :]
    ).astype(jnp.float32)
    relpos = jnp.einsum("ijb,bc->ijc", onehot, relpos_table, precision=lax.Precision.HIGHEST)
    same_chain = (row_chain[:, None] == col_chain[None, :])[:, :, None]
    chain_term = jnp.where(same_chain, chain_table[1][None, None, :], chain_table[0][None, None, :])
    summed = product_term + row_diff[:, None, :] - col_diff[None, :, :] + relpos + chain_term
    return summed.astype(jnp.bfloat16)


def shards(
    hidden_states,
    layer_mix,
    norm_gain,
    norm_bias,
    proj_in,
    proj_in_bias,
    proj_out,
    proj_out_bias,
    residue_tokens,
    residue_table,
    pair_norm_gain,
    pair_norm_bias,
    qk_weight,
    qk_bias,
    pair_weight,
    relpos_bins,
    relpos_table,
    chain_ids,
    chain_table,
):
    mixture = jnp.sum(layer_mix[:, None, None] * hidden_states.astype(jnp.float32), axis=0)
    single_f, queries, key_rows, row_diff = single_path(
        mixture,
        norm_gain,
        norm_bias,
        proj_in,
        proj_in_bias,
        proj_out,
        proj_out_bias,
        residue_tokens,
        residue_table,
        pair_norm_gain,
        pair_norm_bias,
        qk_weight,
        qk_bias,
        pair_weight,
    )
    tok_count = key_rows.shape[0]
    inner_dim = key_rows.shape[1]
    key_pairs = key_rows.reshape(tok_count // 2, 2 * inner_dim)
    chain_pairs = chain_ids.reshape(tok_count // 2, 2)
    key_piece = lax.all_gather(key_pairs, "seq", axis=0, tiled=True)
    chain_piece = lax.all_gather(chain_pairs, "seq", axis=0, tiled=True)
    key_cols = key_piece.reshape(-1, inner_dim)
    diff_cols = jnp.dot(key_cols, pair_weight[inner_dim:], preferred_element_type=jnp.float32)
    tile_value = pair_tile(
        queries,
        row_diff,
        chain_ids,
        key_cols,
        diff_cols,
        chain_piece.reshape(-1),
        relpos_bins,
        pair_weight,
        relpos_table,
        chain_table,
    )
    return (single_f.astype(jnp.bfloat16), tile_value)


def solution(mesh):
    in_specs = (
        P(None, ("groups", "seq"), None),
        P(),
        P(),
        P(),
        P(),
        P(),
        P(),
        P(),
        P(("groups", "seq")),
        P(),
        P(),
        P(),
        P(),
        P(),
        P(),
        P(("groups", "seq"), None),
        P(),
        P(("groups", "seq")),
        P(),
    )
    out_specs = (P(("groups", "seq"), None), P(("groups", "seq"), None, None))
    return jax.shard_map(shards, mesh=mesh, in_specs=in_specs, out_specs=out_specs, check_vma=False)
```

profile of v0, /device:TPU:0, one launch (start us, length us, event | category | flops | bytes accessed | tf_op | source)
XLA Modules:
  0.0 56.9 jit_solution(13759519168361682082)
XLA Ops:
  0.6 0.0 copy-start
  0.6 0.0 copy-start.5
  0.7 0.0 copy-start.6
  0.7 0.0 copy-start.3
  0.7 0.0 copy-start.4
  0.7 0.8 %slice_bitcast_fusion.1 = (f32[128]{0:T(128)S(1)}, f32[128]{0:T(128)S(1)}) fusion(f32[2,128]{1,0:T(2,128)} %param.37), kind=kLoop, calls=%fused_computation.44 | loop fusion | bytes 2048 | tf_op jit(solution)/shard_map/jit(_where)/broadcast_in_dim | solution.py:80
  1.5 0.7 %reshape.95 = s32[1,8,2]{2,1,0:T(8,128)S(1)} reshape(s32[16]{0:T(128)} %param.36) | data formatting | bytes 128
  2.3 0.1 copy.27
  2.3 23.1 %all-gather = s32[16,8,2]{1,2,0:T(2,128)S(1)} all-gather(s32[1,8,2]{1,2,0:T(2,128)S(1)} %copy.27), channel_id=1, replica_groups=mesh['groups'=2,'seq'=16] {'seq'}, dimensions={0}, use_global_device_ids=true | all-gather | bytes 1088 | tf_op jit(solution)/shard_map/all_gather | solution.py:128
  25.4 0.2 copy.28
  25.6 0.1 eq.52
  25.7 0.7 %broadcast_compare_fusion = pred[16,256]{1,0:T(8,128)(4,1)S(1)} fusion(s32[256]{0:T(256)S(1)} %eq.52, s32[16]{0:T(128)} %param.36), kind=kLoop, calls=%fused_computation.38 | loop fusion | flops 4096 | bytes 5184 | tf_op jit(solution)/shard_map/eq | solution.py:79
  26.5 3.0 %fusion = (f32[16]{0:T(128)S(1)}, f32[16,2560]{1,0:T(8,128)S(1)}) fusion(bf16[37,16,2560]{2,1,0:T(8,128)(2,1)} %param.19, f32[37]{0:T(128)} %param.20), kind=kLoop, calls=%fused_computation.1 | loop fusion | flops 6021104 | bytes 3195092 | tf_op jit(solution)/shard_map/reduce_sum | solution.py:10
  29.5 0.2 multiply_reduce_fusion
  29.7 0.0 copy-done
  29.7 0.0 copy-done.5
  29.7 0.0 copy-done.6
  29.7 0.0 copy-done.3
  29.7 0.0 copy-done.4
  29.7 0.0 copy-start.1
  29.8 0.0 copy-start.7
  29.8 0.0 copy-start.8
  29.8 0.0 copy-start.11
  29.8 0.0 copy-start.12
  29.8 0.0 copy-start.13
  29.8 0.0 copy-start.2
  29.8 3.7 %convolution_add_fusion.1 = f32[16,1024]{1,0:T(8,128)S(1)} fusion(bf16[1024,1024]{1,0:T(8,128)(2,1)S(1)} %copy-done, bf16[2560,1024]{1,0:T(8,128)(2,1)} %param.23, f32[16,2560]{1,0:T(8,128)S(1)} %get-tuple-element.3, f32[2560]{0:T(1024)S(1)} %copy-done.3, f32[2560]{0:T(1024)S(1)} %copy-done.4, f32[16]{0:T(128)S(1)} %add_rsqrt_fusion.1, ...), kind=kOutput, calls=%fused_computation.6 | convolution fusion | flops 117710848 | bytes 7598208 | tf_op jit(solution)/shard_map/dot_general | solution.py:40
  33.6 0.0 copy-done.1
  33.6 0.0 copy-done.7
  33.6 0.0 copy-start.9
  33.6 0.0 copy-start.10
  33.6 0.3 fusion.33
  33.9 0.7 %multiply_reduce_fusion.1 = (f32[16]{0:T(128)S(1)}, bf16[16,1024]{1,0:T(8,128)(2,1)}) fusion(f32[16,1024]{1,0:T(8,128)S(1)} %get-tuple-element.11, f32[16]{0:T(128)S(1)} %broadcast_multiply_fusion), kind=kLoop, calls=%fused_computation.24 | loop fusion | flops 65520 | bytes 98432 | tf_op jit(solution)/shard_map/reduce_sum | solution.py:11
  34.7 0.0 copy-done.8
  34.7 0.0 copy-done.11
  34.7 0.0 copy-done.12
  34.7 0.0 copy-done.13
  34.7 0.2 fusion.4
  34.9 0.0 copy-done.2
  34.9 0.1 fusion.28
  35.1 0.1 slice_convert_fusion
  35.1 0.1 reshape.93
  35.2 17.5 %all_gather.6 = bf16[128,128]{1,0:T(8,128)(2,1)S(1)} all-gather(bf16[8,128]{1,0:T(8,128)(2,1)S(1)} %reshape.93), channel_id=1, replica_groups=mesh['groups'=2,'seq'=16] {'seq'}, dimensions={0}, use_global_device_ids=true | all-gather | bytes 34816 | tf_op jit(solution)/shard_map/all_gather | solution.py:127
  52.7 0.1 broadcast_in_dim_reshape.4
  52.8 0.1 copy.26
  52.9 0.1 fusion.26
  53.0 0.7 %fusion.6 = f32[16,256,128]{2,1,0:T(8,128)S(1)} fusion(f32[256,64]{0,1:T(8,128)S(1)} %copy.26, f32[16,64]{1,0:T(8,128)S(1)} %get-tuple-element.6, bf16[128,128]{1,0:T(8,128)(2,1)S(1)} %copy-done.2), kind=kOutput, calls=%fused_computation.14 | convolution fusion | flops 67633152 | bytes 2187264 | tf_op jit(solution)/shard_map/dot_general | solution.py:69
  53.7 0.0 copy-done.9
  53.7 0.0 copy-done.10
  53.7 3.2 %add_convert_fusion = bf16[16,256,128]{2,1,0:T(8,128)(2,1)} fusion(f32[16,256,128]{2,1,0:T(8,128)S(1)} %fusion.6, f32[128]{0:T(128)S(1)} %get-tuple-element.9, f32[128]{0:T(128)S(1)} %get-tuple-element.8, f32[256,128]{1,0:T(8,128)S(1)} %fusion.26, f32[16,128]{1,0:T(8,128)S(1)} %fusion.28, pred[16,256]{1,0:T(8,128)(4,1)S(1)} %broadcast_compare_fusion, ...), kind=kOutput, calls=%fused_computation.3 | convolution fusion | flops 418652160 | bytes 3340288 | tf_op jit(solution)/shard_map/ijb,bc->ijc/dot_general | solution.py:78
  (4 shorter events, 0.0 us)
Async XLA Ops:
  0.6 29.1 %copy-start = (bf16[1024,1024]{1,0:T(8,128)(2,1)S(1)}, bf16[1024,1024]{1,0:T(8,128)(2,1)}, u32[]{:S(2)}) copy-start(bf16[1024,1024]{1,0:T(8,128)(2,1)} %param.25) | copy-start | bytes 6291460
  0.6 29.1 %copy-start.5 = (f32[1024]{0:T(1024)S(1)}, f32[1024]{0:T(1024)}, u32[]{:S(2)}) copy-start(f32[1024]{0:T(1024)} %param.26) | copy-start | bytes 12292
  0.7 29.1 %copy-start.6 = (f32[1024]{0:T(1024)S(1)}, f32[1024]{0:T(1024)}, u32[]{:S(2)}) copy-start(f32[1024]{0:T(1024)} %param.24) | copy-start | bytes 12292
  0.7 29.1 %copy-start.3 = (f32[2560]{0:T(1024)S(1)}, f32[2560]{0:T(1024)}, u32[]{:S(2)}) copy-start(f32[2560]{0:T(1024)} %param.22) | copy-start | bytes 30724
  0.7 29.1 %copy-start.4 = (f32[2560]{0:T(1024)S(1)}, f32[2560]{0:T(1024)}, u32[]{:S(2)}) copy-start(f32[2560]{0:T(1024)} %param.21) | copy-start | bytes 30724
  29.7 3.8 %copy-start.1 = (f32[23,1024]{1,0:T(8,128)S(1)}, f32[23,1024]{1,0:T(8,128)}, u32[]{:S(2)}) copy-start(f32[23,1024]{1,0:T(8,128)} %param.28) | copy-start | bytes 282628
  29.8 3.8 %copy-start.7 = (s32[16]{0:T(128)S(1)}, s32[16]{0:T(128)}, u32[]{:S(2)}) copy-start(s32[16]{0:T(128)} %param.27) | copy-start | bytes 196
  29.8 4.9 %copy-start.8 = (bf16[1024,128]{1,0:T(8,128)(2,1)S(1)}, bf16[1024,128]{1,0:T(8,128)(2,1)}, u32[]{:S(2)}) copy-start(bf16[1024,128]{1,0:T(8,128)(2,1)} %param.31) | copy-start | bytes 786436
  29.8 4.9 %copy-start.11 = (f32[1024]{0:T(1024)S(1)}, f32[1024]{0:T(1024)}, u32[]{:S(2)}) copy-start(f32[1024]{0:T(1024)} %param.30) | copy-start | bytes 12292
  29.8 4.9 %copy-start.12 = (f32[1024]{0:T(1024)S(1)}, f32[1024]{0:T(1024)}, u32[]{:S(2)}) copy-start(f32[1024]{0:T(1024)} %param.29) | copy-start | bytes 12292
  29.8 4.9 %copy-start.13 = (f32[128]{0:T(128)S(1)}, f32[128]{0:T(128)}, u32[]{:S(2)}) copy-start(f32[128]{0:T(128)} %param.32) | copy-start | bytes 1540
  29.8 5.1 %copy-start.2 = (bf16[128,128]{1,0:T(8,128)(2,1)S(1)}, bf16[128,128]{1,0:T(8,128)(2,1)}, u32[]{:S(2)}) copy-start(bf16[128,128]{1,0:T(8,128)(2,1)} %param.33) | copy-start | bytes 98308
  33.6 20.1 %copy-start.9 = (f32[66,128]{1,0:T(8,128)S(1)}, f32[66,128]{1,0:T(8,128)}, u32[]{:S(2)}) copy-start(f32[66,128]{1,0:T(8,128)} %param.35) | copy-start | bytes 101380
  33.6 20.1 %copy-start.10 = (s32[16,256]{1,0:T(8,128)S(1)}, s32[16,256]{1,0:T(8,128)}, u32[]{:S(2)}) copy-start(s32[16,256]{1,0:T(8,128)} %param.34) | copy-start | bytes 49156
where the time goes:
time: 57.2 us; the launch traced here: 56.9 us
  blocking collectives  40.6 us (71%)
  matrix products  8.4 us (15%)
  other arithmetic  4.78 us (8%)
  local copies, waits for them, and re-layouts  2.31 us (4%)
  between operations  0.88 us (2%)
    all_gather x1, blocking collectives, shards(): chain_piece = lax.all_gather(chain_pairs, 'seq', axis=0, tiled=True)  23.1 us
    all_gather x1, blocking collectives, shards(): key_piece = lax.all_gather(key_pairs, 'seq', axis=0, tiled=True)  17.5 us
    dot_general x1, matrix products, single_path(): jnp.dot(hidden, proj_out, preferred_element_type=jnp.float32)  3.73 us
    dot_general x1, matrix products, pair_tile(): jnp.einsum('ijb,bc->ijc', onehot, relpos_table, precision=lax.Precision.H...  3.2 us
    reduce_sum x1, other arithmetic, layer_norm(): center = values - jnp.mean(values, axis=-1, keepdims=True)  3 us

commit v1 on v0

--- a/solution.py
+++ b/solution.py
@@ -122,11 +122,22 @@
     )
     tok_count = key_rows.shape[0]
     inner_dim = key_rows.shape[1]
-    key_pairs = key_rows.reshape(tok_count // 2, 2 * inner_dim)
-    chain_pairs = chain_ids.reshape(tok_count // 2, 2)
-    key_piece = lax.all_gather(key_pairs, "seq", axis=0, tiled=True)
-    chain_piece = lax.all_gather(chain_pairs, "seq", axis=0, tiled=True)
-    key_cols = key_piece.reshape(-1, inner_dim)
+    device_count = lax.axis_size("seq")
+    lane_pad = pair_weight.shape[1] - inner_dim - 1
+    block = jnp.concatenate(
+        [
+            key_rows,
+            chain_ids.astype(jnp.bfloat16)[:, None],
+            jnp.zeros((tok_count, lane_pad), jnp.bfloat16),
+        ],
+        axis=1,
+    )
+    copies = jnp.broadcast_to(block[None], (device_count,) + block.shape)
+    blocks = lax.all_to_all(copies, "seq", split_axis=0, concat_axis=0).reshape(
+        device_count * tok_count, -1
+    )
+    key_cols = blocks[:, :inner_dim]
+    col_chain = blocks[:, inner_dim].astype(jnp.int32)
     diff_cols = jnp.dot(key_cols, pair_weight[inner_dim:], preferred_element_type=jnp.float32)
     tile_value = pair_tile(
         queries,
@@ -134,7 +145,7 @@
         chain_ids,
         key_cols,
         diff_cols,
-        chain_piece.reshape(-1),
+        col_chain,
         relpos_bins,
         pair_weight,
         relpos_table,

time: 57.2 us -> 29.9 us (0.52)
  blocking collectives: 40.6 us -> 0 us
  starting transfers between devices: 0 us -> 7.38 us
  waiting for transfers between devices: 0 us -> 6.76 us
  local copies, waits for them, and re-layouts: 2.31 us -> 1.02 us
    all_gather x2 -> x0, blocking collectives: 40.6 us -> none  [the longest x1 23.1 us: shards(): chain_piece = lax.all_gather(chain_pairs, 'seq', axis=0, tiled=True)]
    all_to_all x0 -> x1, starting transfers between devices: none -> 7.38 us  [shards(): lax.all_to_all(copies, 'seq', split_axis=0, concat_axis=0)]
    all_to_all x0 -> x1, waiting for transfers between devices: none -> 6.76 us  [shards(): lax.all_to_all(copies, 'seq', split_axis=0, concat_axis=0)]
    broadcast_in_dim x1, local copies, waits for them, and re-layouts: 0.84 us -> 0.01 us  [pair_tile(): jnp.where(same_chain, chain_table[1][None, None, :], chain_table[0][None,...]
    broadcast_in_dim x0 -> x1, other arithmetic: none -> 0.8 us  [shards(): chain_ids.astype(jnp.bfloat16)[:, None]]
    broadcast_in_dim x0 -> x3, local copies, waits for them, and re-layouts: none -> 0.75 us  [the longest x1 0.65 us: shards(): copies = jnp.broadcast_to(block[None], (device_count,) + block.shape)]
    unnamed x30 -> x33, local copies, waits for them, and re-layouts: 0.9 us -> 0.19 us
    eq x1, other arithmetic: 0.73 us -> 0.07 us  [pair_tile(): same_chain = (row_chain[:, None] == col_chain[None, :])[:, :, None]]
  transfers between devices with their start and end apart: 0 -> 1, of which waited for: 0 -> 1; matrix products, arithmetic and copies ran while one was open for 0% -> 0% of each run, Pallas kernels for 0% -> 0%
where the time goes in v1:
time: 29.9 us; the launch traced here: 29.7 us
  matrix products  8.4 us (28%)
  starting transfers between devices  7.38 us (25%)
  waiting for transfers between devices  6.76 us (23%)
  other arithmetic  5.19 us (17%)
  local copies, waits for them, and re-layouts  1.02 us (3%)
  between operations  0.92 us (3%)
    all_to_all x1, starting transfers between devices, shards(): lax.all_to_all(copies, 'seq', split_axis=0, concat_axis=0)  7.38 us
    all_to_all x1, waiting for transfers between devices, shards(): lax.all_to_all(copies, 'seq', split_axis=0, concat_axis=0)  6.76 us
    dot_general x1, matrix products, single_path(): jnp.dot(hidden, proj_out, preferred_element_type=jnp.float32)  3.73 us
    dot_general x1, matrix products, pair_tile(): jnp.einsum('ijb,bc->ijc', onehot, relpos_table, precision=lax.Precision.H...  3.2 us
    reduce_sum x1, other arithmetic, layer_norm(): center = values - jnp.mean(values, axis=-1, keepdims=True)  3 us
    reduce_sum x2, other arithmetic, layer_norm(): spread = jnp.mean(center * center, axis=-1, keepdims=True)  0.95 us
    broadcast_in_dim x1, other arithmetic, shards(): chain_ids.astype(jnp.bfloat16)[:, None]  0.8 us
    dot_general x1, matrix products, pair_tile(): jnp.dot(products.reshape(row_count * col_count, inner_dim), pair_weight[:...  0.68 us
  transfers between devices with their start and end apart: 1, of which 1 were waited for; matrix products, arithmetic and copies ran while one was open for 0% of the time, Pallas kernels for 0%

profile of v1, /device:TPU:0, one launch (start us, length us, event | category | flops | bytes accessed | tf_op | source)
XLA Modules:
  0.0 29.7 jit_solution(3412565355992778459)
XLA Ops:
  0.6 0.0 copy-start
  0.6 0.0 copy-start.5
  0.7 0.0 copy-start.6
  0.7 0.0 copy-start.3
  0.7 0.0 copy-start.4
  0.7 0.8 %convert_bitcast_fusion = bf16[16,1]{0,1:T(2,128)(2,1)S(1)} fusion(s32[16]{0:T(128)} %param.36), kind=kLoop, calls=%fused_computation.47 | loop fusion | flops 16 | bytes 96 | tf_op jit(solution)/shard_map/broadcast_in_dim | solution.py:130
  1.5 0.1 copy.29
  1.6 3.0 %fusion = (f32[16]{0:T(128)S(1)}, f32[16,2560]{1,0:T(8,128)S(1)}) fusion(bf16[37,16,2560]{2,1,0:T(8,128)(2,1)} %param.19, f32[37]{0:T(128)} %param.20), kind=kLoop, calls=%fused_computation.1 | loop fusion | flops 6021104 | bytes 3195092 | tf_op jit(solution)/shard_map/reduce_sum | solution.py:10
  4.6 0.2 multiply_reduce_fusion
  4.8 0.0 copy-done
  4.8 0.0 copy-done.5
  4.8 0.0 copy-done.6
  4.8 0.0 copy-done.3
  4.9 0.0 copy-done.4
  4.9 0.0 copy-start.1
  4.9 0.0 copy-start.8
  4.9 0.0 copy-start.10
  4.9 0.0 copy-start.13
  4.9 0.0 copy-start.14
  4.9 0.0 copy-start.15
  4.9 0.0 copy-start.2
  4.9 0.0 copy-start.7
  5.0 0.0 copy-start.9
  5.0 3.7 %convolution_add_fusion.1 = f32[16,1024]{1,0:T(8,128)S(1)} fusion(bf16[1024,1024]{1,0:T(8,128)(2,1)S(1)} %copy-done, bf16[2560,1024]{1,0:T(8,128)(2,1)} %param.23, f32[16,2560]{1,0:T(8,128)S(1)} %get-tuple-element.3, f32[2560]{0:T(1024)S(1)} %copy-done.3, f32[2560]{0:T(1024)S(1)} %copy-done.4, f32[16]{0:T(128)S(1)} %add_rsqrt_fusion.1, ...), kind=kOutput, calls=%fused_computation.6 | convolution fusion | flops 117710848 | bytes 7598208 | tf_op jit(solution)/shard_map/dot_general | solution.py:40
  8.7 0.0 copy-done.1
  8.7 0.0 copy-done.8
  8.7 0.0 copy-start.11
  8.7 0.0 copy-start.12
  8.7 0.3 %fusion.34 = (f32[16]{0:T(128)S(1)}, f32[16,1024]{1,0:T(8,128)S(1)}) fusion(f32[16,1024]{1,0:T(8,128)S(1)} %convolution_add_fusion.1, f32[23,1024]{1,0:T(8,128)S(1)} %copy-done.1, s32[16]{0:T(128)S(1)} %copy-done.8), kind=kOutput, calls=%fused_computation.54 | convolution fusion | flops 4555104 | bytes 225408 | tf_op jit(solution)/shard_map/dot_general | solution.py:38
  9.1 0.7 %multiply_reduce_fusion.1 = (f32[16]{0:T(128)S(1)}, bf16[16,1024]{1,0:T(8,128)(2,1)}) fusion(f32[16,1024]{1,0:T(8,128)S(1)} %get-tuple-element.11, f32[16]{0:T(128)S(1)} %broadcast_multiply_fusion), kind=kLoop, calls=%fused_computation.25 | loop fusion | flops 65520 | bytes 98432 | tf_op jit(solution)/shard_map/reduce_sum | solution.py:11
  9.8 0.0 copy-done.10
  9.8 0.0 copy-done.13
  9.8 0.0 copy-done.14
  9.9 0.0 copy-done.15
  9.9 0.2 fusion.4
  10.1 0.1 slice_convert_fusion
  10.2 0.1 pad.2.clone
  10.2 0.1 maximum_maximum_fusion
  10.3 0.7 %broadcast_in_dim.27 = bf16[16,16,128]{2,1,0:T(8,128)(2,1)} broadcast(bf16[16,128]{1,0:T(8,128)(2,1)S(1)} %maximum_maximum_fusion), dimensions={1,2} | broadcast | bytes 69632 | tf_op jit(solution)/shard_map/broadcast_in_dim | solution.py:135
  11.0 7.4 %all-to-all-start = ((bf16[16,16,128]{2,1,0:T(8,128)(2,1)}), bf16[16,16,128]{2,1,0:T(8,128)(2,1)S(1)}, u32[]{:S(2)}, u32[]{:S(2)}) async-start(bf16[16,16,128]{2,1,0:T(8,128)(2,1)} %broadcast_in_dim.27), calls=%async_computation | async-start | bytes 131072 | tf_op jit(solution)/shard_map/all_to_all | solution.py:136
  18.4 0.0 copy-done.2
  18.4 0.1 fusion.28
  18.5 0.0 copy-done.7
  18.5 6.8 %all-to-all-done = bf16[16,16,128]{2,1,0:T(8,128)(2,1)S(1)} async-done(((bf16[16,16,128]{2,1,0:T(8,128)(2,1)}), bf16[16,16,128]{2,1,0:T(8,128)(2,1)S(1)}, u32[]{:S(2)}, u32[]{:S(2)}) %all-to-all-start) | async-done | bytes 65568 | tf_op jit(solution)/shard_map/all_to_all | solution.py:136
  25.3 0.2 convert_reduce_fusion
  25.4 0.1 fusion.26
  25.6 0.0 copy-done.9
  25.6 0.1 broadcast_compare_fusion
  25.7 0.1 copy.31
  25.8 0.7 %fusion.6 = f32[16,256,128]{2,1,0:T(8,128)S(1)} fusion(f32[256,64]{0,1:T(8,128)S(1)} %convert_element_type.55, f32[16,64]{1,0:T(8,128)S(1)} %get-tuple-element.6, bf16[128,128]{1,0:T(8,128)(2,1)S(1)} %copy-done.2), kind=kOutput, calls=%fused_computation.14 | convolution fusion | flops 67633152 | bytes 2187264 | tf_op jit(solution)/shard_map/dot_general | solution.py:69
  26.5 0.0 copy-done.11
  26.5 0.0 copy-done.12
  26.5 3.2 %add_convert_fusion = bf16[16,256,128]{2,1,0:T(8,128)(2,1)} fusion(f32[16,256,128]{2,1,0:T(8,128)S(1)} %fusion.6, f32[128]{0:T(128)S(1)} %get-tuple-element.9, f32[128]{0:T(128)S(1)} %get-tuple-element.8, f32[256,128]{1,0:T(8,128)S(1)} %fusion.26, f32[16,128]{1,0:T(8,128)S(1)} %fusion.28, pred[16,256]{1,0:T(8,128)(4,1)S(1)} %broadcast_compare_fusion, ...), kind=kOutput, calls=%fused_computation.3 | convolution fusion | flops 418652160 | bytes 3340288 | tf_op jit(solution)/shard_map/ijb,bc->ijc/dot_general | solution.py:78
  (7 shorter events, 0.0 us)
Async XLA Ops:
  0.6 4.2 %copy-start = (bf16[1024,1024]{1,0:T(8,128)(2,1)S(1)}, bf16[1024,1024]{1,0:T(8,128)(2,1)}, u32[]{:S(2)}) copy-start(bf16[1024,1024]{1,0:T(8,128)(2,1)} %param.25) | copy-start | bytes 6291460
  0.6 4.2 %copy-start.5 = (f32[1024]{0:T(1024)S(1)}, f32[1024]{0:T(1024)}, u32[]{:S(2)}) copy-start(f32[1024]{0:T(1024)} %param.26) | copy-start | bytes 12292
  0.7 4.2 %copy-start.6 = (f32[1024]{0:T(1024)S(1)}, f32[1024]{0:T(1024)}, u32[]{:S(2)}) copy-start(f32[1024]{0:T(1024)} %param.24) | copy-start | bytes 12292
  0.7 4.2 %copy-start.3 = (f32[2560]{0:T(1024)S(1)}, f32[2560]{0:T(1024)}, u32[]{:S(2)}) copy-start(f32[2560]{0:T(1024)} %param.22) | copy-start | bytes 30724
  0.7 4.2 %copy-start.4 = (f32[2560]{0:T(1024)S(1)}, f32[2560]{0:T(1024)}, u32[]{:S(2)}) copy-start(f32[2560]{0:T(1024)} %param.21) | copy-start | bytes 30724
  4.9 3.8 %copy-start.1 = (f32[23,1024]{1,0:T(8,128)S(1)}, f32[23,1024]{1,0:T(8,128)}, u32[]{:S(2)}) copy-start(f32[23,1024]{1,0:T(8,128)} %param.28) | copy-start | bytes 282628
  4.9 3.8 %copy-start.8 = (s32[16]{0:T(128)S(1)}, s32[16]{0:T(128)}, u32[]{:S(2)}) copy-start(s32[16]{0:T(128)} %param.27) | copy-start | bytes 196
  4.9 4.9 %copy-start.10 = (bf16[1024,128]{1,0:T(8,128)(2,1)S(1)}, bf16[1024,128]{1,0:T(8,128)(2,1)}, u32[]{:S(2)}) copy-start(bf16[1024,128]{1,0:T(8,128)(2,1)} %param.31) | copy-start | bytes 786436
  4.9 4.9 %copy-start.13 = (f32[1024]{0:T(1024)S(1)}, f32[1024]{0:T(1024)}, u32[]{:S(2)}) copy-start(f32[1024]{0:T(1024)} %param.30) | copy-start | bytes 12292
  4.9 4.9 %copy-start.14 = (f32[1024]{0:T(1024)S(1)}, f32[1024]{0:T(1024)}, u32[]{:S(2)}) copy-start(f32[1024]{0:T(1024)} %param.29) | copy-start | bytes 12292
  4.9 4.9 %copy-start.15 = (f32[128]{0:T(128)S(1)}, f32[128]{0:T(128)}, u32[]{:S(2)}) copy-start(f32[128]{0:T(128)} %param.32) | copy-start | bytes 1540
  4.9 13.4 %copy-start.2 = (bf16[128,128]{1,0:T(8,128)(2,1)S(1)}, bf16[128,128]{1,0:T(8,128)(2,1)}, u32[]{:S(2)}) copy-start(bf16[128,128]{1,0:T(8,128)(2,1)} %param.33) | copy-start | bytes 98308
  4.9 13.5 %copy-start.7 = (f32[2,128]{1,0:T(2,128)S(1)}, f32[2,128]{1,0:T(2,128)}, u32[]{:S(2)}) copy-start(f32[2,128]{1,0:T(2,128)} %param.37) | copy-start | bytes 3076
  5.0 20.6 %copy-start.9 = (s32[16]{0:T(128)S(1)}, s32[16]{0:T(128)}, u32[]{:S(2)}) copy-start(s32[16]{0:T(128)} %param.36) | copy-start | bytes 196
  8.7 17.7 %copy-start.11 = (f32[66,128]{1,0:T(8,128)S(1)}, f32[66,128]{1,0:T(8,128)}, u32[]{:S(2)}) copy-start(f32[66,128]{1,0:T(8,128)} %param.35) | copy-start | bytes 101380
  8.7 17.7 %copy-start.12 = (s32[16,256]{1,0:T(8,128)S(1)}, s32[16,256]{1,0:T(8,128)}, u32[]{:S(2)}) copy-start(s32[16,256]{1,0:T(8,128)} %param.34) | copy-start | bytes 49156
  11.0 14.3 %all-to-all-start = ((bf16[16,16,128]{2,1,0:T(8,128)(2,1)}), bf16[16,16,128]{2,1,0:T(8,128)(2,1)S(1)}, u32[]{:S(2)}, u32[]{:S(2)}) async-start(bf16[16,16,128]{2,1,0:T(8,128)(2,1)} %broadcast_in_dim.27), calls=%async_computation | async-start | bytes 131072 | tf_op jit(solution)/shard_map/all_to_all | solution.py:136

commit v2 on v1

--- a/solution.py
+++ b/solution.py
@@ -82,6 +82,23 @@
     return summed.astype(jnp.bfloat16)
 
 
+def gather_blocks(block, device_count):
+    if device_count & (device_count - 1):
+        return lax.all_gather(block, "seq", axis=0, tiled=True)
+    index = lax.axis_index("seq")
+    span = 1
+    while span < device_count:
+        pairs = [(source, source ^ span) for source in range(device_count)]
+        other = lax.ppermute(block, "seq", pairs)
+        block = jnp.where(
+            index & span,
+            jnp.concatenate([other, block], axis=0),
+            jnp.concatenate([block, other], axis=0),
+        )
+        span *= 2
+    return block
+
+
 def shards(
     hidden_states,
     layer_mix,
@@ -132,10 +149,7 @@
         ],
         axis=1,
     )
-    copies = jnp.broadcast_to(block[None], (device_count,) + block.shape)
-    blocks = lax.all_to_all(copies, "seq", split_axis=0, concat_axis=0).reshape(
-        device_count * tok_count, -1
-    )
+    blocks = gather_blocks(block, device_count)
     key_cols = blocks[:, :inner_dim]
     col_chain = blocks[:, inner_dim].astype(jnp.int32)
     diff_cols = jnp.dot(key_cols, pair_weight[inner_dim:], preferred_element_type=jnp.float32)

time: 29.9 us -> 30.3 us (1.013)
  starting transfers between devices: 7.38 us -> 8.62 us
  local copies, waits for them, and re-layouts: 1.02 us -> 0.44 us
  waiting for transfers between devices: 6.76 us -> 6.38 us
    ppermute x0 -> x4, starting transfers between devices: none -> 8.62 us  [gather_blocks(): other = lax.ppermute(block, 'seq', pairs)]
    all_to_all x1 -> x0, starting transfers between devices: 7.38 us -> none  [shards(): lax.all_to_all(copies, 'seq', split_axis=0, concat_axis=0)]
    all_to_all x1 -> x0, waiting for transfers between devices: 6.76 us -> none  [shards(): lax.all_to_all(copies, 'seq', split_axis=0, concat_axis=0)]
    ppermute x0 -> x4, waiting for transfers between devices: none -> 6.38 us  [gather_blocks(): other = lax.ppermute(block, 'seq', pairs)]
    broadcast_in_dim x1 -> x0, local copies, waits for them, and re-layouts: 0.65 us -> none  [shards(): copies = jnp.broadcast_to(block[None], (device_count,) + block.shape)]
  transfers between devices with their start and end apart: 1 -> 4, of which waited for: 1 -> 4; matrix products, arithmetic and copies ran while one was open for 0% -> 0% of each run, Pallas kernels for 0% -> 0%
where the time goes in v2:
time: 30.3 us; the launch traced here: 30.1 us
  starting transfers between devices  8.62 us (28%)
  matrix products  8.45 us (28%)
  waiting for transfers between devices  6.38 us (21%)
  other arithmetic  5.32 us (18%)
  between operations  0.92 us (3%)
  local copies, waits for them, and re-layouts  0.44 us (1%)
    ppermute x4, starting transfers between devices, gather_blocks(): other = lax.ppermute(block, 'seq', pairs)  8.62 us
    ppermute x4, waiting for transfers between devices, gather_blocks(): other = lax.ppermute(block, 'seq', pairs)  6.38 us
    dot_general x1, matrix products, single_path(): jnp.dot(hidden, proj_out, preferred_element_type=jnp.float32)  3.73 us
    dot_general x1, matrix products, pair_tile(): jnp.einsum('ijb,bc->ijc', onehot, relpos_table, precision=lax.Precision.H...  3.2 us
    reduce_sum x1, other arithmetic, layer_norm(): center = values - jnp.mean(values, axis=-1, keepdims=True)  3 us
    reduce_sum x2, other arithmetic, layer_norm(): spread = jnp.mean(center * center, axis=-1, keepdims=True)  0.95 us
    broadcast_in_dim x1, other arithmetic, shards(): chain_ids.astype(jnp.bfloat16)[:, None]  0.8 us
    dot_general x1, matrix products, pair_tile(): jnp.dot(products.reshape(row_count * col_count, inner_dim), pair_weight[:...  0.68 us
  transfers between devices with their start and end apart: 4, of which 4 were waited for; matrix products, arithmetic and copies ran while one was open for 0% of the time, Pallas kernels for 0%

profile of v2, /device:TPU:0, one launch (start us, length us, event | category | flops | bytes accessed | tf_op | source)
XLA Modules:
  0.0 30.1 jit_solution(4487456130999555282)
XLA Ops:
  0.6 0.0 copy-start
  0.6 0.0 copy-start.5
  0.7 0.0 copy-start.6
  0.7 0.0 copy-start.3
  0.7 0.0 copy-start.4
  0.7 0.8 %convert_bitcast_fusion = bf16[16,1]{0,1:T(2,128)(2,1)S(1)} fusion(s32[16]{0:T(128)} %param.36), kind=kLoop, calls=%fused_computation.55 | loop fusion | flops 16 | bytes 96 | tf_op jit(solution)/shard_map/broadcast_in_dim | solution.py:147
  1.5 0.1 copy.29
  1.6 3.0 %fusion = (f32[16]{0:T(128)S(1)}, f32[16,2560]{1,0:T(8,128)S(1)}) fusion(bf16[37,16,2560]{2,1,0:T(8,128)(2,1)} %param.19, f32[37]{0:T(128)} %param.20), kind=kLoop, calls=%fused_computation.1 | loop fusion | flops 6021104 | bytes 3195092 | tf_op jit(solution)/shard_map/reduce_sum | solution.py:10
  4.6 0.2 multiply_reduce_fusion
  4.8 0.0 copy-done
  4.8 0.0 copy-done.5
  4.8 0.0 copy-done.6
  4.8 0.0 copy-done.3
  4.9 0.0 copy-done.4
  4.9 0.0 copy-start.1
  4.9 0.0 copy-start.8
  4.9 0.0 copy-start.10
  4.9 0.0 copy-start.13
  4.9 0.0 copy-start.14
  4.9 0.0 copy-start.15
  4.9 0.0 copy-start.2
  4.9 0.0 copy-start.7
  5.0 0.0 copy-start.9
  5.0 3.7 %convolution_add_fusion.1 = f32[16,1024]{1,0:T(8,128)S(1)} fusion(bf16[1024,1024]{1,0:T(8,128)(2,1)S(1)} %copy-done, bf16[2560,1024]{1,0:T(8,128)(2,1)} %param.23, f32[16,2560]{1,0:T(8,128)S(1)} %get-tuple-element.3, f32[2560]{0:T(1024)S(1)} %copy-done.3, f32[2560]{0:T(1024)S(1)} %copy-done.4, f32[16]{0:T(128)S(1)} %add_rsqrt_fusion.1, ...), kind=kOutput, calls=%fused_computation.6 | convolution fusion | flops 117710848 | bytes 7598208 | tf_op jit(solution)/shard_map/dot_general | solution.py:40
  8.7 0.0 copy-done.1
  8.7 0.0 copy-done.8
  8.7 0.0 copy-start.11
  8.7 0.0 copy-start.12
  8.7 0.3 %fusion.34 = (f32[16]{0:T(128)S(1)}, f32[16,1024]{1,0:T(8,128)S(1)}) fusion(f32[16,1024]{1,0:T(8,128)S(1)} %convolution_add_fusion.1, f32[23,1024]{1,0:T(8,128)S(1)} %copy-done.1, s32[16]{0:T(128)S(1)} %copy-done.8), kind=kOutput, calls=%fused_computation.61 | convolution fusion | flops 4555104 | bytes 225408 | tf_op jit(solution)/shard_map/dot_general | solution.py:38
  9.1 0.7 %multiply_reduce_fusion.1 = (f32[16]{0:T(128)S(1)}, bf16[16,1024]{1,0:T(8,128)(2,1)}) fusion(f32[16,1024]{1,0:T(8,128)S(1)} %get-tuple-element.13, f32[16]{0:T(128)S(1)} %broadcast_multiply_fusion), kind=kLoop, calls=%fused_computation.25 | loop fusion | flops 65520 | bytes 98432 | tf_op jit(solution)/shard_map/reduce_sum | solution.py:11
  9.8 0.0 copy-done.10
  9.8 0.0 copy-done.13
  9.8 0.0 copy-done.14
  9.9 0.0 copy-done.15
  9.9 0.2 fusion.4
  10.1 0.1 slice_convert_fusion.1
  10.2 0.1 pad_maximum_fusion.1
  10.2 0.5 %collective-permute-start = (bf16[16,128]{1,0:T(8,128)(2,1)S(1)}, bf16[16,128]{1,0:T(8,128)(2,1)S(1)}, u32[]{:S(2)}, u32[]{:S(2)}) collective-permute-start(bf16[16,128]{1,0:T(8,128)(2,1)S(1)} %pad_maximum_fusion.1), channel_id=1, source_target_pairs={{0,1},{1,0},{2,3},{3,2},{4,5},{5,4},{6,7},{7,6},{8,9},{9,8},{10,11... | collective-permute-start | bytes 12296 | tf_op jit(solution)/shard_map/ppermute | solution.py:92
  10.7 0.8 %collective-permute-done = bf16[16,128]{1,0:T(8,128)(2,1)S(1)} collective-permute-done((bf16[16,128]{1,0:T(8,128)(2,1)S(1)}, bf16[16,128]{1,0:T(8,128)(2,1)S(1)}, u32[]{:S(2)}, u32[]{:S(2)}) %collective-permute-start) | collective-permute-done | bytes 4128 | tf_op jit(solution)/shard_map/ppermute | solution.py:92
  11.5 0.1 pad_maximum_fusion
  11.6 0.1 copy.31
  11.7 0.1 copy.30
  11.9 2.9 %collective-permute-start.1 = (bf16[32,128]{0,1:T(8,128)(2,1)S(1)}, bf16[32,128]{0,1:T(8,128)(2,1)S(1)}, u32[]{:S(2)}, u32[]{:S(2)}) collective-permute-start(bf16[32,128]{0,1:T(8,128)(2,1)S(1)} %broadcast_select_fusion), channel_id=1, source_target_pairs={{0,2},{1,3},{2,0},{3,1},{4,6},{5,7},{6,4},{7,5},{8,10},{9,11},{10,... | collective-permute-start | bytes 24584 | tf_op jit(solution)/shard_map/ppermute | solution.py:92
  14.8 1.9 %collective-permute-done.1 = bf16[32,128]{0,1:T(8,128)(2,1)S(1)} collective-permute-done((bf16[32,128]{0,1:T(8,128)(2,1)S(1)}, bf16[32,128]{0,1:T(8,128)(2,1)S(1)}, u32[]{:S(2)}, u32[]{:S(2)}) %collective-permute-start.1) | collective-permute-done | bytes 8224 | tf_op jit(solution)/shard_map/ppermute | solution.py:92
  16.7 0.1 maximum_select_fusion.1
  16.8 2.1 %collective-permute-start.2 = (bf16[64,128]{0,1:T(8,128)(2,1)S(1)}, bf16[64,128]{0,1:T(8,128)(2,1)S(1)}, u32[]{:S(2)}, u32[]{:S(2)}) collective-permute-start(bf16[64,128]{0,1:T(8,128)(2,1)S(1)} %maximum_select_fusion.1), channel_id=1, source_target_pairs={{0,4},{1,5},{2,6},{3,7},{4,0},{5,1},{6,2},{7,3},{8,12},{9,13},{10,... | collective-permute-start | bytes 49160 | tf_op jit(solution)/shard_map/ppermute | solution.py:92
  18.9 0.0 copy-done.2
  18.9 0.1 fusion.29
  19.1 1.8 %collective-permute-done.2 = bf16[64,128]{0,1:T(8,128)(2,1)S(1)} collective-permute-done((bf16[64,128]{0,1:T(8,128)(2,1)S(1)}, bf16[64,128]{0,1:T(8,128)(2,1)S(1)}, u32[]{:S(2)}, u32[]{:S(2)}) %collective-permute-start.2) | collective-permute-done | bytes 16416 | tf_op jit(solution)/shard_map/ppermute | solution.py:92
  20.8 0.1 maximum_select_fusion.2
  20.9 3.1 %collective-permute-start.3 = (bf16[128,128]{0,1:T(8,128)(2,1)S(1)}, bf16[128,128]{0,1:T(8,128)(2,1)S(1)}, u32[]{:S(2)}, u32[]{:S(2)}) collective-permute-start(bf16[128,128]{0,1:T(8,128)(2,1)S(1)} %maximum_select_fusion.2), channel_id=1, source_target_pairs={{0,8},{1,9},{2,10},{3,11},{4,12},{5,13},{6,14},{7,15},{8,0},{9,1},... | collective-permute-start | bytes 98312 | tf_op jit(solution)/shard_map/ppermute | solution.py:92
  24.0 0.0 copy-done.7
  24.0 1.9 %collective-permute-done.3 = bf16[128,128]{0,1:T(8,128)(2,1)S(1)} collective-permute-done((bf16[128,128]{0,1:T(8,128)(2,1)S(1)}, bf16[128,128]{0,1:T(8,128)(2,1)S(1)}, u32[]{:S(2)}, u32[]{:S(2)}) %collective-permute-start.3) | collective-permute-done | bytes 32800 | tf_op jit(solution)/shard_map/ppermute | solution.py:92
  26.0 0.2 fusion.24
  26.1 0.0 copy-done.9
  26.2 0.1 broadcast_compare_fusion
  26.2 0.7 %fusion.6 = f32[16,256,128]{2,1,0:T(8,128)S(1)} fusion(f32[256,64]{0,1:T(8,128)S(1)} %slice_convert_fusion, f32[16,64]{1,0:T(8,128)S(1)} %get-tuple-element.8, bf16[128,128]{1,0:T(8,128)(2,1)S(1)} %copy-done.2), kind=kOutput, calls=%fused_computation.14 | convolution fusion | flops 67633152 | bytes 2187264 | tf_op jit(solution)/shard_map/dot_general | solution.py:69
  26.9 0.0 copy-done.11
  26.9 0.0 copy-done.12
  26.9 3.2 %add_convert_fusion = bf16[16,256,128]{2,1,0:T(8,128)(2,1)} fusion(f32[16,256,128]{2,1,0:T(8,128)S(1)} %fusion.6, f32[128]{0:T(128)S(1)} %get-tuple-element.11, f32[128]{0:T(128)S(1)} %get-tuple-element.10, f32[256,128]{1,0:T(8,128)S(1)} %fusion.24, f32[16,128]{1,0:T(8,128)S(1)} %fusion.29, pred[16,256]{1,0:T(8,128)(4,1)S(1)} %broadcast_compare_fusion, ...), kind=kOutput, calls=%fused_computation.3 | convolution fusion | flops 418652160 | bytes 3340288 | tf_op jit(solution)/shard_map/ijb,bc->ijc/dot_general | solution.py:78
  (10 shorter events, 0.1 us)
Async XLA Ops:
  0.6 4.2 %copy-start = (bf16[1024,1024]{1,0:T(8,128)(2,1)S(1)}, bf16[1024,1024]{1,0:T(8,128)(2,1)}, u32[]{:S(2)}) copy-start(bf16[1024,1024]{1,0:T(8,128)(2,1)} %param.25) | copy-start | bytes 6291460
  0.6 4.2 %copy-start.5 = (f32[1024]{0:T(1024)S(1)}, f32[1024]{0:T(1024)}, u32[]{:S(2)}) copy-start(f32[1024]{0:T(1024)} %param.26) | copy-start | bytes 12292
  0.7 4.2 %copy-start.6 = (f32[1024]{0:T(1024)S(1)}, f32[1024]{0:T(1024)}, u32[]{:S(2)}) copy-start(f32[1024]{0:T(1024)} %param.24) | copy-start | bytes 12292
  0.7 4.2 %copy-start.3 = (f32[2560]{0:T(1024)S(1)}, f32[2560]{0:T(1024)}, u32[]{:S(2)}) copy-start(f32[2560]{0:T(1024)} %param.22) | copy-start | bytes 30724
  0.7 4.2 %copy-start.4 = (f32[2560]{0:T(1024)S(1)}, f32[2560]{0:T(1024)}, u32[]{:S(2)}) copy-start(f32[2560]{0:T(1024)} %param.21) | copy-start | bytes 30724
  4.9 3.8 %copy-start.1 = (f32[23,1024]{1,0:T(8,128)S(1)}, f32[23,1024]{1,0:T(8,128)}, u32[]{:S(2)}) copy-start(f32[23,1024]{1,0:T(8,128)} %param.28) | copy-start | bytes 282628
  4.9 3.8 %copy-start.8 = (s32[16]{0:T(128)S(1)}, s32[16]{0:T(128)}, u32[]{:S(2)}) copy-start(s32[16]{0:T(128)} %param.27) | copy-start | bytes 196
  4.9 4.9 %copy-start.10 = (bf16[1024,128]{1,0:T(8,128)(2,1)S(1)}, bf16[1024,128]{1,0:T(8,128)(2,1)}, u32[]{:S(2)}) copy-start(bf16[1024,128]{1,0:T(8,128)(2,1)} %param.31) | copy-start | bytes 786436
  4.9 4.9 %copy-start.13 = (f32[1024]{0:T(1024)S(1)}, f32[1024]{0:T(1024)}, u32[]{:S(2)}) copy-start(f32[1024]{0:T(1024)} %param.30) | copy-start | bytes 12292
  4.9 4.9 %copy-start.14 = (f32[1024]{0:T(1024)S(1)}, f32[1024]{0:T(1024)}, u32[]{:S(2)}) copy-start(f32[1024]{0:T(1024)} %param.29) | copy-start | bytes 12292
  4.9 4.9 %copy-start.15 = (f32[128]{0:T(128)S(1)}, f32[128]{0:T(128)}, u32[]{:S(2)}) copy-start(f32[128]{0:T(128)} %param.32) | copy-start | bytes 1540
  4.9 14.0 %copy-start.2 = (bf16[128,128]{1,0:T(8,128)(2,1)S(1)}, bf16[128,128]{1,0:T(8,128)(2,1)}, u32[]{:S(2)}) copy-start(bf16[128,128]{1,0:T(8,128)(2,1)} %param.33) | copy-start | bytes 98308
  4.9 19.1 %copy-start.7 = (f32[2,128]{1,0:T(2,128)S(1)}, f32[2,128]{1,0:T(2,128)}, u32[]{:S(2)}) copy-start(f32[2,128]{1,0:T(2,128)} %param.37) | copy-start | bytes 3076
  5.0 21.2 %copy-start.9 = (s32[16]{0:T(128)S(1)}, s32[16]{0:T(128)}, u32[]{:S(2)}) copy-start(s32[16]{0:T(128)} %param.36) | copy-start | bytes 196
  8.7 18.2 %copy-start.11 = (f32[66,128]{1,0:T(8,128)S(1)}, f32[66,128]{1,0:T(8,128)}, u32[]{:S(2)}) copy-start(f32[66,128]{1,0:T(8,128)} %param.35) | copy-start | bytes 101380
  8.7 18.2 %copy-start.12 = (s32[16,256]{1,0:T(8,128)S(1)}, s32[16,256]{1,0:T(8,128)}, u32[]{:S(2)}) copy-start(s32[16,256]{1,0:T(8,128)} %param.34) | copy-start | bytes 49156
  10.2 1.3 %collective-permute-start = (bf16[16,128]{1,0:T(8,128)(2,1)S(1)}, bf16[16,128]{1,0:T(8,128)(2,1)S(1)}, u32[]{:S(2)}, u32[]{:S(2)}) collective-permute-start(bf16[16,128]{1,0:T(8,128)(2,1)S(1)} %pad_maximum_fusion.1), channel_id=1, source_target_pairs={{0,1},{1,0},{2,3},{3,2},{4,5},{5,4},{6,7},{7,6},{8,9},{9,8},{10,11... | collective-permute-start | bytes 12296 | tf_op jit(solution)/shard_map/ppermute | solution.py:92
  11.9 4.8 %collective-permute-start.1 = (bf16[32,128]{0,1:T(8,128)(2,1)S(1)}, bf16[32,128]{0,1:T(8,128)(2,1)S(1)}, u32[]{:S(2)}, u32[]{:S(2)}) collective-permute-start(bf16[32,128]{0,1:T(8,128)(2,1)S(1)} %broadcast_select_fusion), channel_id=1, source_target_pairs={{0,2},{1,3},{2,0},{3,1},{4,6},{5,7},{6,4},{7,5},{8,10},{9,11},{10,... | collective-permute-start | bytes 24584 | tf_op jit(solution)/shard_map/ppermute | solution.py:92
  16.8 4.0 %collective-permute-start.2 = (bf16[64,128]{0,1:T(8,128)(2,1)S(1)}, bf16[64,128]{0,1:T(8,128)(2,1)S(1)}, u32[]{:S(2)}, u32[]{:S(2)}) collective-permute-start(bf16[64,128]{0,1:T(8,128)(2,1)S(1)} %maximum_select_fusion.1), channel_id=1, source_target_pairs={{0,4},{1,5},{2,6},{3,7},{4,0},{5,1},{6,2},{7,3},{8,12},{9,13},{10,... | collective-permute-start | bytes 49160 | tf_op jit(solution)/shard_map/ppermute | solution.py:92
  20.9 5.0 %collective-permute-start.3 = (bf16[128,128]{0,1:T(8,128)(2,1)S(1)}, bf16[128,128]{0,1:T(8,128)(2,1)S(1)}, u32[]{:S(2)}, u32[]{:S(2)}) collective-permute-start(bf16[128,128]{0,1:T(8,128)(2,1)S(1)} %maximum_select_fusion.2), channel_id=1, source_target_pairs={{0,8},{1,9},{2,10},{3,11},{4,12},{5,13},{6,14},{7,15},{8,0},{9,1},... | collective-permute-start | bytes 98312 | tf_op jit(solution)/shard_map/ppermute | solution.py:92

commit v3 on v1

--- a/solution.py
+++ b/solution.py
@@ -132,10 +132,12 @@
         ],
         axis=1,
     )
-    copies = jnp.broadcast_to(block[None], (device_count,) + block.shape)
-    blocks = lax.all_to_all(copies, "seq", split_axis=0, concat_axis=0).reshape(
-        device_count * tok_count, -1
+    placed = lax.dynamic_update_slice(
+        jnp.zeros((device_count * tok_count, block.shape[1]), block.dtype),
+        block,
+        (lax.axis_index("seq") * tok_count, 0),
     )
+    blocks = lax.psum(placed, "seq")
     key_cols = blocks[:, :inner_dim]
     col_chain = blocks[:, inner_dim].astype(jnp.int32)
     diff_cols = jnp.dot(key_cols, pair_weight[inner_dim:], preferred_element_type=jnp.float32)

time: 29.9 us -> 119 us (3.98)
  waiting for transfers between devices: 6.76 us -> 87.4 us
  between operations: 0.92 us -> 14.3 us
  starting transfers between devices: 7.38 us -> 0.04 us
  other arithmetic: 5.19 us -> 6.52 us
    psum x0 -> x1, waiting for transfers between devices: none -> 87.4 us  [shards(): blocks = lax.psum(placed, 'seq')]
    all_to_all x1 -> x0, starting transfers between devices: 7.38 us -> none  [shards(): lax.all_to_all(copies, 'seq', split_axis=0, concat_axis=0)]
    all_to_all x1 -> x0, waiting for transfers between devices: 6.76 us -> none  [shards(): lax.all_to_all(copies, 'seq', split_axis=0, concat_axis=0)]
where the time goes in v3:
time: 119 us; the launch traced here: 118 us
  waiting for transfers between devices  87.4 us (73%)
  between operations  14.3 us (12%)
  matrix products  8.44 us (7%)
  other arithmetic  6.52 us (5%)
  local copies, waits for them, and re-layouts  1.27 us (1%)
    psum x1, waiting for transfers between devices, shards(): blocks = lax.psum(placed, 'seq')  87.4 us
    dot_general x1, matrix products, single_path(): jnp.dot(hidden, proj_out, preferred_element_type=jnp.float32)  3.73 us
    dot_general x1, matrix products, pair_tile(): jnp.einsum('ijb,bc->ijc', onehot, relpos_table, precision=lax.Precision.H...  3.2 us
    reduce_sum x1, other arithmetic, layer_norm(): center = values - jnp.mean(values, axis=-1, keepdims=True)  3 us
  transfers between devices with their start and end apart: 1, of which 1 were waited for; matrix products, arithmetic and copies ran while one was open for 0% of the time, Pallas kernels for 0%

profile of v3, /device:TPU:0, one launch (start us, length us, event | category | flops | bytes accessed | tf_op | source)
XLA Modules:
  0.0 118.0 jit_solution(12350046026314436866)
XLA Ops:
  7.2 0.0 copy-start
  7.2 0.0 copy-start.7
  7.2 0.0 copy-start.8
  7.2 0.0 copy-start.5
  7.2 0.0 copy-start.6
  7.2 0.0 all-reduce.2.cloned.1.call-start
  7.3 0.8 convert_bitcast_fusion
  8.1 0.1 copy.25
  8.2 3.0 %fusion = (f32[16]{0:T(128)S(1)}, f32[16,2560]{1,0:T(8,128)S(1)}) fusion(bf16[37,16,2560]{2,1,0:T(8,128)(2,1)} %param.19, f32[37]{0:T(128)} %param.20), kind=kLoop, calls=%fused_computation.1 | loop fusion | flops 6021104 | bytes 3195092 | tf_op jit(solution)/shard_map/reduce_sum | solution.py:10
  11.2 0.2 multiply_reduce_fusion
  11.4 0.0 copy-done
  11.4 0.0 copy-done.7
  11.4 0.0 copy-done.8
  11.4 0.0 copy-done.5
  11.4 0.0 copy-done.6
  11.4 0.0 copy-start.2
  11.4 0.0 copy-start.10
  11.5 0.0 copy-start.12
  11.5 0.0 copy-start.15
  11.5 0.0 copy-start.16
  11.5 0.0 copy-start.17
  11.5 0.0 copy-start.3
  11.5 0.0 copy-start.9
  11.5 0.0 copy-start.11
  11.5 3.7 %convolution_add_fusion.1 = f32[16,1024]{1,0:T(8,128)S(1)} fusion(bf16[1024,1024]{1,0:T(8,128)(2,1)S(1)} %copy-done, bf16[2560,1024]{1,0:T(8,128)(2,1)} %param.23, f32[16,2560]{1,0:T(8,128)S(1)} %get-tuple-element.3, f32[2560]{0:T(1024)S(1)} %copy-done.5, f32[2560]{0:T(1024)S(1)} %copy-done.6, f32[16]{0:T(128)S(1)} %add_rsqrt_fusion.1, ...), kind=kOutput, calls=%fused_computation.6 | convolution fusion | flops 117710848 | bytes 7598208 | tf_op jit(solution)/shard_map/dot_general | solution.py:40
  15.3 0.0 copy-done.2
  15.3 0.0 copy-done.10
  15.3 0.0 copy-start.13
  15.3 0.0 copy-start.14
  15.3 0.3 fusion.34
  15.7 0.7 multiply_reduce_fusion.1
  16.4 0.0 copy-done.12
  16.4 0.0 copy-done.15
  16.4 0.0 copy-done.16
  16.4 0.0 copy-done.17
  16.4 0.2 fusion.4
  16.6 0.1 slice_convert_fusion.1
  16.7 0.1 pad.2.clone
  16.8 0.1 maximum_maximum_fusion
  16.9 0.1 copy.26
  17.0 0.2 dynamic_update_slice.3
  17.3 0.0 copy-start.1
  17.3 0.6 copy-done.1
  17.9 0.0 all-reduce.2.cloned.1.call-update
  17.9 0.0 copy-done.3
  17.9 0.1 fusion.29
  18.1 0.0 copy-done.9
  18.1 87.4 %all-reduce.2.cloned.1.call-done = bf16[256,128]{0,1:T(8,128)(2,1)} async-done(((bf16[256,128]{0,1:T(8,128)(2,1)}), bf16[256,128]{0,1:T(8,128)(2,1)}) %all-reduce.2.cloned.1.call-update) | async-done | bytes 65552 | tf_op jit(solution)/shard_map/psum | solution.py:140
  105.4 0.0 copy-start.4
  105.4 0.8 slice_convert_fusion.2
  106.2 0.0 copy-done.11
  106.2 0.1 broadcast_compare_fusion
  106.3 0.8 slice_convert_fusion
  107.0 0.7 fusion.6
  107.7 0.0 copy-done.4
  107.7 0.2 fusion.24
  107.9 0.0 copy-done.13
  107.9 0.0 copy-done.14
  107.9 3.2 %add_convert_fusion = bf16[16,256,128]{2,1,0:T(8,128)(2,1)} fusion(f32[16,256,128]{2,1,0:T(8,128)S(1)} %fusion.6, f32[128]{0:T(128)S(1)} %get-tuple-element.9, f32[128]{0:T(128)S(1)} %get-tuple-element.8, f32[256,128]{1,0:T(8,128)S(1)} %fusion.24, f32[16,128]{1,0:T(8,128)S(1)} %fusion.29, pred[16,256]{1,0:T(8,128)(4,1)S(1)} %broadcast_compare_fusion, ...), kind=kOutput, calls=%fused_computation.3 | convolution fusion | flops 418652160 | bytes 3340288 | tf_op jit(solution)/shard_map/ijb,bc->ijc/dot_general | solution.py:78
  (7 shorter events, 0.0 us)
Async XLA Ops:
  7.2 4.2 %copy-start = (bf16[1024,1024]{1,0:T(8,128)(2,1)S(1)}, bf16[1024,1024]{1,0:T(8,128)(2,1)}, u32[]{:S(2)}) copy-start(bf16[1024,1024]{1,0:T(8,128)(2,1)} %param.25) | copy-start | bytes 6291460
  7.2 4.2 %copy-start.7 = (f32[1024]{0:T(1024)S(1)}, f32[1024]{0:T(1024)}, u32[]{:S(2)}) copy-start(f32[1024]{0:T(1024)} %param.26) | copy-start | bytes 12292
  7.2 4.2 %copy-start.8 = (f32[1024]{0:T(1024)S(1)}, f32[1024]{0:T(1024)}, u32[]{:S(2)}) copy-start(f32[1024]{0:T(1024)} %param.24) | copy-start | bytes 12292
  7.2 4.2 %copy-start.5 = (f32[2560]{0:T(1024)S(1)}, f32[2560]{0:T(1024)}, u32[]{:S(2)}) copy-start(f32[2560]{0:T(1024)} %param.22) | copy-start | bytes 30724
  7.2 4.2 %copy-start.6 = (f32[2560]{0:T(1024)S(1)}, f32[2560]{0:T(1024)}, u32[]{:S(2)}) copy-start(f32[2560]{0:T(1024)} %param.21) | copy-start | bytes 30724
  7.2 98.2 %all-reduce.2.cloned.1.call-start = ((), (), s32[]{:S(2)}) async-start(), calls=%async_computation | async-start | bytes 131072 | tf_op jit(solution)/shard_map/psum | solution.py:140
  11.4 3.8 %copy-start.2 = (f32[23,1024]{1,0:T(8,128)S(1)}, f32[23,1024]{1,0:T(8,128)}, u32[]{:S(2)}) copy-start(f32[23,1024]{1,0:T(8,128)} %param.28) | copy-start | bytes 282628
  11.4 3.8 %copy-start.10 = (s32[16]{0:T(128)S(1)}, s32[16]{0:T(128)}, u32[]{:S(2)}) copy-start(s32[16]{0:T(128)} %param.27) | copy-start | bytes 196
  11.5 4.9 %copy-start.12 = (bf16[1024,128]{1,0:T(8,128)(2,1)S(1)}, bf16[1024,128]{1,0:T(8,128)(2,1)}, u32[]{:S(2)}) copy-start(bf16[1024,128]{1,0:T(8,128)(2,1)} %param.31) | copy-start | bytes 786436
  11.5 4.9 %copy-start.15 = (f32[1024]{0:T(1024)S(1)}, f32[1024]{0:T(1024)}, u32[]{:S(2)}) copy-start(f32[1024]{0:T(1024)} %param.30) | copy-start | bytes 12292
  11.5 4.9 %copy-start.16 = (f32[1024]{0:T(1024)S(1)}, f32[1024]{0:T(1024)}, u32[]{:S(2)}) copy-start(f32[1024]{0:T(1024)} %param.29) | copy-start | bytes 12292
  11.5 4.9 %copy-start.17 = (f32[128]{0:T(128)S(1)}, f32[128]{0:T(128)}, u32[]{:S(2)}) copy-start(f32[128]{0:T(128)} %param.32) | copy-start | bytes 1540
  11.5 6.4 %copy-start.3 = (bf16[128,128]{1,0:T(8,128)(2,1)S(1)}, bf16[128,128]{1,0:T(8,128)(2,1)}, u32[]{:S(2)}) copy-start(bf16[128,128]{1,0:T(8,128)(2,1)} %param.33) | copy-start | bytes 98308
  11.5 6.5 %copy-start.9 = (f32[2,128]{1,0:T(2,128)S(1)}, f32[2,128]{1,0:T(2,128)}, u32[]{:S(2)}) copy-start(f32[2,128]{1,0:T(2,128)} %param.37) | copy-start | bytes 3076
  11.5 94.7 %copy-start.11 = (s32[16]{0:T(128)S(1)}, s32[16]{0:T(128)}, u32[]{:S(2)}) copy-start(s32[16]{0:T(128)} %param.36) | copy-start | bytes 196
  15.3 92.6 %copy-start.13 = (f32[66,128]{1,0:T(8,128)S(1)}, f32[66,128]{1,0:T(8,128)}, u32[]{:S(2)}) copy-start(f32[66,128]{1,0:T(8,128)} %param.35) | copy-start | bytes 101380
  15.3 92.6 %copy-start.14 = (s32[16,256]{1,0:T(8,128)S(1)}, s32[16,256]{1,0:T(8,128)}, u32[]{:S(2)}) copy-start(s32[16,256]{1,0:T(8,128)} %param.34) | copy-start | bytes 49156
  17.3 0.6 copy-start.1
  105.4 2.3 %copy-start.4 = (bf16[256,128]{0,1:T(8,128)(2,1)S(1)}, bf16[256,128]{0,1:T(8,128)(2,1)}, u32[]{:S(2)}) copy-start(bf16[256,128]{0,1:T(8,128)(2,1)} %all-reduce.2.cloned.1.call-done) | copy-start | bytes 196612
Sparse Core Ops, SparseCore 0:
  18.0 87.3 all-reduce.1

commit v4 on v0

v4 whole, which is shorter than its diff:
```python
import functools

import jax
import jax.numpy as jnp
from jax import lax
from jax.experimental import pallas as pl
from jax.experimental.pallas import tpu as pltpu
from jax.sharding import PartitionSpec as P

epsilon = 1e-05
BF16 = jnp.bfloat16
F32 = jnp.float32


def pieces(total, count):
    count = max(1, min(count, total))
    ends = [total * step // count for step in range(count + 1)]
    return [(low, high - low) for low, high in zip(ends[:-1], ends[1:])]


def row_norm(values, gain, bias):
    center = values - jnp.mean(values, axis=-1, keepdims=True)
    spread = jnp.mean(center * center, axis=-1, keepdims=True)
    return center * lax.rsqrt(spread + epsilon) * gain + bias


def single_kernel(
    plan,
    hidden_hbm, mix_hbm, norm_gain_hbm, norm_bias_hbm, proj_in_hbm, proj_in_bias_hbm,
    proj_out_hbm, proj_out_bias_hbm, tokens_hbm, residue_hbm, pair_gain_hbm, pair_bias_hbm,
    qk_hbm, qk_bias_hbm, chain_hbm,
    single_hbm, query_key_ref, copies_ref,
    hidden, mix, norm_gain, norm_bias, proj_in, proj_in_bias, proj_out, proj_out_bias, tokens,
    residue, pair_gain, pair_bias, qk, qk_bias, chain, mixture, residue_rows, single,
    sem_hidden, sem_in, sem_out, sem_small, sem_single,
):
    state_pieces, in_pieces, out_pieces, lane_step = plan
    tok_count = mixture.shape[0]
    inner_dim = qk.shape[1] // 2

    small = [
        (mix_hbm, mix), (tokens_hbm, tokens), (residue_hbm, residue),
        (norm_gain_hbm, norm_gain), (norm_bias_hbm, norm_bias),
        (proj_in_bias_hbm, proj_in_bias), (proj_out_bias_hbm, proj_out_bias),
        (pair_gain_hbm, pair_gain), (pair_bias_hbm, pair_bias),
        (qk_hbm, qk), (qk_bias_hbm, qk_bias), (chain_hbm, chain),
    ]
    small = [
        pltpu.make_async_copy(source, target, sem_small.at[at])
        for at, (source, target) in enumerate(small)
    ]
    states = [
        pltpu.make_async_copy(
            hidden_hbm.at[pl.ds(low, size)], hidden.at[pl.ds(low, size)], sem_hidden.at[at]
        )
        for at, (low, size) in enumerate(state_pieces)
    ]
    firsts = [
        pltpu.make_async_copy(
            proj_in_hbm.at[pl.ds(low, size)], proj_in.at[pl.ds(low, size)], sem_in.at[at]
        )
        for at, (low, size) in enumerate(in_pieces)
    ]
    seconds = [
        pltpu.make_async_copy(
            proj_out_hbm.at[pl.ds(low, size)], proj_out.at[pl.ds(low, size)], sem_out.at[at]
        )
        for at, (low, size) in enumerate(out_pieces)
    ]
    small[0].start()
    for copy in states:
        copy.start()
    for copy in small[1:]:
        copy.start()
    for copy in firsts + seconds:
        copy.start()

    small[0].wait()
    width = mixture.shape[1]
    for at, (low, size) in enumerate(state_pieces):
        states[at].wait()
        for lane in range(0, width, lane_step):
            span = slice(lane, min(lane + lane_step, width))
            total = mixture[:, span] if at else None
            for state in range(low, low + size):
                term = mix[state] * hidden[state, :, span].astype(F32)
                total = term if total is None else total + term
            mixture[:, span] = total

    for copy in small[1:]:
        copy.wait()
    for row in range(tok_count):
        residue_rows[pl.ds(row, 1), :] = residue[pl.ds(tokens[row], 1), :]

    normed = row_norm(mixture[...], norm_gain[...], norm_bias[...]).astype(BF16)
    total = None
    for at, (low, size) in enumerate(in_pieces):
        firsts[at].wait()
        term = jnp.dot(
            normed[:, low:low + size], proj_in[pl.ds(low, size), :], preferred_element_type=F32
        )
        total = term if total is None else total + term
    middle = jnp.maximum(total + proj_in_bias[...], 0.0).astype(BF16)

    total = None
    for at, (low, size) in enumerate(out_pieces):
        seconds[at].wait()
        term = jnp.dot(
            middle[:, low:low + size], proj_out[pl.ds(low, size), :], preferred_element_type=F32
        )
        total = term if total is None else total + term
    single_f = total + proj_out_bias[...] + residue_rows[...]
    single[...] = single_f.astype(BF16)
    out_copy = pltpu.make_async_copy(single, single_hbm, sem_single)
    out_copy.start()

    pair_in = row_norm(single_f, pair_gain[...], pair_bias[...]).astype(BF16)
    query_key = jnp.dot(pair_in, qk[...], preferred_element_type=F32) + qk_bias[...]
    query_key_ref[...] = query_key.astype(BF16)

    shape = (tok_count, 2 * inner_dim)
    lanes = lax.broadcasted_iota(jnp.int32, shape, 1)
    square = (tok_count, tok_count)
    own = lax.broadcasted_iota(jnp.int32, square, 0) == lax.broadcasted_iota(jnp.int32, square, 1)
    chain_col = jnp.sum(
        jnp.where(own, chain[...].astype(F32), 0.0), axis=1, keepdims=True
    )
    keys = pltpu.roll(query_key, inner_dim, 1)
    block = jnp.where(lanes < inner_dim, keys, jnp.where(lanes == inner_dim, chain_col, 0.0))
    block = block.astype(BF16)
    for peer in range(copies_ref.shape[0]):
        copies_ref[peer] = block
    out_copy.wait()


def single_part(device_count, operands):
    (hidden, mix, norm_gain, norm_bias, proj_in, proj_in_bias, proj_out, proj_out_bias, tokens,
     residue, pair_gain, pair_bias, qk, qk_bias, chain) = operands
    state_count, tok_count, width = hidden.shape
    channels = proj_out.shape[1]
    lanes = qk.shape[1]
    plan = (pieces(state_count, 4), pieces(width, 5), pieces(channels, 2), 512)
    args = (
        hidden, mix, norm_gain[None], norm_bias[None], proj_in, proj_in_bias[None],
        proj_out, proj_out_bias[None], tokens, residue, pair_gain[None], pair_bias[None],
        qk, qk_bias[None], chain[None],
    )
    in_smem = (1, 8)
    scratch = [
        (pltpu.SMEM if at in in_smem else pltpu.VMEM)(arg.shape, arg.dtype)
        for at, arg in enumerate(args)
    ]
    scratch += [
        pltpu.VMEM((tok_count, width), F32),
        pltpu.VMEM((tok_count, channels), F32),
        pltpu.VMEM((tok_count, channels), BF16),
        pltpu.SemaphoreType.DMA((len(plan[0]),)),
        pltpu.SemaphoreType.DMA((len(plan[1]),)),
        pltpu.SemaphoreType.DMA((len(plan[2]),)),
        pltpu.SemaphoreType.DMA((12,)),
        pltpu.SemaphoreType.DMA,
    ]
    moved = sum(arg.size * arg.dtype.itemsize for arg in args)
    return pl.pallas_call(
        functools.partial(single_kernel, plan),
        out_shape=(
            jax.ShapeDtypeStruct((tok_count, channels), BF16),
            jax.ShapeDtypeStruct((tok_count, lanes), BF16),
            jax.ShapeDtypeStruct((device_count, tok_count, lanes), BF16),
        ),
        in_specs=[pl.BlockSpec(memory_space=pltpu.HBM)] * len(args),
        out_specs=(
            pl.BlockSpec(memory_space=pltpu.HBM),
            pl.BlockSpec(memory_space=pltpu.VMEM),
            pl.BlockSpec(memory_space=pltpu.VMEM),
        ),
        scratch_shapes=scratch,
        compiler_params=pltpu.CompilerParams(vmem_limit_bytes=32 * 2**20),
        cost_estimate=pl.CostEstimate(
            flops=2 * tok_count * channels * (width + channels + lanes),
            bytes_accessed=moved,
            transcendentals=0,
        ),
        name="single_path",
    )(*args)


def pair_kernel(
    blocks, query_key, chain, bins, pair_weight, relpos, chain_table,
    pair_hbm, right, table, pair, sem,
):
    tok_count, col_count = bins.shape
    bin_count, lanes_count = relpos.shape
    inner_dim = pair_weight.shape[0] // 2
    half = 2 * inner_dim

    step = chain_table[1:2, :] - chain_table[0:1, :]
    step_high = step.astype(BF16).astype(F32)
    table[...] = jnp.zeros(table.shape, F32)
    table[0:bin_count, :] = relpos[...]
    table[bin_count:bin_count + 1, :] = step_high
    table[bin_count + 1:bin_count + 2, :] = step - step_high
    right[0:inner_dim, :] = pair_weight[0:inner_dim, :]
    right[inner_dim:half, :] = -pair_weight[inner_dim:half, :]
    right[half:, :] = table[...].astype(BF16)

    lanes = lax.broadcasted_iota(jnp.int32, (tok_count, half), 1)
    queries = query_key[...]
    row_base = jnp.dot(
        queries[:, 0:inner_dim], pair_weight[inner_dim:half, :], preferred_element_type=F32
    ) + chain_table[0:1, :]
    queries = jnp.where(lanes < inner_dim, queries.astype(F32), 1.0).astype(BF16)

    lanes = lax.broadcasted_iota(jnp.int32, (col_count, half), 1)
    keys = blocks[...].astype(F32)
    col_chain = keys[:, inner_dim:inner_dim + 1].astype(jnp.int32)
    keys = jnp.where(lanes < inner_dim, keys, pltpu.roll(keys, inner_dim, 1)).astype(BF16)

    lanes = lax.broadcasted_iota(jnp.int32, (col_count, table.shape[0]), 1)
    chain_lanes = (lanes >= bin_count) & (lanes < bin_count + 2)
    col_chain = jnp.where(chain_lanes, col_chain, -1)

    padded = jnp.concatenate(
        [bins[...], jnp.zeros((128 - tok_count, col_count), jnp.int32)], axis=0
    )
    bins_col = padded.T
    copies = []
    for row in range(tok_count):
        products = keys * queries[row:row + 1, :]
        hit = (bins_col[:, row:row + 1] == lanes) | (col_chain == chain[row])
        onehot = jnp.where(hit, 1.0, 0.0).astype(BF16)
        value = jnp.dot(
            jnp.concatenate([products, onehot], axis=1), right[...], preferred_element_type=F32
        )
        pair[row] = (value + row_base[row:row + 1, :]).astype(BF16)
        copy = pltpu.make_async_copy(pair.at[row], pair_hbm.at[row], sem.at[row])
        copy.start()
        copies.append(copy)
    for copy in copies:
        copy.wait()


def pair_part(blocks, query_key, chain, bins, pair_weight, relpos, chain_table):
    tok_count, col_count = bins.shape
    channels = pair_weight.shape[1]
    half = pair_weight.shape[0]
    table_rows = -(-(relpos.shape[0] + 2) // 128) * 128
    vmem = pl.BlockSpec(memory_space=pltpu.VMEM)
    return pl.pallas_call(
        pair_kernel,
        out_shape=jax.ShapeDtypeStruct((tok_count, col_count, channels), BF16),
        in_specs=[vmem, vmem, pl.BlockSpec(memory_space=pltpu.SMEM), vmem, vmem, vmem, vmem],
        out_specs=pl.BlockSpec(memory_space=pltpu.HBM),
        scratch_shapes=[
            pltpu.VMEM((half + table_rows, channels), BF16),
            pltpu.VMEM((table_rows, channels), F32),
            pltpu.VMEM((tok_count, col_count, channels), BF16),
            pltpu.SemaphoreType.DMA((tok_count,)),
        ],
        compiler_params=pltpu.CompilerParams(vmem_limit_bytes=32 * 2**20),
        cost_estimate=pl.CostEstimate(
            flops=2 * tok_count * col_count * channels * (half + table_rows),
            bytes_accessed=2 * tok_count * col_count * channels,
            transcendentals=0,
        ),
        name="pair_rows",
    )(blocks, query_key, chain, bins, pair_weight, relpos, chain_table)


def shards(
    hidden_states,
    layer_mix,
    norm_gain,
    norm_bias,
    proj_in,
    proj_in_bias,
    proj_out,
    proj_out_bias,
    residue_tokens,
    residue_table,
    pair_norm_gain,
    pair_norm_bias,
    qk_weight,
    qk_bias,
    pair_weight,
    relpos_bins,
    relpos_table,
    chain_ids,
    chain_table,
):
    device_count = lax.axis_size("seq")
    single, query_key, copies = single_part(
        device_count,
        (
            hidden_states, layer_mix, norm_gain, norm_bias, proj_in, proj_in_bias, proj_out,
            proj_out_bias, residue_tokens, residue_table, pair_norm_gain, pair_norm_bias,
            qk_weight, qk_bias, chain_ids,
        ),
    )
    blocks = lax.all_to_all(copies, "seq", split_axis=0, concat_axis=0)
    blocks = blocks.reshape(-1, blocks.shape[-1])
    pair = pair_part(
        blocks, query_key, chain_ids, relpos_bins, pair_weight, relpos_table, chain_table
    )
    return (single, pair)


def solution(mesh):
    in_specs = (
        P(None, ("groups", "seq"), None),
        P(),
        P(),
        P(),
        P(),
        P(),
        P(),
        P(),
        P(("groups", "seq")),
        P(),
        P(),
        P(),
        P(),
        P(),
        P(),
        P(("groups", "seq"), None),
        P(),
        P(("groups", "seq")),
        P(),
    )
    out_specs = (P(("groups", "seq"), None), P(("groups", "seq"), None, None))
    return jax.shard_map(shards, mesh=mesh, in_specs=in_specs, out_specs=out_specs, check_vma=False)
```

time: 57.2 us -> 37.1 us (0.65)
  blocking collectives: 40.6 us -> 14.1 us
  local copies, waits for them, and re-layouts: 2.31 us -> 14.6 us
  matrix products: 8.4 us -> 0 us
  Pallas kernels: 0 us -> 7.2 us
  other arithmetic: 4.78 us -> 0 us
    all_gather x2 -> x0, blocking collectives: 40.6 us -> none  [the longest x1 23.1 us: shards(): chain_piece = lax.all_gather(chain_pairs, 'seq', axis=0, tiled=True)]
    all_to_all x0 -> x1, blocking collectives: none -> 14.1 us  [shards(): blocks = lax.all_to_all(copies, 'seq', split_axis=0, concat_axis=0)]
    unnamed x30 -> x34, local copies, waits for them, and re-layouts: 0.9 us -> 13.2 us
    dot_general x7 -> x0, matrix products: 8.4 us -> none  [the longest x1 3.73 us: single_path(): jnp.dot(hidden, proj_out, preferred_element_type=jnp.float32)]
    pallas_call x0 -> x2, Pallas kernels: none -> 7.2 us  [the longest x1 4.92 us: single_part(): pl.pallas_call(functools.partial(single_kernel, plan), out_shape=(jax.Sha...]
    reduce_sum x3 -> x0, other arithmetic: 3.95 us -> none  [the longest x1 3 us: layer_norm(): center = values - jnp.mean(values, axis=-1, keepdims=True)]
    eq x1 -> x0, other arithmetic: 0.73 us -> none  [pair_tile(): same_chain = (row_chain[:, None] == col_chain[None, :])[:, :, None]]
    broadcast_in_dim x1 -> x2, local copies, waits for them, and re-layouts: 0.84 us -> 1.43 us  [the longest x1 0.72 us: single_part(): norm_gain[None]]
where the time goes in v4:
time: 37.1 us; the launch traced here: 36.5 us
  local copies, waits for them, and re-layouts  14.6 us (39%)
  blocking collectives  14.1 us (38%)
  Pallas kernels  7.2 us (19%)
  between operations  0.67 us (2%)
    all_to_all x1, blocking collectives, shards(): blocks = lax.all_to_all(copies, 'seq', split_axis=0, concat_axis=0)  14.1 us
    unnamed x34, local copies, waits for them, and re-layouts  13.2 us
    pallas_call x1, Pallas kernels, single_part(): pl.pallas_call(functools.partial(single_kernel, plan), out_shape=(jax.Sha...  4.92 us
    pallas_call x1, Pallas kernels, pair_part(): pl.pallas_call(pair_kernel, out_shape=jax.ShapeDtypeStruct((tok_count, co...  2.28 us

profile of v4, /device:TPU:0, one launch (start us, length us, event | category | flops | bytes accessed | tf_op | source)
XLA Modules:
  0.0 36.5 jit_solution(13421143455576826320)
XLA Ops:
  0.6 0.7 %broadcast_in_dim.24.norm_gain_hbm = f32[1,2560]{1,0:T(1,128)S(1)} reshape(f32[2560]{0:T(1024)} %param.21) | data formatting | bytes 20480 | tf_op jit(solution)/shard_map/broadcast_in_dim | solution.py:144
  1.3 0.7 %broadcast_in_dim.25.norm_bias_hbm = f32[1,2560]{1,0:T(1,128)S(1)} reshape(f32[2560]{0:T(1024)} %param.22) | data formatting | bytes 20480 | tf_op jit(solution)/shard_map/broadcast_in_dim | solution.py:144
  2.1 0.0 copy-start
  2.1 2.5 %copy-done = bf16[2560,1024]{1,0:T(8,128)(2,1)S(1)} copy-done((bf16[2560,1024]{1,0:T(8,128)(2,1)S(1)}, bf16[2560,1024]{1,0:T(8,128)(2,1)}, u32[]{:S(2)}) %copy-start) | copy-done | bytes 5242904
  4.5 0.0 copy-start.1
  4.5 1.9 %copy-done.1 = bf16[37,16,2560]{2,1,0:T(8,128)(2,1)S(1)} copy-done((bf16[37,16,2560]{2,1,0:T(8,128)(2,1)S(1)}, bf16[37,16,2560]{2,1,0:T(8,128)(2,1)}, u32[]{:S(2)}) %copy-start.1) | copy-done | bytes 3031064
  6.4 0.0 copy-start.2
  6.4 1.6 %copy-done.2 = bf16[1024,1024]{1,0:T(8,128)(2,1)S(1)} copy-done((bf16[1024,1024]{1,0:T(8,128)(2,1)S(1)}, bf16[1024,1024]{1,0:T(8,128)(2,1)}, u32[]{:S(2)}) %copy-start.2) | copy-done | bytes 2097176
  8.0 0.0 copy-start.3
  8.0 0.9 %copy-done.3 = bf16[1024,128]{1,0:T(8,128)(2,1)S(1)} copy-done((bf16[1024,128]{1,0:T(8,128)(2,1)S(1)}, bf16[1024,128]{1,0:T(8,128)(2,1)}, u32[]{:S(2)}) %copy-start.3) | copy-done | bytes 262168
  8.9 0.0 copy-start.4
  8.9 0.9 %copy-done.4 = f32[23,1024]{1,0:T(8,128)S(1)} copy-done((f32[23,1024]{1,0:T(8,128)S(1)}, f32[23,1024]{1,0:T(8,128)}, u32[]{:S(2)}) %copy-start.4) | copy-done | bytes 94232
  9.8 0.0 copy-start.8
  9.8 0.7 %copy-done.8 = f32[1024]{0:T(1024)S(1)} copy-done((f32[1024]{0:T(1024)S(1)}, f32[1024]{0:T(1024)}, u32[]{:S(2)}) %copy-start.8) | copy-done | bytes 4120
  10.5 0.0 copy-start.9
  10.5 0.7 %copy-done.9 = f32[1024]{0:T(1024)S(1)} copy-done((f32[1024]{0:T(1024)S(1)}, f32[1024]{0:T(1024)}, u32[]{:S(2)}) %copy-start.9) | copy-done | bytes 4120
  11.2 0.0 copy-start.10
  11.2 0.7 %copy-done.10 = f32[1024]{0:T(1024)S(1)} copy-done((f32[1024]{0:T(1024)S(1)}, f32[1024]{0:T(1024)}, u32[]{:S(2)}) %copy-start.10) | copy-done | bytes 4120
  11.9 0.0 copy-start.11
  11.9 0.7 %copy-done.11 = f32[1024]{0:T(1024)S(1)} copy-done((f32[1024]{0:T(1024)S(1)}, f32[1024]{0:T(1024)}, u32[]{:S(2)}) %copy-start.11) | copy-done | bytes 4120
  12.6 0.0 copy-start.12
  12.6 0.7 %copy-done.12 = s32[16]{0:T(128)S(1)} copy-done((s32[16]{0:T(128)S(1)}, s32[16]{0:T(128)}, u32[]{:S(2)}) %copy-start.12) | copy-done | bytes 88
  13.2 0.0 copy-start.14
  13.2 0.7 %copy-done.14 = f32[37]{0:T(128)S(1)} copy-done((f32[37]{0:T(128)S(1)}, f32[37]{0:T(128)}, u32[]{:S(2)}) %copy-start.14) | copy-done | bytes 172
  13.9 0.0 copy-start.15
  13.9 0.7 %copy-done.15 = s32[16]{0:T(128)S(1)} copy-done((s32[16]{0:T(128)S(1)}, s32[16]{0:T(128)}, u32[]{:S(2)}) %copy-start.15) | copy-done | bytes 88
  14.6 0.0 copy-start.16
  14.6 0.7 %copy-done.16 = f32[128]{0:T(128)S(1)} copy-done((f32[128]{0:T(128)S(1)}, f32[128]{0:T(128)}, u32[]{:S(2)}) %copy-start.16) | copy-done | bytes 536
  15.2 0.0 copy-start.5
  15.2 0.0 copy-start.6
  15.2 0.0 copy-start.7
  15.2 0.0 copy-start.13
  15.2 4.9 %single_path.1 = (bf16[16,1024]{1,0:T(8,128)(2,1)}, bf16[16,128]{1,0:T(8,128)(2,1)S(1)}, bf16[16,16,128]{2,1,0:T(8,128)(2,1)S(1)}) custom-call(bf16[37,16,2560]{2,1,0:T(8,128)(2,1)S(1)} %copy-done.1, f32[37]{0:T(128)S(1)} %copy-done.14, f32[1,2560]{1,0:T(1,128)S(1)} %broadcast_in_dim.24.norm_gain_hbm, f32[1,2560]{1,0:T(1,128)S(1)} %broadcast_in_dim.25.norm_bias_hbm, ...), custom_call_target="tpu_custom_call" | custom-call | flops 121634816 | bytes 10765076 | tf_op jit(solution)/shard_map/single_path/pallas_call | solution.py:164
  20.1 14.1 %all_to_all.5 = bf16[16,16,128]{2,1,0:T(8,128)(2,1)S(1)} all-to-all(bf16[16,16,128]{2,1,0:T(8,128)(2,1)S(1)} %get-tuple-element.6), channel_id=1, replica_groups=mesh['groups'=2,'seq'=16] {'seq'}, dimensions={0} | all-to-all | bytes 131072 | tf_op jit(solution)/shard_map/all_to_all | solution.py:300
  34.2 0.0 copy-done.5
  34.2 0.0 copy-done.6
  34.2 0.0 copy-done.7
  34.2 0.0 copy-done.13
  34.3 2.3 %pair_rows.1 = bf16[16,256,128]{2,1,0:T(8,128)(2,1)} custom-call(bf16[256,128]{1,0:T(8,128)(2,1)S(1)} %bitcast.7, bf16[16,128]{1,0:T(8,128)(2,1)S(1)} %get-tuple-element.7.query_key, s32[16]{0:T(128)S(1)} %copy-done.12, s32[16,256]{1,0:T(8,128)S(1)} %copy-done.7, bf16[128,128]{1,0:T(8,128)(2,1)S(1)} %copy-done.6, f32[66,128]{1,0:T(8,128)S(1)} %copy-done.5, ...), custom_call_target="tpu_custom_call" | custom-call | flops 268435456 | bytes 1048576 | tf_op jit(solution)/shard_map/pair_rows/pallas_call | solution.py:249
Async XLA Ops:
  2.1 2.5 %copy-start = (bf16[2560,1024]{1,0:T(8,128)(2,1)S(1)}, bf16[2560,1024]{1,0:T(8,128)(2,1)}, u32[]{:S(2)}) copy-start(bf16[2560,1024]{1,0:T(8,128)(2,1)} %proj_in_hbm.1) | copy-start | bytes 15728644
  4.5 1.9 %copy-start.1 = (bf16[37,16,2560]{2,1,0:T(8,128)(2,1)S(1)}, bf16[37,16,2560]{2,1,0:T(8,128)(2,1)}, u32[]{:S(2)}) copy-start(bf16[37,16,2560]{2,1,0:T(8,128)(2,1)} %hidden_hbm.1) | copy-start | bytes 9093124
  6.4 1.6 %copy-start.2 = (bf16[1024,1024]{1,0:T(8,128)(2,1)S(1)}, bf16[1024,1024]{1,0:T(8,128)(2,1)}, u32[]{:S(2)}) copy-start(bf16[1024,1024]{1,0:T(8,128)(2,1)} %proj_out_hbm.1) | copy-start | bytes 6291460
  8.0 0.9 %copy-start.3 = (bf16[1024,128]{1,0:T(8,128)(2,1)S(1)}, bf16[1024,128]{1,0:T(8,128)(2,1)}, u32[]{:S(2)}) copy-start(bf16[1024,128]{1,0:T(8,128)(2,1)} %qk_hbm.1) | copy-start | bytes 786436
  8.9 0.9 %copy-start.4 = (f32[23,1024]{1,0:T(8,128)S(1)}, f32[23,1024]{1,0:T(8,128)}, u32[]{:S(2)}) copy-start(f32[23,1024]{1,0:T(8,128)} %residue_hbm.1) | copy-start | bytes 282628
  9.8 0.7 %copy-start.8 = (f32[1024]{0:T(1024)S(1)}, f32[1024]{0:T(1024)}, u32[]{:S(2)}) copy-start(f32[1024]{0:T(1024)} %param.24) | copy-start | bytes 12292
  10.5 0.7 %copy-start.9 = (f32[1024]{0:T(1024)S(1)}, f32[1024]{0:T(1024)}, u32[]{:S(2)}) copy-start(f32[1024]{0:T(1024)} %param.26) | copy-start | bytes 12292
  11.2 0.7 %copy-start.10 = (f32[1024]{0:T(1024)S(1)}, f32[1024]{0:T(1024)}, u32[]{:S(2)}) copy-start(f32[1024]{0:T(1024)} %param.29) | copy-start | bytes 12292
  11.9 0.7 %copy-start.11 = (f32[1024]{0:T(1024)S(1)}, f32[1024]{0:T(1024)}, u32[]{:S(2)}) copy-start(f32[1024]{0:T(1024)} %param.30) | copy-start | bytes 12292
  12.6 0.7 %copy-start.12 = (s32[16]{0:T(128)S(1)}, s32[16]{0:T(128)}, u32[]{:S(2)}) copy-start(s32[16]{0:T(128)} %chain.1) | copy-start | bytes 196
  13.2 0.7 %copy-start.14 = (f32[37]{0:T(128)S(1)}, f32[37]{0:T(128)}, u32[]{:S(2)}) copy-start(f32[37]{0:T(128)} %mix_hbm.1) | copy-start | bytes 448
  13.9 0.7 %copy-start.15 = (s32[16]{0:T(128)S(1)}, s32[16]{0:T(128)}, u32[]{:S(2)}) copy-start(s32[16]{0:T(128)} %tokens_hbm.1) | copy-start | bytes 196
  14.6 0.7 %copy-start.16 = (f32[128]{0:T(128)S(1)}, f32[128]{0:T(128)}, u32[]{:S(2)}) copy-start(f32[128]{0:T(128)} %param.32) | copy-start | bytes 1540
  15.2 19.0 %copy-start.5 = (f32[66,128]{1,0:T(8,128)S(1)}, f32[66,128]{1,0:T(8,128)}, u32[]{:S(2)}) copy-start(f32[66,128]{1,0:T(8,128)} %relpos.1) | copy-start | bytes 101380
  15.2 19.0 %copy-start.6 = (bf16[128,128]{1,0:T(8,128)(2,1)S(1)}, bf16[128,128]{1,0:T(8,128)(2,1)}, u32[]{:S(2)}) copy-start(bf16[128,128]{1,0:T(8,128)(2,1)} %pair_weight.1) | copy-start | bytes 98308
  15.2 19.0 %copy-start.7 = (s32[16,256]{1,0:T(8,128)S(1)}, s32[16,256]{1,0:T(8,128)}, u32[]{:S(2)}) copy-start(s32[16,256]{1,0:T(8,128)} %bins.1) | copy-start | bytes 49156
  15.2 19.0 %copy-start.13 = (f32[2,128]{1,0:T(2,128)S(1)}, f32[2,128]{1,0:T(2,128)}, u32[]{:S(2)}) copy-start(f32[2,128]{1,0:T(2,128)} %chain_table.1) | copy-start | bytes 3076

commit v5 on v4

--- a/solution.py
+++ b/solution.py
@@ -92,7 +92,9 @@
     for row in range(tok_count):
         residue_rows[pl.ds(row, 1), :] = residue[pl.ds(tokens[row], 1), :]
 
-    normed = row_norm(mixture[...], norm_gain[...], norm_bias[...]).astype(BF16)
+    normed = row_norm(
+        mixture[...], norm_gain[...].reshape(1, width), norm_bias[...].reshape(1, width)
+    ).astype(BF16)
     total = None
     for at, (low, size) in enumerate(in_pieces):
         firsts[at].wait()
@@ -141,7 +143,7 @@
     lanes = qk.shape[1]
     plan = (pieces(state_count, 4), pieces(width, 5), pieces(channels, 2), 512)
     args = (
-        hidden, mix, norm_gain[None], norm_bias[None], proj_in, proj_in_bias[None],
+        hidden, mix, norm_gain, norm_bias, proj_in, proj_in_bias[None],
         proj_out, proj_out_bias[None], tokens, residue, pair_gain[None], pair_bias[None],
         qk, qk_bias[None], chain[None],
     )
@@ -175,7 +177,7 @@
             pl.BlockSpec(memory_space=pltpu.VMEM),
         ),
         scratch_shapes=scratch,
-        compiler_params=pltpu.CompilerParams(vmem_limit_bytes=32 * 2**20),
+        compiler_params=pltpu.CompilerParams(vmem_limit_bytes=60 * 2**20),
         cost_estimate=pl.CostEstimate(
             flops=2 * tok_count * channels * (width + channels + lanes),
             bytes_accessed=moved,
@@ -257,7 +259,7 @@
             pltpu.VMEM((tok_count, col_count, channels), BF16),
             pltpu.SemaphoreType.DMA((tok_count,)),
         ],
-        compiler_params=pltpu.CompilerParams(vmem_limit_bytes=32 * 2**20),
+        compiler_params=pltpu.CompilerParams(vmem_limit_bytes=60 * 2**20),
         cost_estimate=pl.CostEstimate(
             flops=2 * tok_count * col_count * channels * (half + table_rows),
             bytes_accessed=2 * tok_count * col_count * channels,

time: 37.1 us -> 24.7 us (0.67)
  local copies, waits for them, and re-layouts: 14.6 us -> 0 us
  Pallas kernels: 7.2 us -> 9.4 us
    unnamed x34 -> x0, local copies, waits for them, and re-layouts: 13.2 us -> none
    pallas_call x1, Pallas kernels: 4.92 us -> 6.79 us  [single_part(): pl.pallas_call(functools.partial(single_kernel, plan), out_shape=(jax.Sha...]
    broadcast_in_dim x2 -> x0, local copies, waits for them, and re-layouts: 1.43 us -> none  [the longest x1 0.72 us: single_part(): norm_gain[None]]
where the time goes in v5:
time: 24.7 us; the launch traced here: 24.4 us
  blocking collectives  14.4 us (58%)
  Pallas kernels  9.4 us (38%)
  between operations  0.64 us (3%)
    all_to_all x1, blocking collectives, shards(): blocks = lax.all_to_all(copies, 'seq', split_axis=0, concat_axis=0)  14.4 us
    pallas_call x1, Pallas kernels, single_part(): pl.pallas_call(functools.partial(single_kernel, plan), out_shape=(jax.Sha...  6.79 us
    pallas_call x1, Pallas kernels, pair_part(): pl.pallas_call(pair_kernel, out_shape=jax.ShapeDtypeStruct((tok_count, co...  2.62 us

profile of v5, /device:TPU:0, one launch (start us, length us, event | category | flops | bytes accessed | tf_op | source)
XLA Modules:
  0.0 24.4 jit_solution(18311150255318769678)
XLA Ops:
  0.6 6.8 %single_path.1 = (bf16[16,1024]{1,0:T(8,128)(2,1)}, bf16[16,128]{1,0:T(8,128)(2,1)}, bf16[16,16,128]{2,1,0:T(8,128)(2,1)}) custom-call(bf16[37,16,2560]{2,1,0:T(8,128)(2,1)} %hidden_hbm.1, f32[37]{0:T(128)} %mix_hbm.1, f32[2560]{0:T(1024)} %norm_gain_hbm.1, f32[2560]{0:T(1024)} %norm_bias_hbm.1, bf16[2560,1024]{1,0:T(8,128)(2,1)} %proj_in_hbm.1, ...), custom_call_target="tpu_custom_call" | custom-call | flops 121634816 | bytes 10765076 | tf_op jit(solution)/shard_map/single_path/pallas_call | solution.py:166
  7.4 14.4 %all_to_all.5 = bf16[16,16,128]{2,1,0:T(8,128)(2,1)} all-to-all(bf16[16,16,128]{2,1,0:T(8,128)(2,1)} %get-tuple-element.6), channel_id=1, replica_groups=mesh['groups'=2,'seq'=16] {'seq'}, dimensions={0} | all-to-all | bytes 131072 | tf_op jit(solution)/shard_map/all_to_all | solution.py:302
  21.8 2.6 %pair_rows.1 = bf16[16,256,128]{2,1,0:T(8,128)(2,1)} custom-call(bf16[256,128]{1,0:T(8,128)(2,1)} %bitcast.7, bf16[16,128]{1,0:T(8,128)(2,1)} %get-tuple-element.7.query_key, s32[16]{0:T(128)} %chain.1, s32[16,256]{1,0:T(8,128)} %bins.1, bf16[128,128]{1,0:T(8,128)(2,1)} %pair_weight.1, f32[66,128]{1,0:T(8,128)} %relpos.1, f32[2,128]{1,0:T(2,128)} %chain_table.1), custom_call_target="tpu_custom_call" | custom-call | flops 268435456 | bytes 1048576 | tf_op jit(solution)/shard_map/pair_rows/pallas_call | solution.py:251

commit v6 on v5

--- a/solution.py
+++ b/solution.py
@@ -70,15 +70,19 @@
     small[0].start()
     for copy in states:
         copy.start()
+    firsts[0].start()
     for copy in small[1:]:
         copy.start()
-    for copy in firsts + seconds:
-        copy.start()
+    later = firsts[1:] + seconds
 
     small[0].wait()
     width = mixture.shape[1]
     for at, (low, size) in enumerate(state_pieces):
         states[at].wait()
+        last = at == len(state_pieces) - 1
+        for copy in later if last else later[:1]:
+            copy.start()
+        later = later[1:]
         for lane in range(0, width, lane_step):
             span = slice(lane, min(lane + lane_step, width))
             total = mixture[:, span] if at else None
@@ -89,9 +93,6 @@
 
     for copy in small[1:]:
         copy.wait()
-    for row in range(tok_count):
-        residue_rows[pl.ds(row, 1), :] = residue[pl.ds(tokens[row], 1), :]
-
     normed = row_norm(
         mixture[...], norm_gain[...].reshape(1, width), norm_bias[...].reshape(1, width)
     ).astype(BF16)
@@ -102,6 +103,8 @@
             normed[:, low:low + size], proj_in[pl.ds(low, size), :], preferred_element_type=F32
         )
         total = term if total is None else total + term
+    for row in range(tok_count):
+        residue_rows[pl.ds(row, 1), :] = residue[pl.ds(tokens[row], 1), :]
     middle = jnp.maximum(total + proj_in_bias[...], 0.0).astype(BF16)
 
     total = None
@@ -141,12 +144,13 @@
     state_count, tok_count, width = hidden.shape
     channels = proj_out.shape[1]
     lanes = qk.shape[1]
-    plan = (pieces(state_count, 4), pieces(width, 5), pieces(channels, 2), 512)
+    plan = (pieces(state_count, 6), pieces(width, 5), pieces(channels, 2), 512)
     args = (
         hidden, mix, norm_gain, norm_bias, proj_in, proj_in_bias[None],
         proj_out, proj_out_bias[None], tokens, residue, pair_gain[None], pair_bias[None],
         qk, qk_bias[None], chain[None],
     )
+    args = [pltpu.with_memory_space_constraint(arg, pltpu.HBM) for arg in args]
     in_smem = (1, 8)
     scratch = [
         (pltpu.SMEM if at in in_smem else pltpu.VMEM)(arg.shape, arg.dtype)
@@ -177,7 +181,7 @@
             pl.BlockSpec(memory_space=pltpu.VMEM),
         ),
         scratch_shapes=scratch,
-        compiler_params=pltpu.CompilerParams(vmem_limit_bytes=60 * 2**20),
+        compiler_params=pltpu.CompilerParams(vmem_limit_bytes=32 * 2**20),
         cost_estimate=pl.CostEstimate(
             flops=2 * tok_count * channels * (width + channels + lanes),
             bytes_accessed=moved,
@@ -259,7 +263,7 @@
             pltpu.VMEM((tok_count, col_count, channels), BF16),
             pltpu.SemaphoreType.DMA((tok_count,)),
         ],
-        compiler_params=pltpu.CompilerParams(vmem_limit_bytes=60 * 2**20),
+        compiler_params=pltpu.CompilerParams(vmem_limit_bytes=32 * 2**20),
         cost_estimate=pl.CostEstimate(
             flops=2 * tok_count * col_count * channels * (half + table_rows),
             bytes_accessed=2 * tok_count * col_count * channels,

time: 24.7 us -> 22.9 us (0.927)
  Pallas kernels: 9.4 us -> 7.89 us
  blocking collectives: 14.4 us -> 14.1 us
    pallas_call x1, Pallas kernels: 6.79 us -> 5.61 us  [single_part(): pl.pallas_call(functools.partial(single_kernel, plan), out_shape=(jax.Sha...]
    pallas_call x1, Pallas kernels: 2.62 us -> 2.28 us  [pair_part(): pl.pallas_call(pair_kernel, out_shape=jax.ShapeDtypeStruct((tok_count, co...]
    all_to_all x1, blocking collectives: 14.4 us -> 14.1 us  [shards(): blocks = lax.all_to_all(copies, 'seq', split_axis=0, concat_axis=0)]
where the time goes in v6:
time: 22.9 us; the launch traced here: 22.7 us
  blocking collectives  14.1 us (62%)
  Pallas kernels  7.89 us (34%)
  between operations  0.71 us (3%)
    all_to_all x1, blocking collectives, shards(): blocks = lax.all_to_all(copies, 'seq', split_axis=0, concat_axis=0)  14.1 us
    pallas_call x1, Pallas kernels, single_part(): pl.pallas_call(functools.partial(single_kernel, plan), out_shape=(jax.Sha...  5.61 us
    pallas_call x1, Pallas kernels, pair_part(): pl.pallas_call(pair_kernel, out_shape=jax.ShapeDtypeStruct((tok_count, co...  2.28 us

profile of v6, /device:TPU:0, one launch (start us, length us, event | category | flops | bytes accessed | tf_op | source)
XLA Modules:
  0.0 22.7 jit_solution(13463464169765640739)
XLA Ops:
  0.6 0.0 copy-start
  0.6 0.0 copy-start.1
  0.7 0.0 copy-start.2
  0.7 0.0 copy-start.3
  0.7 0.0 copy-start.4
  0.7 5.6 %single_path.1 = (bf16[16,1024]{1,0:T(8,128)(2,1)}, bf16[16,128]{1,0:T(8,128)(2,1)S(1)}, bf16[16,16,128]{2,1,0:T(8,128)(2,1)S(1)}) custom-call(bf16[37,16,2560]{2,1,0:T(8,128)(2,1)} %hidden_hbm.1, f32[37]{0:T(128)} %mix_hbm.1, f32[2560]{0:T(1024)} %norm_gain_hbm.1, f32[2560]{0:T(1024)} %norm_bias_hbm.1, bf16[2560,1024]{1,0:T(8,128)(2,1)} %proj_in_hbm.1, ...), custom_call_target="tpu_custom_call" | custom-call | flops 121634816 | bytes 10765076 | tf_op jit(solution)/shard_map/single_path/pallas_call | solution.py:170
  6.3 14.1 %all_to_all.5 = bf16[16,16,128]{2,1,0:T(8,128)(2,1)S(1)} all-to-all(bf16[16,16,128]{2,1,0:T(8,128)(2,1)S(1)} %get-tuple-element.6), channel_id=1, replica_groups=mesh['groups'=2,'seq'=16] {'seq'}, dimensions={0} | all-to-all | bytes 131072 | tf_op jit(solution)/shard_map/all_to_all | solution.py:306
  20.4 0.0 copy-done
  20.4 0.0 copy-done.1
  20.4 0.0 copy-done.2
  20.4 0.0 copy-done.3
  20.4 0.0 copy-done.4
  20.4 2.3 %pair_rows.1 = bf16[16,256,128]{2,1,0:T(8,128)(2,1)} custom-call(bf16[256,128]{1,0:T(8,128)(2,1)S(1)} %bitcast.7, bf16[16,128]{1,0:T(8,128)(2,1)S(1)} %get-tuple-element.7.query_key, s32[16]{0:T(128)S(1)} %copy-done.3, s32[16,256]{1,0:T(8,128)S(1)} %copy-done.2, bf16[128,128]{1,0:T(8,128)(2,1)S(1)} %copy-done.1, f32[66,128]{1,0:T(8,128)S(1)} %copy-done, ...), custom_call_target="tpu_custom_call" | custom-call | flops 268435456 | bytes 1048576 | tf_op jit(solution)/shard_map/pair_rows/pallas_call | solution.py:255
Async XLA Ops:
  0.6 19.8 %copy-start = (f32[66,128]{1,0:T(8,128)S(1)}, f32[66,128]{1,0:T(8,128)}, u32[]{:S(2)}) copy-start(f32[66,128]{1,0:T(8,128)} %relpos.1) | copy-start | bytes 101380
  0.6 19.7 %copy-start.1 = (bf16[128,128]{1,0:T(8,128)(2,1)S(1)}, bf16[128,128]{1,0:T(8,128)(2,1)}, u32[]{:S(2)}) copy-start(bf16[128,128]{1,0:T(8,128)(2,1)} %pair_weight.1) | copy-start | bytes 98308
  0.7 19.7 %copy-start.2 = (s32[16,256]{1,0:T(8,128)S(1)}, s32[16,256]{1,0:T(8,128)}, u32[]{:S(2)}) copy-start(s32[16,256]{1,0:T(8,128)} %bins.1) | copy-start | bytes 49156
  0.7 19.7 %copy-start.3 = (s32[16]{0:T(128)S(1)}, s32[16]{0:T(128)}, u32[]{:S(2)}) copy-start(s32[16]{0:T(128)} %chain.1) | copy-start | bytes 196
  0.7 19.7 %copy-start.4 = (f32[2,128]{1,0:T(2,128)S(1)}, f32[2,128]{1,0:T(2,128)}, u32[]{:S(2)}) copy-start(f32[2,128]{1,0:T(2,128)} %chain_table.1) | copy-start | bytes 3076

commit v7 on v6

--- a/solution.py
+++ b/solution.py
@@ -138,7 +138,7 @@
     out_copy.wait()
 
 
-def single_part(device_count, operands):
+def single_part(copy_count, operands):
     (hidden, mix, norm_gain, norm_bias, proj_in, proj_in_bias, proj_out, proj_out_bias, tokens,
      residue, pair_gain, pair_bias, qk, qk_bias, chain) = operands
     state_count, tok_count, width = hidden.shape
@@ -172,7 +172,7 @@
         out_shape=(
             jax.ShapeDtypeStruct((tok_count, channels), BF16),
             jax.ShapeDtypeStruct((tok_count, lanes), BF16),
-            jax.ShapeDtypeStruct((device_count, tok_count, lanes), BF16),
+            jax.ShapeDtypeStruct((copy_count, tok_count, lanes), BF16),
         ),
         in_specs=[pl.BlockSpec(memory_space=pltpu.HBM)] * len(args),
         out_specs=(
@@ -192,7 +192,7 @@
 
 
 def pair_kernel(
-    blocks, query_key, chain, bins, pair_weight, relpos, chain_table,
+    blocks, other, query_key, chain, bins, pair_weight, relpos, chain_table,
     pair_hbm, right, table, pair, sem,
 ):
     tok_count, col_count = bins.shape
@@ -218,7 +218,12 @@
     queries = jnp.where(lanes < inner_dim, queries.astype(F32), 1.0).astype(BF16)
 
     lanes = lax.broadcasted_iota(jnp.int32, (col_count, half), 1)
-    keys = blocks[...].astype(F32)
+    odd = lax.axis_index("seq") % 2 == 1
+    own_blocks, other_blocks = blocks[...].astype(F32), other[...].astype(F32)
+    keys = jnp.stack(
+        [jnp.where(odd, other_blocks, own_blocks), jnp.where(odd, own_blocks, other_blocks)],
+        axis=1,
+    ).reshape(col_count, half)
     col_chain = keys[:, inner_dim:inner_dim + 1].astype(jnp.int32)
     keys = jnp.where(lanes < inner_dim, keys, pltpu.roll(keys, inner_dim, 1)).astype(BF16)
 
@@ -246,7 +251,7 @@
         copy.wait()
 
 
-def pair_part(blocks, query_key, chain, bins, pair_weight, relpos, chain_table):
+def pair_part(blocks, other, query_key, chain, bins, pair_weight, relpos, chain_table):
     tok_count, col_count = bins.shape
     channels = pair_weight.shape[1]
     half = pair_weight.shape[0]
@@ -255,7 +260,7 @@
     return pl.pallas_call(
         pair_kernel,
         out_shape=jax.ShapeDtypeStruct((tok_count, col_count, channels), BF16),
-        in_specs=[vmem, vmem, pl.BlockSpec(memory_space=pltpu.SMEM), vmem, vmem, vmem, vmem],
+        in_specs=[vmem, vmem, vmem, pl.BlockSpec(memory_space=pltpu.SMEM)] + [vmem] * 4,
         out_specs=pl.BlockSpec(memory_space=pltpu.HBM),
         scratch_shapes=[
             pltpu.VMEM((half + table_rows, channels), BF16),
@@ -270,7 +275,7 @@
             transcendentals=0,
         ),
         name="pair_rows",
-    )(blocks, query_key, chain, bins, pair_weight, relpos, chain_table)
+    )(blocks, other, query_key, chain, bins, pair_weight, relpos, chain_table)
 
 
 def shards(
@@ -296,17 +301,20 @@
 ):
     device_count = lax.axis_size("seq")
     single, query_key, copies = single_part(
-        device_count,
+        device_count // 2,
         (
             hidden_states, layer_mix, norm_gain, norm_bias, proj_in, proj_in_bias, proj_out,
             proj_out_bias, residue_tokens, residue_table, pair_norm_gain, pair_norm_bias,
             qk_weight, qk_bias, chain_ids,
         ),
     )
-    blocks = lax.all_to_all(copies, "seq", split_axis=0, concat_axis=0)
-    blocks = blocks.reshape(-1, blocks.shape[-1])
+    chips = [list(range(core, device_count, 2)) for core in range(2)]
+    blocks = lax.all_to_all(
+        copies, "seq", split_axis=0, concat_axis=0, axis_index_groups=chips
+    )
+    other = lax.ppermute(blocks, "seq", [(at, at ^ 1) for at in range(device_count)])
     pair = pair_part(
-        blocks, query_key, chain_ids, relpos_bins, pair_weight, relpos_table, chain_table
+        blocks, other, query_key, chain_ids, relpos_bins, pair_weight, relpos_table, chain_table
     )
     return (single, pair)
 

time: 22.9 us -> 23.8 us (1.039)
  waiting for transfers between devices: 0 us -> 1.2 us
  blocking collectives: 14.1 us -> 13.8 us
    ppermute x0 -> x1, waiting for transfers between devices: none -> 1.2 us  [shards(): lax.ppermute(blocks, 'seq', [(at, at ^ 1) for at in range(device_count)])]
    all_to_all x1, blocking collectives: 14.1 us -> 13.8 us  [shards(): lax.all_to_all(copies, 'seq', split_axis=0, concat_axis=0, axis_index_gro...]
  transfers between devices with their start and end apart: 0 -> 1, of which waited for: 0 -> 1; matrix products, arithmetic and copies ran while one was open for 0% -> 0% of each run, Pallas kernels for 0% -> 0%
where the time goes in v7:
time: 23.8 us; the launch traced here: 23.6 us
  blocking collectives  13.8 us (58%)
  Pallas kernels  7.89 us (33%)
  waiting for transfers between devices  1.2 us (5%)
  between operations  0.71 us (3%)
    all_to_all x1, blocking collectives, shards(): lax.all_to_all(copies, 'seq', split_axis=0, concat_axis=0, axis_index_gro...  13.8 us
    pallas_call x1, Pallas kernels, single_part(): pl.pallas_call(functools.partial(single_kernel, plan), out_shape=(jax.Sha...  5.61 us
    pallas_call x1, Pallas kernels, pair_part(): pl.pallas_call(pair_kernel, out_shape=jax.ShapeDtypeStruct((tok_count, co...  2.28 us
    ppermute x1, waiting for transfers between devices, shards(): lax.ppermute(blocks, 'seq', [(at, at ^ 1) for at in range(device_count)])  1.2 us
  transfers between devices with their start and end apart: 1, of which 1 were waited for; matrix products, arithmetic and copies ran while one was open for 0% of the time, Pallas kernels for 0%

profile of v7, /device:TPU:0, one launch (start us, length us, event | category | flops | bytes accessed | tf_op | source)
XLA Modules:
  0.0 23.6 jit_solution(8484466834092907518)
XLA Ops:
  0.6 0.0 copy-start
  0.6 0.0 copy-start.1
  0.7 0.0 copy-start.2
  0.7 0.0 copy-start.3
  0.7 0.0 copy-start.4
  0.7 5.6 %single_path.1 = (bf16[16,1024]{1,0:T(8,128)(2,1)}, bf16[16,128]{1,0:T(8,128)(2,1)S(1)}, bf16[8,16,128]{2,1,0:T(8,128)(2,1)S(1)}) custom-call(bf16[37,16,2560]{2,1,0:T(8,128)(2,1)} %hidden_hbm.1, f32[37]{0:T(128)} %mix_hbm.1, f32[2560]{0:T(1024)} %norm_gain_hbm.1, f32[2560]{0:T(1024)} %norm_bias_hbm.1, bf16[2560,1024]{1,0:T(8,128)(2,1)} %proj_in_hbm.1, ...), custom_call_target="tpu_custom_call" | custom-call | flops 121634816 | bytes 10765076 | tf_op jit(solution)/shard_map/single_path/pallas_call | solution.py:170
  6.3 13.8 %all_to_all.5.blocks = bf16[8,16,128]{2,1,0:T(8,128)(2,1)S(1)} all-to-all(bf16[8,16,128]{2,1,0:T(8,128)(2,1)S(1)} %get-tuple-element.6), channel_id=1, replica_groups={{0,2,4,6,8,10,12,14},{1,3,5,7,9,11,13,15},{16,18,20,22,24,26,28,30},{17..., dimensions={0} | all-to-all | bytes 65536 | tf_op jit(solution)/shard_map/all_to_all | solution.py:312
  20.1 0.0 collective-permute-start
  20.1 1.2 %collective-permute-done.other = bf16[8,16,128]{2,1,0:T(8,128)(2,1)S(1)} collective-permute-done((bf16[8,16,128]{2,1,0:T(8,128)(2,1)S(1)}, bf16[8,16,128]{2,1,0:T(8,128)(2,1)S(1)}, u32[]{:S(2)}, u32[]{:S(2)}) %collective-permute-start) | collective-permute-done | bytes 32800 | tf_op jit(solution)/shard_map/ppermute | solution.py:315
  21.3 0.0 copy-done
  21.3 0.0 copy-done.1
  21.3 0.0 copy-done.2
  21.3 0.0 copy-done.3
  21.3 0.0 copy-done.4
  21.3 2.3 %pair_rows.1 = bf16[16,256,128]{2,1,0:T(8,128)(2,1)} custom-call(bf16[8,16,128]{2,1,0:T(8,128)(2,1)S(1)} %all_to_all.5.blocks, bf16[8,16,128]{2,1,0:T(8,128)(2,1)S(1)} %collective-permute-done.other, bf16[16,128]{1,0:T(8,128)(2,1)S(1)} %get-tuple-element.7.query_key, s32[16]{0:T(128)S(1)} %copy-done.3, s32[16,256]{1,0:T(8,128)S(1)} %copy-done.2, ...), custom_call_target="tpu_custom_call" | custom-call | flops 268435456 | bytes 1048576 | tf_op jit(solution)/shard_map/pair_rows/pallas_call | solution.py:260
Async XLA Ops:
  0.6 20.6 %copy-start = (f32[66,128]{1,0:T(8,128)S(1)}, f32[66,128]{1,0:T(8,128)}, u32[]{:S(2)}) copy-start(f32[66,128]{1,0:T(8,128)} %relpos.1) | copy-start | bytes 101380
  0.6 20.6 %copy-start.1 = (bf16[128,128]{1,0:T(8,128)(2,1)S(1)}, bf16[128,128]{1,0:T(8,128)(2,1)}, u32[]{:S(2)}) copy-start(bf16[128,128]{1,0:T(8,128)(2,1)} %pair_weight.1) | copy-start | bytes 98308
  0.7 20.6 %copy-start.2 = (s32[16,256]{1,0:T(8,128)S(1)}, s32[16,256]{1,0:T(8,128)}, u32[]{:S(2)}) copy-start(s32[16,256]{1,0:T(8,128)} %bins.1) | copy-start | bytes 49156
  0.7 20.6 %copy-start.3 = (s32[16]{0:T(128)S(1)}, s32[16]{0:T(128)}, u32[]{:S(2)}) copy-start(s32[16]{0:T(128)} %chain.1) | copy-start | bytes 196
  0.7 20.6 %copy-start.4 = (f32[2,128]{1,0:T(2,128)S(1)}, f32[2,128]{1,0:T(2,128)}, u32[]{:S(2)}) copy-start(f32[2,128]{1,0:T(2,128)} %chain_table.1) | copy-start | bytes 3076
  20.1 1.2 %collective-permute-start = (bf16[8,16,128]{2,1,0:T(8,128)(2,1)S(1)}, bf16[8,16,128]{2,1,0:T(8,128)(2,1)S(1)}, u32[]{:S(2)}, u32[]{:S(2)}) collective-permute-start(bf16[8,16,128]{2,1,0:T(8,128)(2,1)S(1)} %all_to_all.5.blocks), channel_id=1, source_target_pairs={{0,1},{1,0},{2,3},{3,2},{4,5},{5,4},{6,7},{7,6},{8,9},{9,8},{10,11... | collective-permute-start | bytes 98312 | tf_op jit(solution)/shard_map/ppermute | solution.py:315

commit v8 on v6

--- a/solution.py
+++ b/solution.py
@@ -29,7 +29,7 @@
     hidden_hbm, mix_hbm, norm_gain_hbm, norm_bias_hbm, proj_in_hbm, proj_in_bias_hbm,
     proj_out_hbm, proj_out_bias_hbm, tokens_hbm, residue_hbm, pair_gain_hbm, pair_bias_hbm,
     qk_hbm, qk_bias_hbm, chain_hbm,
-    single_hbm, query_key_ref, copies_ref,
+    single_hbm, query_ref, copies_ref,
     hidden, mix, norm_gain, norm_bias, proj_in, proj_in_bias, proj_out, proj_out_bias, tokens,
     residue, pair_gain, pair_bias, qk, qk_bias, chain, mixture, residue_rows, single,
     sem_hidden, sem_in, sem_out, sem_small, sem_single,
@@ -121,18 +121,17 @@
 
     pair_in = row_norm(single_f, pair_gain[...], pair_bias[...]).astype(BF16)
     query_key = jnp.dot(pair_in, qk[...], preferred_element_type=F32) + qk_bias[...]
-    query_key_ref[...] = query_key.astype(BF16)
 
     shape = (tok_count, 2 * inner_dim)
     lanes = lax.broadcasted_iota(jnp.int32, shape, 1)
+    flag = lax.rem(lanes, inner_dim // 2).astype(F32)
     square = (tok_count, tok_count)
     own = lax.broadcasted_iota(jnp.int32, square, 0) == lax.broadcasted_iota(jnp.int32, square, 1)
-    chain_col = jnp.sum(
-        jnp.where(own, chain[...].astype(F32), 0.0), axis=1, keepdims=True
-    )
-    keys = pltpu.roll(query_key, inner_dim, 1)
-    block = jnp.where(lanes < inner_dim, keys, jnp.where(lanes == inner_dim, chain_col, 0.0))
-    block = block.astype(BF16)
+    chain_col = jnp.sum(jnp.where(own, chain[...].astype(F32), 0.0), axis=1, keepdims=True)
+    flags = jnp.where(flag == chain_col, 1.0, 0.0)
+    front = lanes < inner_dim
+    query_ref[...] = jnp.where(front, query_key, flags).astype(BF16)
+    block = jnp.where(front, pltpu.roll(query_key, inner_dim, 1), flags).astype(BF16)
     for peer in range(copies_ref.shape[0]):
         copies_ref[peer] = block
     out_copy.wait()
@@ -191,54 +190,69 @@
     )(*args)
 
 
-def pair_kernel(
-    blocks, query_key, chain, bins, pair_weight, relpos, chain_table,
-    pair_hbm, right, table, pair, sem,
-):
+def first_kernel(queries, bins, pair_weight, relpos, chain_table, first, right, minus, table):
     tok_count, col_count = bins.shape
-    bin_count, lanes_count = relpos.shape
+    bin_count = relpos.shape[0]
     inner_dim = pair_weight.shape[0] // 2
-    half = 2 * inner_dim
+    flag_count = inner_dim // 2
 
     step = chain_table[1:2, :] - chain_table[0:1, :]
     step_high = step.astype(BF16).astype(F32)
+    shape = (flag_count, step.shape[1])
+    right[0:inner_dim, :] = pair_weight[0:inner_dim, :]
+    right[inner_dim:inner_dim + flag_count, :] = jnp.broadcast_to(step_high, shape).astype(BF16)
+    right[inner_dim + flag_count:, :] = jnp.broadcast_to(step - step_high, shape).astype(BF16)
+    minus[0:inner_dim, :] = pair_weight[inner_dim:, :]
+    minus[inner_dim:, :] = jnp.zeros((inner_dim, step.shape[1]), BF16)
+
+    row_base = jnp.dot(queries[...], minus[...], preferred_element_type=F32) + chain_table[0:1, :]
     table[...] = jnp.zeros(table.shape, F32)
     table[0:bin_count, :] = relpos[...]
-    table[bin_count:bin_count + 1, :] = step_high
-    table[bin_count + 1:bin_count + 2, :] = step - step_high
-    right[0:inner_dim, :] = pair_weight[0:inner_dim, :]
-    right[inner_dim:half, :] = -pair_weight[inner_dim:half, :]
-    right[half:, :] = table[...].astype(BF16)
-
-    lanes = lax.broadcasted_iota(jnp.int32, (tok_count, half), 1)
-    queries = query_key[...]
-    row_base = jnp.dot(
-        queries[:, 0:inner_dim], pair_weight[inner_dim:half, :], preferred_element_type=F32
-    ) + chain_table[0:1, :]
-    queries = jnp.where(lanes < inner_dim, queries.astype(F32), 1.0).astype(BF16)
-
-    lanes = lax.broadcasted_iota(jnp.int32, (col_count, half), 1)
-    keys = blocks[...].astype(F32)
-    col_chain = keys[:, inner_dim:inner_dim + 1].astype(jnp.int32)
-    keys = jnp.where(lanes < inner_dim, keys, pltpu.roll(keys, inner_dim, 1)).astype(BF16)
-
-    lanes = lax.broadcasted_iota(jnp.int32, (col_count, table.shape[0]), 1)
-    chain_lanes = (lanes >= bin_count) & (lanes < bin_count + 2)
-    col_chain = jnp.where(chain_lanes, col_chain, -1)
-
+    bin_rows = table[...].astype(BF16)
     padded = jnp.concatenate(
         [bins[...], jnp.zeros((128 - tok_count, col_count), jnp.int32)], axis=0
     )
     bins_col = padded.T
+    lanes = lax.broadcasted_iota(jnp.int32, (col_count, table.shape[0]), 1)
+    for row in range(tok_count):
+        onehot = jnp.where(bins_col[:, row:row + 1] == lanes, 1.0, 0.0).astype(BF16)
+        value = jnp.dot(onehot, bin_rows, preferred_element_type=F32)
+        first[row] = value + row_base[row:row + 1, :]
+
+
+def first_part(queries, bins, pair_weight, relpos, chain_table):
+    tok_count, col_count = bins.shape
+    channels = pair_weight.shape[1]
+    table_rows = -(-relpos.shape[0] // 128) * 128
+    vmem = pl.BlockSpec(memory_space=pltpu.VMEM)
+    return pl.pallas_call(
+        first_kernel,
+        out_shape=(
+            jax.ShapeDtypeStruct((tok_count, col_count, channels), F32),
+            jax.ShapeDtypeStruct(pair_weight.shape, BF16),
+            jax.ShapeDtypeStruct(pair_weight.shape, BF16),
+        ),
+        in_specs=[vmem] * 5,
+        out_specs=(vmem, vmem, vmem),
+        scratch_shapes=[pltpu.VMEM((table_rows, channels), F32)],
+        compiler_params=pltpu.CompilerParams(vmem_limit_bytes=32 * 2**20),
+        cost_estimate=pl.CostEstimate(
+            flops=2 * tok_count * col_count * channels * table_rows,
+            bytes_accessed=4 * tok_count * col_count * channels,
+            transcendentals=0,
+        ),
+        name="rows_first",
+    )(queries, bins, pair_weight, relpos, chain_table)
+
+
+def pair_kernel(blocks, queries, first, right, minus, pair_hbm, pair, sem):
+    keys = blocks[...]
+    col_diff = jnp.dot(keys, minus[...], preferred_element_type=F32)
     copies = []
-    for row in range(tok_count):
+    for row in range(first.shape[0]):
         products = keys * queries[row:row + 1, :]
-        hit = (bins_col[:, row:row + 1] == lanes) | (col_chain == chain[row])
-        onehot = jnp.where(hit, 1.0, 0.0).astype(BF16)
-        value = jnp.dot(
-            jnp.concatenate([products, onehot], axis=1), right[...], preferred_element_type=F32
-        )
-        pair[row] = (value + row_base[row:row + 1, :]).astype(BF16)
+        value = jnp.dot(products, right[...], preferred_element_type=F32)
+        pair[row] = (value + first[row] - col_diff).astype(BF16)
         copy = pltpu.make_async_copy(pair.at[row], pair_hbm.at[row], sem.at[row])
         copy.start()
         copies.append(copy)
@@ -246,31 +260,26 @@
         copy.wait()
 
 
-def pair_part(blocks, query_key, chain, bins, pair_weight, relpos, chain_table):
-    tok_count, col_count = bins.shape
-    channels = pair_weight.shape[1]
-    half = pair_weight.shape[0]
-    table_rows = -(-(relpos.shape[0] + 2) // 128) * 128
+def pair_part(blocks, queries, first, right, minus):
+    tok_count = first.shape[0]
     vmem = pl.BlockSpec(memory_space=pltpu.VMEM)
     return pl.pallas_call(
         pair_kernel,
-        out_shape=jax.ShapeDtypeStruct((tok_count, col_count, channels), BF16),
-        in_specs=[vmem, vmem, pl.BlockSpec(memory_space=pltpu.SMEM), vmem, vmem, vmem, vmem],
+        out_shape=jax.ShapeDtypeStruct(first.shape, BF16),
+        in_specs=[vmem] * 5,
         out_specs=pl.BlockSpec(memory_space=pltpu.HBM),
         scratch_shapes=[
-            pltpu.VMEM((half + table_rows, channels), BF16),
-            pltpu.VMEM((table_rows, channels), F32),
-            pltpu.VMEM((tok_count, col_count, channels), BF16),
+            pltpu.VMEM(first.shape, BF16),
             pltpu.SemaphoreType.DMA((tok_count,)),
         ],
         compiler_params=pltpu.CompilerParams(vmem_limit_bytes=32 * 2**20),
         cost_estimate=pl.CostEstimate(
-            flops=2 * tok_count * col_count * channels * (half + table_rows),
-            bytes_accessed=2 * tok_count * col_count * channels,
+            flops=2 * first.size * right.shape[0],
+            bytes_accessed=6 * first.size,
             transcendentals=0,
         ),
         name="pair_rows",
-    )(blocks, query_key, chain, bins, pair_weight, relpos, chain_table)
+    )(blocks, queries, first, right, minus)
 
 
 def shards(
@@ -295,7 +304,7 @@
     chain_table,
 ):
     device_count = lax.axis_size("seq")
-    single, query_key, copies = single_part(
+    single, queries, copies = single_part(
         device_count,
         (
             hidden_states, layer_mix, norm_gain, norm_bias, proj_in, proj_in_bias, proj_out,
@@ -305,9 +314,10 @@
     )
     blocks = lax.all_to_all(copies, "seq", split_axis=0, concat_axis=0)
     blocks = blocks.reshape(-1, blocks.shape[-1])
-    pair = pair_part(
-        blocks, query_key, chain_ids, relpos_bins, pair_weight, relpos_table, chain_table
-    )
+    first, right, minus = first_part(
+        queries, relpos_bins, pair_weight, relpos_table, chain_table
+    )
+    pair = pair_part(blocks, queries, first, right, minus)
     return (single, pair)
 
 

time: 22.9 us -> 22.7 us (level)
  blocking collectives: 14.1 us -> 0 us
  starting transfers between devices: 0 us -> 7.4 us
  waiting for transfers between devices: 0 us -> 5.99 us
  Pallas kernels: 7.89 us -> 8.39 us
    all_to_all x1 -> x0, blocking collectives: 14.1 us -> none  [shards(): blocks = lax.all_to_all(copies, 'seq', split_axis=0, concat_axis=0)]
    all_to_all x0 -> x1, starting transfers between devices: none -> 7.4 us  [shards(): blocks = lax.all_to_all(copies, 'seq', split_axis=0, concat_axis=0)]
    all_to_all x0 -> x1, waiting for transfers between devices: none -> 5.99 us  [shards(): blocks = lax.all_to_all(copies, 'seq', split_axis=0, concat_axis=0)]
    pallas_call x1, Pallas kernels: 5.61 us -> 6.23 us  [single_part(): pl.pallas_call(functools.partial(single_kernel, plan), out_shape=(jax.Sha...]
    pallas_call x1 -> x2, Pallas kernels: 2.28 us -> 2.16 us  [the longest x1 1.3 us: pair_part(): pl.pallas_call(pair_kernel, out_shape=jax.ShapeDtypeStruct(first.shape, B...]
  transfers between devices with their start and end apart: 0 -> 1, of which waited for: 0 -> 1; matrix products, arithmetic and copies ran while one was open for 0% -> 0% of each run, Pallas kernels for 0% -> 4%
where the time goes in v8:
time: 22.7 us; the launch traced here: 22.5 us
  Pallas kernels  8.39 us (37%)
  starting transfers between devices  7.4 us (33%)
  waiting for transfers between devices  5.99 us (26%)
  between operations  0.72 us (3%)
    all_to_all x1, starting transfers between devices, shards(): blocks = lax.all_to_all(copies, 'seq', split_axis=0, concat_axis=0)  7.4 us
    pallas_call x1, Pallas kernels, single_part(): pl.pallas_call(functools.partial(single_kernel, plan), out_shape=(jax.Sha...  6.23 us
    all_to_all x1, waiting for transfers between devices, shards(): blocks = lax.all_to_all(copies, 'seq', split_axis=0, concat_axis=0)  5.99 us
    pallas_call x1, Pallas kernels, pair_part(): pl.pallas_call(pair_kernel, out_shape=jax.ShapeDtypeStruct(first.shape, B...  1.3 us
    pallas_call x1, Pallas kernels, first_part(): pl.pallas_call(first_kernel, out_shape=(jax.ShapeDtypeStruct((tok_count,...  0.86 us
  transfers between devices with their start and end apart: 1, of which 1 were waited for; matrix products, arithmetic and copies ran while one was open for 0% of the time, Pallas kernels for 4%

profile of v8, /device:TPU:0, one launch (start us, length us, event | category | flops | bytes accessed | tf_op | source)
XLA Modules:
  0.0 22.5 jit_solution(7714606602257168461)
XLA Ops:
  0.6 0.0 copy-start
  0.6 0.0 copy-start.1
  0.7 0.0 copy-start.2
  0.7 0.0 copy-start.3
  0.7 6.2 %single_path.1 = (bf16[16,1024]{1,0:T(8,128)(2,1)}, bf16[16,128]{1,0:T(8,128)(2,1)S(1)}, bf16[16,16,128]{2,1,0:T(8,128)(2,1)}) custom-call(bf16[37,16,2560]{2,1,0:T(8,128)(2,1)} %hidden_hbm.1, f32[37]{0:T(128)} %mix_hbm.1, f32[2560]{0:T(1024)} %norm_gain_hbm.1, f32[2560]{0:T(1024)} %norm_bias_hbm.1, bf16[2560,1024]{1,0:T(8,128)(2,1)} %proj_in_hbm.1, ...), custom_call_target="tpu_custom_call" | custom-call | flops 121634816 | bytes 10765076 | tf_op jit(solution)/shard_map/single_path/pallas_call | solution.py:169
  6.9 7.4 %all-to-all-start = ((bf16[16,16,128]{2,1,0:T(8,128)(2,1)}), bf16[16,16,128]{2,1,0:T(8,128)(2,1)S(1)}, u32[]{:S(2)}, u32[]{:S(2)}) async-start(bf16[16,16,128]{2,1,0:T(8,128)(2,1)} %get-tuple-element.9), calls=%async_computation | async-start | bytes 131072 | tf_op jit(solution)/shard_map/all_to_all | solution.py:315
  14.3 0.0 copy-done
  14.3 0.0 copy-done.1
  14.3 0.0 copy-done.2
  14.3 0.0 copy-done.3
  14.4 0.9 %rows_first.1 = (f32[16,256,128]{2,1,0:T(8,128)S(1)}, bf16[128,128]{1,0:T(8,128)(2,1)S(1)}, bf16[128,128]{1,0:T(8,128)(2,1)S(1)}) custom-call(bf16[16,128]{1,0:T(8,128)(2,1)S(1)} %get-tuple-element.10.queries, s32[16,256]{1,0:T(8,128)S(1)} %copy-done.2, bf16[128,128]{1,0:T(8,128)(2,1)S(1)} %copy-done.1, f32[66,128]{1,0:T(8,128)S(1)} %copy-done, ...), custom_call_target="tpu_custom_call" | custom-call | flops 134217728 | bytes 2097152 | tf_op jit(solution)/shard_map/rows_first/pallas_call | solution.py:228
  15.2 6.0 %all-to-all-done = bf16[16,16,128]{2,1,0:T(8,128)(2,1)S(1)} async-done(((bf16[16,16,128]{2,1,0:T(8,128)(2,1)}), bf16[16,16,128]{2,1,0:T(8,128)(2,1)S(1)}, u32[]{:S(2)}, u32[]{:S(2)}) %all-to-all-start) | async-done | bytes 65568 | tf_op jit(solution)/shard_map/all_to_all | solution.py:315
  21.2 1.3 %pair_rows.1 = bf16[16,256,128]{2,1,0:T(8,128)(2,1)} custom-call(bf16[256,128]{1,0:T(8,128)(2,1)S(1)} %bitcast.7, bf16[16,128]{1,0:T(8,128)(2,1)S(1)} %get-tuple-element.10.queries, f32[16,256,128]{2,1,0:T(8,128)S(1)} %get-tuple-element.11.first, bf16[128,128]{1,0:T(8,128)(2,1)S(1)} %get-tuple-element.12.right, bf16[128,128]{1,0:T(8,128)(2,1)S(1)} %get-tuple-element.13.minus), custom_call_target="tpu_custom_call" | custom-call | flops 134217728 | bytes 3145728 | tf_op jit(solution)/shard_map/pair_rows/pallas_call | solution.py:266
Async XLA Ops:
  0.6 13.7 %copy-start = (f32[66,128]{1,0:T(8,128)S(1)}, f32[66,128]{1,0:T(8,128)}, u32[]{:S(2)}) copy-start(f32[66,128]{1,0:T(8,128)} %relpos.1) | copy-start | bytes 101380
  0.6 13.7 %copy-start.1 = (bf16[128,128]{1,0:T(8,128)(2,1)S(1)}, bf16[128,128]{1,0:T(8,128)(2,1)}, u32[]{:S(2)}) copy-start(bf16[128,128]{1,0:T(8,128)(2,1)} %pair_weight.1) | copy-start | bytes 98308
  0.7 13.7 %copy-start.2 = (s32[16,256]{1,0:T(8,128)S(1)}, s32[16,256]{1,0:T(8,128)}, u32[]{:S(2)}) copy-start(s32[16,256]{1,0:T(8,128)} %bins.1) | copy-start | bytes 49156
  0.7 13.7 %copy-start.3 = (f32[2,128]{1,0:T(2,128)S(1)}, f32[2,128]{1,0:T(2,128)}, u32[]{:S(2)}) copy-start(f32[2,128]{1,0:T(2,128)} %chain_table.1) | copy-start | bytes 3076
  6.9 14.3 %all-to-all-start = ((bf16[16,16,128]{2,1,0:T(8,128)(2,1)}), bf16[16,16,128]{2,1,0:T(8,128)(2,1)S(1)}, u32[]{:S(2)}, u32[]{:S(2)}) async-start(bf16[16,16,128]{2,1,0:T(8,128)(2,1)} %get-tuple-element.9), calls=%async_computation | async-start | bytes 131072 | tf_op jit(solution)/shard_map/all_to_all | solution.py:315

commit v9 on v8

v9 whole, which is shorter than its diff:
```python
import functools

import jax
import jax.numpy as jnp
from jax import lax
from jax.experimental import pallas as pl
from jax.experimental.pallas import tpu as pltpu
from jax.sharding import PartitionSpec as P

epsilon = 1e-05
BF16 = jnp.bfloat16
F32 = jnp.float32


def pieces(total, count):
    count = max(1, min(count, total))
    ends = [total * step // count for step in range(count + 1)]
    return [(low, high - low) for low, high in zip(ends[:-1], ends[1:])]


def row_norm(values, gain, bias):
    center = values - jnp.mean(values, axis=-1, keepdims=True)
    spread = jnp.mean(center * center, axis=-1, keepdims=True)
    return center * lax.rsqrt(spread + epsilon) * gain + bias


def chain_flags(chain, tok_count, inner_dim):
    lanes = lax.broadcasted_iota(jnp.int32, (tok_count, 2 * inner_dim), 1)
    flag = lax.rem(lanes, inner_dim // 2).astype(F32)
    square = (tok_count, tok_count)
    own = lax.broadcasted_iota(jnp.int32, square, 0) == lax.broadcasted_iota(jnp.int32, square, 1)
    chain_col = jnp.sum(jnp.where(own, chain[...].astype(F32), 0.0), axis=1, keepdims=True)
    return jnp.where(flag == chain_col, 1.0, 0.0)


def operand_rows(bins, pair_weight, relpos, chain_table, bin_rows, right, minus, tok_count):
    bin_count = relpos.shape[0]
    inner_dim = pair_weight.shape[0] // 2
    flag_count = inner_dim // 2
    step = chain_table[1:2, :] - chain_table[0:1, :]
    step_high = step.astype(BF16).astype(F32)
    shape = (flag_count, step.shape[1])
    right[0:inner_dim, :] = pair_weight[0:inner_dim, :]
    right[inner_dim:inner_dim + flag_count, :] = jnp.broadcast_to(step_high, shape).astype(BF16)
    right[inner_dim + flag_count:, :] = jnp.broadcast_to(step - step_high, shape).astype(BF16)
    minus[0:inner_dim, :] = pair_weight[inner_dim:, :]
    minus[inner_dim:, :] = jnp.zeros((inner_dim, step.shape[1]), BF16)
    bin_rows[...] = jnp.zeros(bin_rows.shape, F32)
    bin_rows[0:bin_count, :] = relpos[...] + chain_table[0:1, :]
    padded = jnp.concatenate(
        [bins[...], jnp.zeros((128 - tok_count, bins.shape[1]), jnp.int32)], axis=0
    )
    return padded.T


def single_kernel(
    plan,
    hidden_hbm, mix_hbm, norm_gain_hbm, norm_bias_hbm, proj_in_hbm, proj_in_bias_hbm,
    proj_out_hbm, proj_out_bias_hbm, tokens_hbm, residue_hbm, pair_gain_hbm, pair_bias_hbm,
    qk_hbm, qk_bias_hbm, chain_hbm, bins_hbm, pair_weight_hbm, relpos_hbm, chain_table_hbm,
    single, query_ref, copies_ref, first, right, minus,
    hidden, mix, norm_gain, norm_bias, proj_in, proj_in_bias, proj_out, proj_out_bias, tokens,
    residue, pair_gain, pair_bias, qk, qk_bias, chain, bins, pair_weight, relpos, chain_table,
    mixture, residue_rows, bin_rows, sem_hidden, sem_in, sem_out, sem_small,
):
    state_pieces, in_pieces, out_pieces, lane_step = plan
    tok_count = mixture.shape[0]
    inner_dim = qk.shape[1] // 2

    small = [
        (mix_hbm, mix), (tokens_hbm, tokens), (residue_hbm, residue),
        (norm_gain_hbm, norm_gain), (norm_bias_hbm, norm_bias),
        (proj_in_bias_hbm, proj_in_bias), (proj_out_bias_hbm, proj_out_bias),
        (pair_gain_hbm, pair_gain), (pair_bias_hbm, pair_bias),
        (qk_hbm, qk), (qk_bias_hbm, qk_bias), (chain_hbm, chain), (bins_hbm, bins),
        (pair_weight_hbm, pair_weight), (relpos_hbm, relpos), (chain_table_hbm, chain_table),
    ]
    small = [
        pltpu.make_async_copy(source, target, sem_small.at[at])
        for at, (source, target) in enumerate(small)
    ]
    states = [
        pltpu.make_async_copy(
            hidden_hbm.at[pl.ds(low, size)], hidden.at[pl.ds(low, size)], sem_hidden.at[at]
        )
        for at, (low, size) in enumerate(state_pieces)
    ]
    firsts = [
        pltpu.make_async_copy(
            proj_in_hbm.at[pl.ds(low, size)], proj_in.at[pl.ds(low, size)], sem_in.at[at]
        )
        for at, (low, size) in enumerate(in_pieces)
    ]
    seconds = [
        pltpu.make_async_copy(
            proj_out_hbm.at[pl.ds(low, size)], proj_out.at[pl.ds(low, size)], sem_out.at[at]
        )
        for at, (low, size) in enumerate(out_pieces)
    ]
    small[0].start()
    for copy in states:
        copy.start()
    firsts[0].start()
    for copy in small[1:]:
        copy.start()
    later = firsts[1:] + seconds

    small[0].wait()
    width = mixture.shape[1]
    for at, (low, size) in enumerate(state_pieces):
        states[at].wait()
        last = at == len(state_pieces) - 1
        for copy in later if last else later[:1]:
            copy.start()
        later = later[1:]
        for lane in range(0, width, lane_step):
            span = slice(lane, min(lane + lane_step, width))
            total = mixture[:, span] if at else None
            for state in range(low, low + size):
                term = mix[state] * hidden[state, :, span].astype(F32)
                total = term if total is None else total + term
            mixture[:, span] = total

    for copy in small[1:]:
        copy.wait()
    normed = row_norm(
        mixture[...], norm_gain[...].reshape(1, width), norm_bias[...].reshape(1, width)
    ).astype(BF16)
    bins_col = operand_rows(
        bins, pair_weight, relpos, chain_table, bin_rows, right, minus, tok_count
    )
    flags = chain_flags(chain, tok_count, inner_dim)
    bin_table = bin_rows[...].astype(BF16)
    lanes = lax.broadcasted_iota(jnp.int32, (bins_col.shape[0], bin_table.shape[0]), 1)
    row_pieces = pieces(tok_count, max(1, len(in_pieces) - 1))
    total = None
    for at, (low, size) in enumerate(in_pieces):
        firsts[at].wait()
        term = jnp.dot(
            normed[:, low:low + size], proj_in[pl.ds(low, size), :], preferred_element_type=F32
        )
        total = term if total is None else total + term
        if at < len(row_pieces):
            for row in range(row_pieces[at][0], sum(row_pieces[at])):
                onehot = jnp.where(bins_col[:, row:row + 1] == lanes, 1.0, 0.0).astype(BF16)
                first[row] = jnp.dot(onehot, bin_table, preferred_element_type=F32)
    for row in range(tok_count):
        residue_rows[pl.ds(row, 1), :] = residue[pl.ds(tokens[row], 1), :]
    middle = jnp.maximum(total + proj_in_bias[...], 0.0).astype(BF16)

    total = None
    for at, (low, size) in enumerate(out_pieces):
        seconds[at].wait()
        term = jnp.dot(
            middle[:, low:low + size], proj_out[pl.ds(low, size), :], preferred_element_type=F32
        )
        total = term if total is None else total + term
    single_f = total + proj_out_bias[...] + residue_rows[...]
    single[...] = single_f.astype(BF16)

    pair_in = row_norm(single_f, pair_gain[...], pair_bias[...]).astype(BF16)
    query_key = jnp.dot(pair_in, qk[...], preferred_element_type=F32) + qk_bias[...]

    front = lax.broadcasted_iota(jnp.int32, flags.shape, 1) < inner_dim
    query_ref[...] = jnp.where(front, query_key, flags).astype(BF16)
    block = jnp.where(front, pltpu.roll(query_key, inner_dim, 1), flags).astype(BF16)
    for peer in range(copies_ref.shape[0]):
        copies_ref[peer] = block


def single_part(device_count, operands):
    (hidden, mix, norm_gain, norm_bias, proj_in, proj_in_bias, proj_out, proj_out_bias, tokens,
     residue, pair_gain, pair_bias, qk, qk_bias, chain, bins, pair_weight, relpos,
     chain_table) = operands
    state_count, tok_count, width = hidden.shape
    channels = proj_out.shape[1]
    lanes = qk.shape[1]
    table_rows = -(-relpos.shape[0] // 128) * 128
    vmem = pl.BlockSpec(memory_space=pltpu.VMEM)
    plan = (pieces(state_count, 6), pieces(width, 5), pieces(channels, 2), 512)
    args = (
        hidden, mix, norm_gain, norm_bias, proj_in, proj_in_bias[None],
        proj_out, proj_out_bias[None], tokens, residue, pair_gain[None], pair_bias[None],
        qk, qk_bias[None], chain[None], bins, pair_weight, relpos, chain_table,
    )
    args = [pltpu.with_memory_space_constraint(arg, pltpu.HBM) for arg in args]
    in_smem = (1, 8)
    scratch = [
        (pltpu.SMEM if at in in_smem else pltpu.VMEM)(arg.shape, arg.dtype)
        for at, arg in enumerate(args)
    ]
    scratch += [
        pltpu.VMEM((tok_count, width), F32),
        pltpu.VMEM((tok_count, channels), F32),
        pltpu.VMEM((table_rows, pair_weight.shape[1]), F32),
        pltpu.SemaphoreType.DMA((len(plan[0]),)),
        pltpu.SemaphoreType.DMA((len(plan[1]),)),
        pltpu.SemaphoreType.DMA((len(plan[2]),)),
        pltpu.SemaphoreType.DMA((16,)),
    ]
    moved = sum(arg.size * arg.dtype.itemsize for arg in args)
    return pl.pallas_call(
        functools.partial(single_kernel, plan),
        out_shape=(
            jax.ShapeDtypeStruct((tok_count, channels), BF16),
            jax.ShapeDtypeStruct((tok_count, lanes), BF16),
            jax.ShapeDtypeStruct((device_count, tok_count, lanes), BF16),
            jax.ShapeDtypeStruct(bins.shape + pair_weight.shape[1:], F32),
            jax.ShapeDtypeStruct(pair_weight.shape, BF16),
            jax.ShapeDtypeStruct(pair_weight.shape, BF16),
        ),
        in_specs=[pl.BlockSpec(memory_space=pltpu.HBM)] * len(args),
        out_specs=(vmem,) * 6,
        scratch_shapes=scratch,
        compiler_params=pltpu.CompilerParams(vmem_limit_bytes=32 * 2**20),
        cost_estimate=pl.CostEstimate(
            flops=2 * tok_count * channels * (width + channels + lanes),
            bytes_accessed=moved,
            transcendentals=0,
        ),
        name="single_path",
    )(*args)


def pair_kernel(
    blocks, queries, first, right, minus, single, single_hbm, pair_hbm, pair, sem, sem_single
):
    single_copy = pltpu.make_async_copy(single, single_hbm, sem_single)
    single_copy.start()
    keys = blocks[...]
    row_diff = jnp.dot(queries[...], minus[...], preferred_element_type=F32)
    col_diff = jnp.dot(keys, minus[...], preferred_element_type=F32)
    copies = []
    for row in range(first.shape[0]):
        products = keys * queries[row:row + 1, :]
        value = jnp.dot(products, right[...], preferred_element_type=F32)
        value = value + first[row] + (row_diff[row:row + 1, :] - col_diff)
        pair[row] = value.astype(BF16)
        copy = pltpu.make_async_copy(pair.at[row], pair_hbm.at[row], sem.at[row])
        copy.start()
        copies.append(copy)
    for copy in copies:
        copy.wait()
    single_copy.wait()


def pair_part(blocks, queries, first, right, minus, single):
    tok_count = first.shape[0]
    vmem = pl.BlockSpec(memory_space=pltpu.VMEM)
    return pl.pallas_call(
        pair_kernel,
        out_shape=(
            jax.ShapeDtypeStruct(single.shape, BF16),
            jax.ShapeDtypeStruct(first.shape, BF16),
        ),
        in_specs=[vmem] * 6,
        out_specs=(pl.BlockSpec(memory_space=pltpu.HBM),) * 2,
        scratch_shapes=[
            pltpu.VMEM(first.shape, BF16),
            pltpu.SemaphoreType.DMA((tok_count,)),
            pltpu.SemaphoreType.DMA,
        ],
        compiler_params=pltpu.CompilerParams(vmem_limit_bytes=32 * 2**20),
        cost_estimate=pl.CostEstimate(
            flops=2 * first.size * right.shape[0],
            bytes_accessed=6 * first.size,
            transcendentals=0,
        ),
        name="pair_rows",
    )(blocks, queries, first, right, minus, single)


def shards(
    hidden_states,
    layer_mix,
    norm_gain,
    norm_bias,
    proj_in,
    proj_in_bias,
    proj_out,
    proj_out_bias,
    residue_tokens,
    residue_table,
    pair_norm_gain,
    pair_norm_bias,
    qk_weight,
    qk_bias,
    pair_weight,
    relpos_bins,
    relpos_table,
    chain_ids,
    chain_table,
):
    device_count = lax.axis_size("seq")
    single, queries, copies, first, right, minus = single_part(
        device_count,
        (
            hidden_states, layer_mix, norm_gain, norm_bias, proj_in, proj_in_bias, proj_out,
            proj_out_bias, residue_tokens, residue_table, pair_norm_gain, pair_norm_bias,
            qk_weight, qk_bias, chain_ids, relpos_bins, pair_weight, relpos_table, chain_table,
        ),
    )
    blocks = lax.all_to_all(copies, "seq", split_axis=0, concat_axis=0)
    blocks = blocks.reshape(-1, blocks.shape[-1])
    return pair_part(blocks, queries, first, right, minus, single)


def solution(mesh):
    in_specs = (
        P(None, ("groups", "seq"), None),
        P(),
        P(),
        P(),
        P(),
        P(),
        P(),
        P(),
        P(("groups", "seq")),
        P(),
        P(),
        P(),
        P(),
        P(),
        P(),
        P(("groups", "seq"), None),
        P(),
        P(("groups", "seq")),
        P(),
    )
    out_specs = (P(("groups", "seq"), None), P(("groups", "seq"), None, None))
    return jax.shard_map(shards, mesh=mesh, in_specs=in_specs, out_specs=out_specs, check_vma=False)
```

time: 22.7 us -> 21.8 us (0.960)
  blocking collectives: 0 us -> 14.1 us
  starting transfers between devices: 7.4 us -> 0 us
  waiting for transfers between devices: 5.99 us -> 0 us
  Pallas kernels: 8.39 us -> 6.89 us
    all_to_all x0 -> x1, blocking collectives: none -> 14.1 us  [shards(): blocks = lax.all_to_all(copies, 'seq', split_axis=0, concat_axis=0)]
    all_to_all x1 -> x0, starting transfers between devices: 7.4 us -> none  [shards(): blocks = lax.all_to_all(copies, 'seq', split_axis=0, concat_axis=0)]
    all_to_all x1 -> x0, waiting for transfers between devices: 5.99 us -> none  [shards(): blocks = lax.all_to_all(copies, 'seq', split_axis=0, concat_axis=0)]
    pallas_call x2 -> x1, Pallas kernels: 2.16 us -> 1.35 us  [pair_part(): pl.pallas_call(pair_kernel, out_shape=(jax.ShapeDtypeStruct(single.shape,...]
    pallas_call x1, Pallas kernels: 6.23 us -> 5.54 us  [single_part(): pl.pallas_call(functools.partial(single_kernel, plan), out_shape=(jax.Sha...]
  transfers between devices with their start and end apart: 1 -> 0, of which waited for: 1 -> 0; matrix products, arithmetic and copies ran while one was open for 0% -> 0% of each run, Pallas kernels for 4% -> 0%
where the time goes in v9:
time: 21.8 us; the launch traced here: 21.6 us
  blocking collectives  14.1 us (65%)
  Pallas kernels  6.89 us (32%)
  between operations  0.65 us (3%)
    all_to_all x1, blocking collectives, shards(): blocks = lax.all_to_all(copies, 'seq', split_axis=0, concat_axis=0)  14.1 us
    pallas_call x1, Pallas kernels, single_part(): pl.pallas_call(functools.partial(single_kernel, plan), out_shape=(jax.Sha...  5.54 us
    pallas_call x1, Pallas kernels, pair_part(): pl.pallas_call(pair_kernel, out_shape=(jax.ShapeDtypeStruct(single.shape,...  1.35 us

profile of v9, /device:TPU:0, one launch (start us, length us, event | category | flops | bytes accessed | tf_op | source)
XLA Modules:
  0.0 21.6 jit_solution(867493193788973831)
XLA Ops:
  0.6 5.5 %single_path.1 = (bf16[16,1024]{1,0:T(8,128)(2,1)S(1)}, bf16[16,128]{1,0:T(8,128)(2,1)S(1)}, bf16[16,16,128]{2,1,0:T(8,128)(2,1)S(1)}, f32[16,256,128]{2,1,0:T(8...) custom-call(bf16[37,16,2560]{2,1,0:T(8,128)(2,1)} %hidden_hbm.1, f32[37]{0:T(128)} %mix_hbm.1, ...), custom_call_target="tpu_custom_call" | custom-call | flops 121634816 | bytes 10849044 | tf_op jit(solution)/shard_map/single_path/pallas_call | solution.py:202
  6.2 14.1 %all_to_all.5 = bf16[16,16,128]{2,1,0:T(8,128)(2,1)S(1)} all-to-all(bf16[16,16,128]{2,1,0:T(8,128)(2,1)S(1)} %get-tuple-element.8), channel_id=1, replica_groups=mesh['groups'=2,'seq'=16] {'seq'}, dimensions={0} | all-to-all | bytes 131072 | tf_op jit(solution)/shard_map/all_to_all | solution.py:303
  20.3 1.3 %pair_rows.1 = (bf16[16,1024]{1,0:T(8,128)(2,1)}, bf16[16,256,128]{2,1,0:T(8,128)(2,1)}) custom-call(bf16[256,128]{1,0:T(8,128)(2,1)S(1)} %bitcast.7, bf16[16,128]{1,0:T(8,128)(2,1)S(1)} %get-tuple-element.9.queries, f32[16,256,128]{2,1,0:T(8,128)S(1)} %get-tuple-element.10.first, bf16[128,128]{1,0:T(8,128)(2,1)S(1)} %get-tuple-element.11.right, ...), custom_call_target="tpu_custom_call" | custom-call | flops 134217728 | bytes 3145728 | tf_op jit(solution)/shard_map/pair_rows/pallas_call | solution.py:250

commit v10 on v9

--- a/solution.py
+++ b/solution.py
@@ -227,7 +227,8 @@
 ):
     single_copy = pltpu.make_async_copy(single, single_hbm, sem_single)
     single_copy.start()
-    keys = blocks[...]
+    device_count = blocks.shape[0]
+    keys = jnp.concatenate([blocks[device_count - 1 - at] for at in range(device_count)], axis=0)
     row_diff = jnp.dot(queries[...], minus[...], preferred_element_type=F32)
     col_diff = jnp.dot(keys, minus[...], preferred_element_type=F32)
     copies = []
@@ -300,8 +301,10 @@
             qk_weight, qk_bias, chain_ids, relpos_bins, pair_weight, relpos_table, chain_table,
         ),
     )
-    blocks = lax.all_to_all(copies, "seq", split_axis=0, concat_axis=0)
-    blocks = blocks.reshape(-1, blocks.shape[-1])
+    falling = list(reversed(range(device_count)))
+    blocks = lax.all_to_all(
+        copies, "seq", split_axis=0, concat_axis=0, axis_index_groups=[falling]
+    )
     return pair_part(blocks, queries, first, right, minus, single)
 
 

time: 21.8 us -> 18.5 us (0.85)
  blocking collectives: 14.1 us -> 10.8 us
    all_to_all x1, blocking collectives: 14.1 us -> 10.8 us  [shards(): lax.all_to_all(copies, 'seq', split_axis=0, concat_axis=0, axis_index_gro...]
where the time goes in v10:
time: 18.5 us; the launch traced here: 18.3 us
  blocking collectives  10.8 us (58%)
  Pallas kernels  6.89 us (37%)
  between operations  0.65 us (4%)
    all_to_all x1, blocking collectives, shards(): lax.all_to_all(copies, 'seq', split_axis=0, concat_axis=0, axis_index_gro...  10.8 us
    pallas_call x1, Pallas kernels, single_part(): pl.pallas_call(functools.partial(single_kernel, plan), out_shape=(jax.Sha...  5.54 us
    pallas_call x1, Pallas kernels, pair_part(): pl.pallas_call(pair_kernel, out_shape=(jax.ShapeDtypeStruct(single.shape,...  1.35 us

profile of v10, /device:TPU:0, one launch (start us, length us, event | category | flops | bytes accessed | tf_op | source)
XLA Modules:
  0.0 18.3 jit_solution(8090812951937419187)
XLA Ops:
  0.6 5.5 %single_path.1 = (bf16[16,1024]{1,0:T(8,128)(2,1)S(1)}, bf16[16,128]{1,0:T(8,128)(2,1)S(1)}, bf16[16,16,128]{2,1,0:T(8,128)(2,1)S(1)}, f32[16,256,128]{2,1,0:T(8...) custom-call(bf16[37,16,2560]{2,1,0:T(8,128)(2,1)} %hidden_hbm.1, f32[37]{0:T(128)} %mix_hbm.1, ...), custom_call_target="tpu_custom_call" | custom-call | flops 121634816 | bytes 10849044 | tf_op jit(solution)/shard_map/single_path/pallas_call | solution.py:202
  6.2 10.8 %all_to_all.5.blocks = bf16[16,16,128]{2,1,0:T(8,128)(2,1)S(1)} all-to-all(bf16[16,16,128]{2,1,0:T(8,128)(2,1)S(1)} %get-tuple-element.8), channel_id=1, replica_groups={{15,14,13,12,11,10,9,8,7,6,5,4,3,2,1,0},{31,30,29,28,27,26,25,24,23,22,..., dimensions={0} | all-to-all | bytes 131072 | tf_op jit(solution)/shard_map/all_to_all | solution.py:305
  17.0 1.4 %pair_rows.1 = (bf16[16,1024]{1,0:T(8,128)(2,1)}, bf16[16,256,128]{2,1,0:T(8,128)(2,1)}) custom-call(bf16[16,16,128]{2,1,0:T(8,128)(2,1)S(1)} %all_to_all.5.blocks, bf16[16,128]{1,0:T(8,128)(2,1)S(1)} %get-tuple-element.9.queries, f32[16,256,128]{2,1,0:T(8,128)S(1)} %get-tuple-element.10.first, bf16[128,128]{1,0:T(8,128)(2,1)S(1)} %get-tuple-element.11.right, ...), custom_call_target="tpu_custom_call" | custom-call | flops 134217728 | bytes 3145728 | tf_op jit(solution)/shard_map/pair_rows/pallas_call | solution.py:251

commit v11 on v10

--- a/solution.py
+++ b/solution.py
@@ -227,8 +227,7 @@
 ):
     single_copy = pltpu.make_async_copy(single, single_hbm, sem_single)
     single_copy.start()
-    device_count = blocks.shape[0]
-    keys = jnp.concatenate([blocks[device_count - 1 - at] for at in range(device_count)], axis=0)
+    keys = jnp.concatenate([blocks[1:].reshape(-1, blocks.shape[2]), blocks[0]], axis=0)
     row_diff = jnp.dot(queries[...], minus[...], preferred_element_type=F32)
     col_diff = jnp.dot(keys, minus[...], preferred_element_type=F32)
     copies = []
@@ -301,9 +300,9 @@
             qk_weight, qk_bias, chain_ids, relpos_bins, pair_weight, relpos_table, chain_table,
         ),
     )
-    falling = list(reversed(range(device_count)))
+    order = [device_count - 1] + list(range(device_count - 1))
     blocks = lax.all_to_all(
-        copies, "seq", split_axis=0, concat_axis=0, axis_index_groups=[falling]
+        copies, "seq", split_axis=0, concat_axis=0, axis_index_groups=[order]
     )
     return pair_part(blocks, queries, first, right, minus, single)
 

time: 18.5 us -> 18.4 us (level)
  no operation moved by 1% of the time
where the time goes in v11:
time: 18.4 us; the launch traced here: 18.2 us
  blocking collectives  10.7 us (58%)
  Pallas kernels  6.89 us (37%)
  between operations  0.65 us (4%)
    all_to_all x1, blocking collectives, shards(): lax.all_to_all(copies, 'seq', split_axis=0, concat_axis=0, axis_index_gro...  10.7 us
    pallas_call x1, Pallas kernels, single_part(): pl.pallas_call(functools.partial(single_kernel, plan), out_shape=(jax.Sha...  5.54 us
    pallas_call x1, Pallas kernels, pair_part(): pl.pallas_call(pair_kernel, out_shape=(jax.ShapeDtypeStruct(single.shape,...  1.35 us

profile of v11, /device:TPU:0, one launch (start us, length us, event | category | flops | bytes accessed | tf_op | source)
XLA Modules:
  0.0 18.2 jit_solution(9822328155621255278)
XLA Ops:
  0.6 5.5 %single_path.1 = (bf16[16,1024]{1,0:T(8,128)(2,1)S(1)}, bf16[16,128]{1,0:T(8,128)(2,1)S(1)}, bf16[16,16,128]{2,1,0:T(8,128)(2,1)S(1)}, f32[16,256,128]{2,1,0:T(8...) custom-call(bf16[37,16,2560]{2,1,0:T(8,128)(2,1)} %hidden_hbm.1, f32[37]{0:T(128)} %mix_hbm.1, ...), custom_call_target="tpu_custom_call" | custom-call | flops 121634816 | bytes 10849044 | tf_op jit(solution)/shard_map/single_path/pallas_call | solution.py:202
  6.2 10.7 %all_to_all.5.blocks = bf16[16,16,128]{2,1,0:T(8,128)(2,1)S(1)} all-to-all(bf16[16,16,128]{2,1,0:T(8,128)(2,1)S(1)} %get-tuple-element.8), channel_id=1, replica_groups={{15,0,1,2,3,4,5,6,7,8,9,10,11,12,13,14},{31,16,17,18,19,20,21,22,23,24,..., dimensions={0} | all-to-all | bytes 131072 | tf_op jit(solution)/shard_map/all_to_all | solution.py:304
  16.9 1.4 %pair_rows.1 = (bf16[16,1024]{1,0:T(8,128)(2,1)}, bf16[16,256,128]{2,1,0:T(8,128)(2,1)}) custom-call(bf16[16,16,128]{2,1,0:T(8,128)(2,1)S(1)} %all_to_all.5.blocks, bf16[16,128]{1,0:T(8,128)(2,1)S(1)} %get-tuple-element.9.queries, f32[16,256,128]{2,1,0:T(8,128)S(1)} %get-tuple-element.10.first, bf16[128,128]{1,0:T(8,128)(2,1)S(1)} %get-tuple-element.11.right, ...), custom_call_target="tpu_custom_call" | custom-call | flops 134217728 | bytes 3145728 | tf_op jit(solution)/shard_map/pair_rows/pallas_call | solution.py:250

commit v12 on v11

--- a/solution.py
+++ b/solution.py
@@ -68,13 +68,14 @@
     inner_dim = qk.shape[1] // 2
 
     small = [
-        (mix_hbm, mix), (tokens_hbm, tokens), (residue_hbm, residue),
-        (norm_gain_hbm, norm_gain), (norm_bias_hbm, norm_bias),
+        (mix_hbm, mix), (bins_hbm, bins), (relpos_hbm, relpos), (chain_table_hbm, chain_table),
+        (pair_weight_hbm, pair_weight), (chain_hbm, chain), (norm_gain_hbm, norm_gain),
+        (norm_bias_hbm, norm_bias), (tokens_hbm, tokens), (residue_hbm, residue),
         (proj_in_bias_hbm, proj_in_bias), (proj_out_bias_hbm, proj_out_bias),
         (pair_gain_hbm, pair_gain), (pair_bias_hbm, pair_bias),
-        (qk_hbm, qk), (qk_bias_hbm, qk_bias), (chain_hbm, chain), (bins_hbm, bins),
-        (pair_weight_hbm, pair_weight), (relpos_hbm, relpos), (chain_table_hbm, chain_table),
-    ]
+        (qk_hbm, qk), (qk_bias_hbm, qk_bias),
+    ]
+    first_small = 6
     small = [
         pltpu.make_async_copy(source, target, sem_small.at[at])
         for at, (source, target) in enumerate(small)
@@ -98,21 +99,27 @@
         for at, (low, size) in enumerate(out_pieces)
     ]
     small[0].start()
-    for copy in states:
+    states[0].start()
+    for copy in small[1:first_small] + states[1:] + firsts[:2] + small[first_small:]:
         copy.start()
-    firsts[0].start()
-    for copy in small[1:]:
-        copy.start()
-    later = firsts[1:] + seconds
+    later = firsts[2:] + seconds
+    per_piece = -(-len(later) // len(states))
+
+    width = mixture.shape[1]
+    row_pieces = pieces(tok_count, len(states) + len(in_pieces) - 2)
+
+    def bins_rows(at):
+        if at < len(row_pieces):
+            for row in range(row_pieces[at][0], sum(row_pieces[at])):
+                onehot = jnp.where(bins_col[:, row:row + 1] == lanes, 1.0, 0.0).astype(BF16)
+                first[row] = jnp.dot(onehot, bin_table, preferred_element_type=F32)
 
     small[0].wait()
-    width = mixture.shape[1]
     for at, (low, size) in enumerate(state_pieces):
         states[at].wait()
-        last = at == len(state_pieces) - 1
-        for copy in later if last else later[:1]:
+        for copy in later[:per_piece]:
             copy.start()
-        later = later[1:]
+        later = later[per_piece:]
         for lane in range(0, width, lane_step):
             span = slice(lane, min(lane + lane_step, width))
             total = mixture[:, span] if at else None
@@ -120,19 +127,23 @@
                 term = mix[state] * hidden[state, :, span].astype(F32)
                 total = term if total is None else total + term
             mixture[:, span] = total
-
-    for copy in small[1:]:
+        if at == 0:
+            for copy in small[1:first_small]:
+                copy.wait()
+            bins_col = operand_rows(
+                bins, pair_weight, relpos, chain_table, bin_rows, right, minus, tok_count
+            )
+            flags = chain_flags(chain, tok_count, inner_dim)
+            bin_table = bin_rows[...].astype(BF16)
+            lanes = lax.broadcasted_iota(jnp.int32, (bins_col.shape[0], bin_table.shape[0]), 1)
+        if at < len(states) - 1:
+            bins_rows(at)
+
+    for copy in small[first_small:]:
         copy.wait()
     normed = row_norm(
         mixture[...], norm_gain[...].reshape(1, width), norm_bias[...].reshape(1, width)
     ).astype(BF16)
-    bins_col = operand_rows(
-        bins, pair_weight, relpos, chain_table, bin_rows, right, minus, tok_count
-    )
-    flags = chain_flags(chain, tok_count, inner_dim)
-    bin_table = bin_rows[...].astype(BF16)
-    lanes = lax.broadcasted_iota(jnp.int32, (bins_col.shape[0], bin_table.shape[0]), 1)
-    row_pieces = pieces(tok_count, max(1, len(in_pieces) - 1))
     total = None
     for at, (low, size) in enumerate(in_pieces):
         firsts[at].wait()
@@ -140,10 +151,7 @@
             normed[:, low:low + size], proj_in[pl.ds(low, size), :], preferred_element_type=F32
         )
         total = term if total is None else total + term
-        if at < len(row_pieces):
-            for row in range(row_pieces[at][0], sum(row_pieces[at])):
-                onehot = jnp.where(bins_col[:, row:row + 1] == lanes, 1.0, 0.0).astype(BF16)
-                first[row] = jnp.dot(onehot, bin_table, preferred_element_type=F32)
+        bins_rows(len(states) - 1 + at)
     for row in range(tok_count):
         residue_rows[pl.ds(row, 1), :] = residue[pl.ds(tokens[row], 1), :]
     middle = jnp.maximum(total + proj_in_bias[...], 0.0).astype(BF16)
@@ -177,7 +185,7 @@
     lanes = qk.shape[1]
     table_rows = -(-relpos.shape[0] // 128) * 128
     vmem = pl.BlockSpec(memory_space=pltpu.VMEM)
-    plan = (pieces(state_count, 6), pieces(width, 5), pieces(channels, 2), 512)
+    plan = (pieces(state_count, 6), pieces(width, 10), pieces(channels, 4), 512)
     args = (
         hidden, mix, norm_gain, norm_bias, proj_in, proj_in_bias[None],
         proj_out, proj_out_bias[None], tokens, residue, pair_gain[None], pair_bias[None],

time: 18.4 us -> 19.3 us (1.049)
  Pallas kernels: 6.89 us -> 7.75 us
    pallas_call x1, Pallas kernels: 5.54 us -> 6.4 us  [single_part(): pl.pallas_call(functools.partial(single_kernel, plan), out_shape=(jax.Sha...]
where the time goes in v12:
time: 19.3 us; the launch traced here: 19.1 us
  blocking collectives  10.7 us (55%)
  Pallas kernels  7.75 us (40%)
  between operations  0.65 us (3%)
    all_to_all x1, blocking collectives, shards(): lax.all_to_all(copies, 'seq', split_axis=0, concat_axis=0, axis_index_gro...  10.7 us
    pallas_call x1, Pallas kernels, single_part(): pl.pallas_call(functools.partial(single_kernel, plan), out_shape=(jax.Sha...  6.4 us
    pallas_call x1, Pallas kernels, pair_part(): pl.pallas_call(pair_kernel, out_shape=(jax.ShapeDtypeStruct(single.shape,...  1.35 us

profile of v12, /device:TPU:0, one launch (start us, length us, event | category | flops | bytes accessed | tf_op | source)
XLA Modules:
  0.0 19.1 jit_solution(9771364318010632113)
XLA Ops:
  0.6 6.4 %single_path.1 = (bf16[16,1024]{1,0:T(8,128)(2,1)S(1)}, bf16[16,128]{1,0:T(8,128)(2,1)S(1)}, bf16[16,16,128]{2,1,0:T(8,128)(2,1)S(1)}, f32[16,256,128]{2,1,0:T(8...) custom-call(bf16[37,16,2560]{2,1,0:T(8,128)(2,1)} %hidden_hbm.1, f32[37]{0:T(128)} %mix_hbm.1, ...), custom_call_target="tpu_custom_call" | custom-call | flops 121634816 | bytes 10849044 | tf_op jit(solution)/shard_map/single_path/pallas_call | solution.py:210
  7.0 10.7 %all_to_all.5.blocks = bf16[16,16,128]{2,1,0:T(8,128)(2,1)S(1)} all-to-all(bf16[16,16,128]{2,1,0:T(8,128)(2,1)S(1)} %get-tuple-element.8), channel_id=1, replica_groups={{15,0,1,2,3,4,5,6,7,8,9,10,11,12,13,14},{31,16,17,18,19,20,21,22,23,24,..., dimensions={0} | all-to-all | bytes 131072 | tf_op jit(solution)/shard_map/all_to_all | solution.py:312
  17.7 1.4 %pair_rows.1 = (bf16[16,1024]{1,0:T(8,128)(2,1)}, bf16[16,256,128]{2,1,0:T(8,128)(2,1)}) custom-call(bf16[16,16,128]{2,1,0:T(8,128)(2,1)S(1)} %all_to_all.5.blocks, bf16[16,128]{1,0:T(8,128)(2,1)S(1)} %get-tuple-element.9.queries, f32[16,256,128]{2,1,0:T(8,128)S(1)} %get-tuple-element.10.first, bf16[128,128]{1,0:T(8,128)(2,1)S(1)} %get-tuple-element.11.right, ...), custom_call_target="tpu_custom_call" | custom-call | flops 134217728 | bytes 3145728 | tf_op jit(solution)/shard_map/pair_rows/pallas_call | solution.py:258

commit v13 on v12

--- a/solution.py
+++ b/solution.py
@@ -98,28 +98,28 @@
         )
         for at, (low, size) in enumerate(out_pieces)
     ]
-    small[0].start()
-    states[0].start()
-    for copy in small[1:first_small] + states[1:] + firsts[:2] + small[first_small:]:
+    for copy in small[:first_small] + states + firsts[:1] + small[first_small:]:
         copy.start()
-    later = firsts[2:] + seconds
-    per_piece = -(-len(later) // len(states))
+    later = firsts[1:] + seconds
+
+    for copy in small[:first_small]:
+        copy.wait()
+    bins_col = operand_rows(
+        bins, pair_weight, relpos, chain_table, bin_rows, right, minus, tok_count
+    )
+    bin_table = bin_rows[...].astype(BF16)
+    lanes = lax.broadcasted_iota(jnp.int32, (bins_col.shape[0], bin_table.shape[0]), 1)
+    for row in range(tok_count):
+        onehot = jnp.where(bins_col[:, row:row + 1] == lanes, 1.0, 0.0).astype(BF16)
+        first[row] = jnp.dot(onehot, bin_table, preferred_element_type=F32)
+    flags = chain_flags(chain, tok_count, inner_dim)
 
     width = mixture.shape[1]
-    row_pieces = pieces(tok_count, len(states) + len(in_pieces) - 2)
-
-    def bins_rows(at):
-        if at < len(row_pieces):
-            for row in range(row_pieces[at][0], sum(row_pieces[at])):
-                onehot = jnp.where(bins_col[:, row:row + 1] == lanes, 1.0, 0.0).astype(BF16)
-                first[row] = jnp.dot(onehot, bin_table, preferred_element_type=F32)
-
-    small[0].wait()
     for at, (low, size) in enumerate(state_pieces):
         states[at].wait()
-        for copy in later[:per_piece]:
+        for copy in later if at else later[:1]:
             copy.start()
-        later = later[per_piece:]
+        later = later[1:]
         for lane in range(0, width, lane_step):
             span = slice(lane, min(lane + lane_step, width))
             total = mixture[:, span] if at else None
@@ -127,17 +127,6 @@
                 term = mix[state] * hidden[state, :, span].astype(F32)
                 total = term if total is None else total + term
             mixture[:, span] = total
-        if at == 0:
-            for copy in small[1:first_small]:
-                copy.wait()
-            bins_col = operand_rows(
-                bins, pair_weight, relpos, chain_table, bin_rows, right, minus, tok_count
-            )
-            flags = chain_flags(chain, tok_count, inner_dim)
-            bin_table = bin_rows[...].astype(BF16)
-            lanes = lax.broadcasted_iota(jnp.int32, (bins_col.shape[0], bin_table.shape[0]), 1)
-        if at < len(states) - 1:
-            bins_rows(at)
 
     for copy in small[first_small:]:
         copy.wait()
@@ -151,7 +140,6 @@
             normed[:, low:low + size], proj_in[pl.ds(low, size), :], preferred_element_type=F32
         )
         total = term if total is None else total + term
-        bins_rows(len(states) - 1 + at)
     for row in range(tok_count):
         residue_rows[pl.ds(row, 1), :] = residue[pl.ds(tokens[row], 1), :]
     middle = jnp.maximum(total + proj_in_bias[...], 0.0).astype(BF16)
@@ -185,7 +173,7 @@
     lanes = qk.shape[1]
     table_rows = -(-relpos.shape[0] // 128) * 128
     vmem = pl.BlockSpec(memory_space=pltpu.VMEM)
-    plan = (pieces(state_count, 6), pieces(width, 10), pieces(channels, 4), 512)
+    plan = (pieces(state_count, 2), pieces(width, 2), pieces(channels, 2), 512)
     args = (
         hidden, mix, norm_gain, norm_bias, proj_in, proj_in_bias[None],
         proj_out, proj_out_bias[None], tokens, residue, pair_gain[None], pair_bias[None],

time: 19.3 us -> 18.6 us (0.964)
  Pallas kernels: 7.75 us -> 7.11 us
    pallas_call x1, Pallas kernels: 6.4 us -> 5.75 us  [single_part(): pl.pallas_call(functools.partial(single_kernel, plan), out_shape=(jax.Sha...]
where the time goes in v13:
time: 18.6 us; the launch traced here: 18.4 us
  blocking collectives  10.7 us (58%)
  Pallas kernels  7.11 us (38%)
  between operations  0.65 us (3%)
    all_to_all x1, blocking collectives, shards(): lax.all_to_all(copies, 'seq', split_axis=0, concat_axis=0, axis_index_gro...  10.7 us
    pallas_call x1, Pallas kernels, single_part(): pl.pallas_call(functools.partial(single_kernel, plan), out_shape=(jax.Sha...  5.75 us
    pallas_call x1, Pallas kernels, pair_part(): pl.pallas_call(pair_kernel, out_shape=(jax.ShapeDtypeStruct(single.shape,...  1.35 us

profile of v13, /device:TPU:0, one launch (start us, length us, event | category | flops | bytes accessed | tf_op | source)
XLA Modules:
  0.0 18.4 jit_solution(10575714768001226679)
XLA Ops:
  0.6 5.8 %single_path.1 = (bf16[16,1024]{1,0:T(8,128)(2,1)S(1)}, bf16[16,128]{1,0:T(8,128)(2,1)S(1)}, bf16[16,16,128]{2,1,0:T(8,128)(2,1)S(1)}, f32[16,256,128]{2,1,0:T(8...) custom-call(bf16[37,16,2560]{2,1,0:T(8,128)(2,1)} %hidden_hbm.1, f32[37]{0:T(128)} %mix_hbm.1, ...), custom_call_target="tpu_custom_call" | custom-call | flops 121634816 | bytes 10849044 | tf_op jit(solution)/shard_map/single_path/pallas_call | solution.py:198
  6.4 10.7 %all_to_all.5.blocks = bf16[16,16,128]{2,1,0:T(8,128)(2,1)S(1)} all-to-all(bf16[16,16,128]{2,1,0:T(8,128)(2,1)S(1)} %get-tuple-element.8), channel_id=1, replica_groups={{15,0,1,2,3,4,5,6,7,8,9,10,11,12,13,14},{31,16,17,18,19,20,21,22,23,24,..., dimensions={0} | all-to-all | bytes 131072 | tf_op jit(solution)/shard_map/all_to_all | solution.py:300
  17.1 1.4 %pair_rows.1 = (bf16[16,1024]{1,0:T(8,128)(2,1)}, bf16[16,256,128]{2,1,0:T(8,128)(2,1)}) custom-call(bf16[16,16,128]{2,1,0:T(8,128)(2,1)S(1)} %all_to_all.5.blocks, bf16[16,128]{1,0:T(8,128)(2,1)S(1)} %get-tuple-element.9.queries, f32[16,256,128]{2,1,0:T(8,128)S(1)} %get-tuple-element.10.first, bf16[128,128]{1,0:T(8,128)(2,1)S(1)} %get-tuple-element.11.right, ...), custom_call_target="tpu_custom_call" | custom-call | flops 134217728 | bytes 3145728 | tf_op jit(solution)/shard_map/pair_rows/pallas_call | solution.py:246

commit v14 on v11

--- a/solution.py
+++ b/solution.py
@@ -63,7 +63,7 @@
     residue, pair_gain, pair_bias, qk, qk_bias, chain, bins, pair_weight, relpos, chain_table,
     mixture, residue_rows, bin_rows, sem_hidden, sem_in, sem_out, sem_small,
 ):
-    state_pieces, in_pieces, out_pieces, lane_step = plan
+    state_pieces, in_pieces, out_pieces = plan
     tok_count = mixture.shape[0]
     inner_dim = qk.shape[1] // 2
 
@@ -107,19 +107,36 @@
 
     small[0].wait()
     width = mixture.shape[1]
+    state_count = hidden.shape[0]
+    shape = (tok_count, state_count * tok_count)
+    lanes = lax.broadcasted_iota(jnp.int32, shape, 1)
+    state_of = lanes // tok_count
+    weights = jnp.zeros(shape, F32)
+    for state in range(state_count):
+        weights = jnp.where(state_of == state, mix[state], weights)
+    own = lanes - state_of * tok_count == lax.broadcasted_iota(jnp.int32, shape, 0)
+    weights = jnp.where(own, weights, 0.0)
+    high = weights.astype(BF16)
+    middle = (weights - high.astype(F32)).astype(BF16)
+    low_part = (weights - high.astype(F32) - middle.astype(F32)).astype(BF16)
+    weights = jnp.concatenate([high, middle, low_part], axis=0)
+
+    mixed = None
     for at, (low, size) in enumerate(state_pieces):
         states[at].wait()
         last = at == len(state_pieces) - 1
-        for copy in later if last else later[:1]:
+        for copy in later if last else later[:2]:
             copy.start()
-        later = later[1:]
-        for lane in range(0, width, lane_step):
-            span = slice(lane, min(lane + lane_step, width))
-            total = mixture[:, span] if at else None
-            for state in range(low, low + size):
-                term = mix[state] * hidden[state, :, span].astype(F32)
-                total = term if total is None else total + term
-            mixture[:, span] = total
+        later = later[2:]
+        term = jnp.dot(
+            weights[:, low * tok_count:(low + size) * tok_count],
+            hidden[pl.ds(low, size)].reshape(size * tok_count, width),
+            preferred_element_type=F32,
+        )
+        mixed = term if mixed is None else mixed + term
+    mixture[...] = (
+        mixed[0:tok_count] + (mixed[tok_count:2 * tok_count] + mixed[2 * tok_count:])
+    )
 
     for copy in small[1:]:
         copy.wait()
@@ -177,7 +194,11 @@
     lanes = qk.shape[1]
     table_rows = -(-relpos.shape[0] // 128) * 128
     vmem = pl.BlockSpec(memory_space=pltpu.VMEM)
-    plan = (pieces(state_count, 6), pieces(width, 5), pieces(channels, 2), 512)
+    states_step = max(1, 256 // tok_count)
+    state_pieces = [
+        (low, min(states_step, state_count - low)) for low in range(0, state_count, states_step)
+    ]
+    plan = (state_pieces, pieces(width, 5), pieces(channels, 2))
     args = (
         hidden, mix, norm_gain, norm_bias, proj_in, proj_in_bias[None],
         proj_out, proj_out_bias[None], tokens, residue, pair_gain[None], pair_bias[None],

time: 18.4 us -> 18.7 us (1.016)
  Pallas kernels: 6.89 us -> 7.22 us
    pallas_call x1, Pallas kernels: 5.54 us -> 5.87 us  [single_part(): pl.pallas_call(functools.partial(single_kernel, plan), out_shape=(jax.Sha...]
where the time goes in v14:
time: 18.7 us; the launch traced here: 18.5 us
  blocking collectives  10.7 us (57%)
  Pallas kernels  7.22 us (39%)
  between operations  0.65 us (3%)
    all_to_all x1, blocking collectives, shards(): lax.all_to_all(copies, 'seq', split_axis=0, concat_axis=0, axis_index_gro...  10.7 us
    pallas_call x1, Pallas kernels, single_part(): pl.pallas_call(functools.partial(single_kernel, plan), out_shape=(jax.Sha...  5.87 us
    pallas_call x1, Pallas kernels, pair_part(): pl.pallas_call(pair_kernel, out_shape=(jax.ShapeDtypeStruct(single.shape,...  1.35 us

profile of v14, /device:TPU:0, one launch (start us, length us, event | category | flops | bytes accessed | tf_op | source)
XLA Modules:
  0.0 18.5 jit_solution(16924731034894418594)
XLA Ops:
  0.6 5.9 %single_path.1 = (bf16[16,1024]{1,0:T(8,128)(2,1)S(1)}, bf16[16,128]{1,0:T(8,128)(2,1)S(1)}, bf16[16,16,128]{2,1,0:T(8,128)(2,1)S(1)}, f32[16,256,128]{2,1,0:T(8...) custom-call(bf16[37,16,2560]{2,1,0:T(8,128)(2,1)} %hidden_hbm.1, f32[37]{0:T(128)} %mix_hbm.1, ...), custom_call_target="tpu_custom_call" | custom-call | flops 121634816 | bytes 10849044 | tf_op jit(solution)/shard_map/single_path/pallas_call | solution.py:223
  6.5 10.7 %all_to_all.5.blocks = bf16[16,16,128]{2,1,0:T(8,128)(2,1)S(1)} all-to-all(bf16[16,16,128]{2,1,0:T(8,128)(2,1)S(1)} %get-tuple-element.8), channel_id=1, replica_groups={{15,0,1,2,3,4,5,6,7,8,9,10,11,12,13,14},{31,16,17,18,19,20,21,22,23,24,..., dimensions={0} | all-to-all | bytes 131072 | tf_op jit(solution)/shard_map/all_to_all | solution.py:325
  17.2 1.4 %pair_rows.1 = (bf16[16,1024]{1,0:T(8,128)(2,1)}, bf16[16,256,128]{2,1,0:T(8,128)(2,1)}) custom-call(bf16[16,16,128]{2,1,0:T(8,128)(2,1)S(1)} %all_to_all.5.blocks, bf16[16,128]{1,0:T(8,128)(2,1)S(1)} %get-tuple-element.9.queries, f32[16,256,128]{2,1,0:T(8,128)S(1)} %get-tuple-element.10.first, bf16[128,128]{1,0:T(8,128)(2,1)S(1)} %get-tuple-element.11.right, ...), custom_call_target="tpu_custom_call" | custom-call | flops 134217728 | bytes 3145728 | tf_op jit(solution)/shard_map/pair_rows/pallas_call | solution.py:271

commit v15 on v11

--- a/solution.py
+++ b/solution.py
@@ -63,7 +63,7 @@
     residue, pair_gain, pair_bias, qk, qk_bias, chain, bins, pair_weight, relpos, chain_table,
     mixture, residue_rows, bin_rows, sem_hidden, sem_in, sem_out, sem_small,
 ):
-    state_pieces, in_pieces, out_pieces, lane_step = plan
+    in_pieces, out_pieces = plan
     tok_count = mixture.shape[0]
     inner_dim = qk.shape[1] // 2
 
@@ -81,9 +81,11 @@
     ]
     states = [
         pltpu.make_async_copy(
-            hidden_hbm.at[pl.ds(low, size)], hidden.at[pl.ds(low, size)], sem_hidden.at[at]
+            hidden_hbm.at[:, :, pl.ds(low, size)],
+            hidden.at[:, :, pl.ds(low, size)],
+            sem_hidden.at[at],
         )
-        for at, (low, size) in enumerate(state_pieces)
+        for at, (low, size) in enumerate(in_pieces)
     ]
     firsts = [
         pltpu.make_async_copy(
@@ -98,54 +100,60 @@
         for at, (low, size) in enumerate(out_pieces)
     ]
     small[0].start()
-    for copy in states:
-        copy.start()
-    firsts[0].start()
-    for copy in small[1:]:
+    states[0].start()
+    for copy in small[1:] + states[1:] + firsts[:1]:
         copy.start()
     later = firsts[1:] + seconds
 
+    width = mixture.shape[1]
     small[0].wait()
-    width = mixture.shape[1]
-    for at, (low, size) in enumerate(state_pieces):
+    shift = sums = squares = None
+    for at, (low, size) in enumerate(in_pieces):
         states[at].wait()
-        last = at == len(state_pieces) - 1
-        for copy in later if last else later[:1]:
+        for copy in later if at == len(in_pieces) - 1 else later[:1]:
             copy.start()
         later = later[1:]
-        for lane in range(0, width, lane_step):
-            span = slice(lane, min(lane + lane_step, width))
-            total = mixture[:, span] if at else None
-            for state in range(low, low + size):
-                term = mix[state] * hidden[state, :, span].astype(F32)
-                total = term if total is None else total + term
-            mixture[:, span] = total
-
-    for copy in small[1:]:
-        copy.wait()
-    normed = row_norm(
-        mixture[...], norm_gain[...].reshape(1, width), norm_bias[...].reshape(1, width)
-    ).astype(BF16)
-    bins_col = operand_rows(
-        bins, pair_weight, relpos, chain_table, bin_rows, right, minus, tok_count
-    )
-    flags = chain_flags(chain, tok_count, inner_dim)
+        total = None
+        for state in range(hidden.shape[0]):
+            term = mix[state] * hidden[state, :, low:low + size].astype(F32)
+            total = term if total is None else total + term
+        mixture[:, low:low + size] = total
+        if shift is None:
+            shift = jnp.mean(total, axis=1, keepdims=True)
+        total = total - shift
+        for lane in range(0, size, 128):
+            part = total[:, lane:lane + 128]
+            sums = part if sums is None else sums + part
+            squares = part * part if squares is None else squares + part * part
+        if at == min(1, len(in_pieces) - 1):
+            for copy in small[1:]:
+                copy.wait()
+            bins_col = operand_rows(
+                bins, pair_weight, relpos, chain_table, bin_rows, right, minus, tok_count
+            )
+            flags = chain_flags(chain, tok_count, inner_dim)
+            for row in range(tok_count):
+                residue_rows[pl.ds(row, 1), :] = residue[pl.ds(tokens[row], 1), :]
+
+    offset = jnp.sum(sums, axis=1, keepdims=True) / width
+    spread = jnp.sum(squares, axis=1, keepdims=True) / width - offset * offset
+    mean = shift + offset
+    scale = lax.rsqrt(jnp.maximum(spread, 0.0) + epsilon)
+    gain, bias = norm_gain[...].reshape(1, width), norm_bias[...].reshape(1, width)
     bin_table = bin_rows[...].astype(BF16)
     lanes = lax.broadcasted_iota(jnp.int32, (bins_col.shape[0], bin_table.shape[0]), 1)
     row_pieces = pieces(tok_count, max(1, len(in_pieces) - 1))
     total = None
     for at, (low, size) in enumerate(in_pieces):
+        span = slice(low, low + size)
+        normed = ((mixture[:, span] - mean) * scale * gain[:, span] + bias[:, span]).astype(BF16)
         firsts[at].wait()
-        term = jnp.dot(
-            normed[:, low:low + size], proj_in[pl.ds(low, size), :], preferred_element_type=F32
-        )
+        term = jnp.dot(normed, proj_in[pl.ds(low, size), :], preferred_element_type=F32)
         total = term if total is None else total + term
         if at < len(row_pieces):
             for row in range(row_pieces[at][0], sum(row_pieces[at])):
                 onehot = jnp.where(bins_col[:, row:row + 1] == lanes, 1.0, 0.0).astype(BF16)
                 first[row] = jnp.dot(onehot, bin_table, preferred_element_type=F32)
-    for row in range(tok_count):
-        residue_rows[pl.ds(row, 1), :] = residue[pl.ds(tokens[row], 1), :]
     middle = jnp.maximum(total + proj_in_bias[...], 0.0).astype(BF16)
 
     total = None
@@ -172,12 +180,12 @@
     (hidden, mix, norm_gain, norm_bias, proj_in, proj_in_bias, proj_out, proj_out_bias, tokens,
      residue, pair_gain, pair_bias, qk, qk_bias, chain, bins, pair_weight, relpos,
      chain_table) = operands
-    state_count, tok_count, width = hidden.shape
+    tok_count, width = hidden.shape[1:]
     channels = proj_out.shape[1]
     lanes = qk.shape[1]
     table_rows = -(-relpos.shape[0] // 128) * 128
     vmem = pl.BlockSpec(memory_space=pltpu.VMEM)
-    plan = (pieces(state_count, 6), pieces(width, 5), pieces(channels, 2), 512)
+    plan = (pieces(width, 5), pieces(channels, 2))
     args = (
         hidden, mix, norm_gain, norm_bias, proj_in, proj_in_bias[None],
         proj_out, proj_out_bias[None], tokens, residue, pair_gain[None], pair_bias[None],
@@ -194,8 +202,8 @@
         pltpu.VMEM((tok_count, channels), F32),
         pltpu.VMEM((table_rows, pair_weight.shape[1]), F32),
         pltpu.SemaphoreType.DMA((len(plan[0]),)),
+        pltpu.SemaphoreType.DMA((len(plan[0]),)),
         pltpu.SemaphoreType.DMA((len(plan[1]),)),
-        pltpu.SemaphoreType.DMA((len(plan[2]),)),
         pltpu.SemaphoreType.DMA((16,)),
     ]
     moved = sum(arg.size * arg.dtype.itemsize for arg in args)

time: 18.4 us -> 18.4 us (level)
  no operation moved by 1% of the time
where the time goes in v15:
time: 18.4 us; the launch traced here: 18.2 us
  blocking collectives  10.7 us (58%)
  Pallas kernels  6.9 us (38%)
  between operations  0.65 us (4%)
    all_to_all x1, blocking collectives, shards(): lax.all_to_all(copies, 'seq', split_axis=0, concat_axis=0, axis_index_gro...  10.7 us
    pallas_call x1, Pallas kernels, single_part(): pl.pallas_call(functools.partial(single_kernel, plan), out_shape=(jax.Sha...  5.55 us
    pallas_call x1, Pallas kernels, pair_part(): pl.pallas_call(pair_kernel, out_shape=(jax.ShapeDtypeStruct(single.shape,...  1.35 us

profile of v15, /device:TPU:0, one launch (start us, length us, event | category | flops | bytes accessed | tf_op | source)
XLA Modules:
  0.0 18.2 jit_solution(1492857532741383961)
XLA Ops:
  0.6 5.6 %single_path.1 = (bf16[16,1024]{1,0:T(8,128)(2,1)S(1)}, bf16[16,128]{1,0:T(8,128)(2,1)S(1)}, bf16[16,16,128]{2,1,0:T(8,128)(2,1)S(1)}, f32[16,256,128]{2,1,0:T(8...) custom-call(bf16[37,16,2560]{2,1,0:T(8,128)(2,1)} %hidden_hbm.1, f32[37]{0:T(128)} %mix_hbm.1, ...), custom_call_target="tpu_custom_call" | custom-call | flops 121634816 | bytes 10849044 | tf_op jit(solution)/shard_map/single_path/pallas_call | solution.py:210
  6.2 10.7 %all_to_all.5.blocks = bf16[16,16,128]{2,1,0:T(8,128)(2,1)S(1)} all-to-all(bf16[16,16,128]{2,1,0:T(8,128)(2,1)S(1)} %get-tuple-element.8), channel_id=1, replica_groups={{15,0,1,2,3,4,5,6,7,8,9,10,11,12,13,14},{31,16,17,18,19,20,21,22,23,24,..., dimensions={0} | all-to-all | bytes 131072 | tf_op jit(solution)/shard_map/all_to_all | solution.py:312
  16.9 1.4 %pair_rows.1 = (bf16[16,1024]{1,0:T(8,128)(2,1)}, bf16[16,256,128]{2,1,0:T(8,128)(2,1)}) custom-call(bf16[16,16,128]{2,1,0:T(8,128)(2,1)S(1)} %all_to_all.5.blocks, bf16[16,128]{1,0:T(8,128)(2,1)S(1)} %get-tuple-element.9.queries, f32[16,256,128]{2,1,0:T(8,128)S(1)} %get-tuple-element.10.first, bf16[128,128]{1,0:T(8,128)(2,1)S(1)} %get-tuple-element.11.right, ...), custom_call_target="tpu_custom_call" | custom-call | flops 134217728 | bytes 3145728 | tf_op jit(solution)/shard_map/pair_rows/pallas_call | solution.py:258

commit v16 on v15

--- a/solution.py
+++ b/solution.py
@@ -101,18 +101,14 @@
     ]
     small[0].start()
     states[0].start()
-    for copy in small[1:] + states[1:] + firsts[:1]:
+    for copy in small[1:] + states[1:] + firsts + seconds:
         copy.start()
-    later = firsts[1:] + seconds
 
     width = mixture.shape[1]
     small[0].wait()
     shift = sums = squares = None
     for at, (low, size) in enumerate(in_pieces):
         states[at].wait()
-        for copy in later if at == len(in_pieces) - 1 else later[:1]:
-            copy.start()
-        later = later[1:]
         total = None
         for state in range(hidden.shape[0]):
             term = mix[state] * hidden[state, :, low:low + size].astype(F32)

time: 18.4 us -> 19.7 us (1.071)
  Pallas kernels: 6.9 us -> 8.16 us
    pallas_call x1, Pallas kernels: 5.55 us -> 6.81 us  [single_part(): pl.pallas_call(functools.partial(single_kernel, plan), out_shape=(jax.Sha...]
where the time goes in v16:
time: 19.7 us; the launch traced here: 19.5 us
  blocking collectives  10.7 us (54%)
  Pallas kernels  8.16 us (41%)
  between operations  0.65 us (3%)
    all_to_all x1, blocking collectives, shards(): lax.all_to_all(copies, 'seq', split_axis=0, concat_axis=0, axis_index_gro...  10.7 us
    pallas_call x1, Pallas kernels, single_part(): pl.pallas_call(functools.partial(single_kernel, plan), out_shape=(jax.Sha...  6.81 us
    pallas_call x1, Pallas kernels, pair_part(): pl.pallas_call(pair_kernel, out_shape=(jax.ShapeDtypeStruct(single.shape,...  1.35 us

profile of v16, /device:TPU:0, one launch (start us, length us, event | category | flops | bytes accessed | tf_op | source)
XLA Modules:
  0.0 19.5 jit_solution(16980244058797933870)
XLA Ops:
  0.6 6.8 %single_path.1 = (bf16[16,1024]{1,0:T(8,128)(2,1)S(1)}, bf16[16,128]{1,0:T(8,128)(2,1)S(1)}, bf16[16,16,128]{2,1,0:T(8,128)(2,1)S(1)}, f32[16,256,128]{2,1,0:T(8...) custom-call(bf16[37,16,2560]{2,1,0:T(8,128)(2,1)} %hidden_hbm.1, f32[37]{0:T(128)} %mix_hbm.1, ...), custom_call_target="tpu_custom_call" | custom-call | flops 121634816 | bytes 10849044 | tf_op jit(solution)/shard_map/single_path/pallas_call | solution.py:206
  7.5 10.7 %all_to_all.5.blocks = bf16[16,16,128]{2,1,0:T(8,128)(2,1)S(1)} all-to-all(bf16[16,16,128]{2,1,0:T(8,128)(2,1)S(1)} %get-tuple-element.8), channel_id=1, replica_groups={{15,0,1,2,3,4,5,6,7,8,9,10,11,12,13,14},{31,16,17,18,19,20,21,22,23,24,..., dimensions={0} | all-to-all | bytes 131072 | tf_op jit(solution)/shard_map/all_to_all | solution.py:308
  18.1 1.4 %pair_rows.1 = (bf16[16,1024]{1,0:T(8,128)(2,1)}, bf16[16,256,128]{2,1,0:T(8,128)(2,1)}) custom-call(bf16[16,16,128]{2,1,0:T(8,128)(2,1)S(1)} %all_to_all.5.blocks, bf16[16,128]{1,0:T(8,128)(2,1)S(1)} %get-tuple-element.9.queries, f32[16,256,128]{2,1,0:T(8,128)S(1)} %get-tuple-element.10.first, bf16[128,128]{1,0:T(8,128)(2,1)S(1)} %get-tuple-element.11.right, ...), custom_call_target="tpu_custom_call" | custom-call | flops 134217728 | bytes 3145728 | tf_op jit(solution)/shard_map/pair_rows/pallas_call | solution.py:254

commit v17 on v16

--- a/solution.py
+++ b/solution.py
@@ -99,9 +99,11 @@
         )
         for at, (low, size) in enumerate(out_pieces)
     ]
-    small[0].start()
-    states[0].start()
-    for copy in small[1:] + states[1:] + firsts + seconds:
+    small[0].start(priority=1)
+    states[0].start(priority=1)
+    for copy in small[1:] + states[1:]:
+        copy.start(priority=1)
+    for copy in firsts + seconds:
         copy.start()
 
     width = mixture.shape[1]

time: 19.7 us -> 20.3 us (1.030)
  Pallas kernels: 8.16 us -> 8.8 us
    pallas_call x1, Pallas kernels: 6.81 us -> 7.45 us  [single_part(): pl.pallas_call(functools.partial(single_kernel, plan), out_shape=(jax.Sha...]
where the time goes in v17:
time: 20.3 us; the launch traced here: 20.1 us
  blocking collectives  10.7 us (53%)
  Pallas kernels  8.8 us (43%)
  between operations  0.65 us (3%)
    all_to_all x1, blocking collectives, shards(): lax.all_to_all(copies, 'seq', split_axis=0, concat_axis=0, axis_index_gro...  10.7 us
    pallas_call x1, Pallas kernels, single_part(): pl.pallas_call(functools.partial(single_kernel, plan), out_shape=(jax.Sha...  7.45 us
    pallas_call x1, Pallas kernels, pair_part(): pl.pallas_call(pair_kernel, out_shape=(jax.ShapeDtypeStruct(single.shape,...  1.35 us

profile of v17, /device:TPU:0, one launch (start us, length us, event | category | flops | bytes accessed | tf_op | source)
XLA Modules:
  0.0 20.1 jit_solution(2947051684474574594)
XLA Ops:
  0.6 7.5 %single_path.1 = (bf16[16,1024]{1,0:T(8,128)(2,1)S(1)}, bf16[16,128]{1,0:T(8,128)(2,1)S(1)}, bf16[16,16,128]{2,1,0:T(8,128)(2,1)S(1)}, f32[16,256,128]{2,1,0:T(8...) custom-call(bf16[37,16,2560]{2,1,0:T(8,128)(2,1)} %hidden_hbm.1, f32[37]{0:T(128)} %mix_hbm.1, ...), custom_call_target="tpu_custom_call" | custom-call | flops 121634816 | bytes 10849044 | tf_op jit(solution)/shard_map/single_path/pallas_call | solution.py:208
  8.1 10.7 %all_to_all.5.blocks = bf16[16,16,128]{2,1,0:T(8,128)(2,1)S(1)} all-to-all(bf16[16,16,128]{2,1,0:T(8,128)(2,1)S(1)} %get-tuple-element.8), channel_id=1, replica_groups={{15,0,1,2,3,4,5,6,7,8,9,10,11,12,13,14},{31,16,17,18,19,20,21,22,23,24,..., dimensions={0} | all-to-all | bytes 131072 | tf_op jit(solution)/shard_map/all_to_all | solution.py:310
  18.8 1.4 %pair_rows.1 = (bf16[16,1024]{1,0:T(8,128)(2,1)}, bf16[16,256,128]{2,1,0:T(8,128)(2,1)}) custom-call(bf16[16,16,128]{2,1,0:T(8,128)(2,1)S(1)} %all_to_all.5.blocks, bf16[16,128]{1,0:T(8,128)(2,1)S(1)} %get-tuple-element.9.queries, f32[16,256,128]{2,1,0:T(8,128)S(1)} %get-tuple-element.10.first, bf16[128,128]{1,0:T(8,128)(2,1)S(1)} %get-tuple-element.11.right, ...), custom_call_target="tpu_custom_call" | custom-call | flops 134217728 | bytes 3145728 | tf_op jit(solution)/shard_map/pair_rows/pallas_call | solution.py:256

commit v18 on v16

--- a/solution.py
+++ b/solution.py
@@ -101,8 +101,10 @@
     ]
     small[0].start()
     states[0].start()
-    for copy in small[1:] + states[1:] + firsts + seconds:
+    for copy in small[1:] + states[1:]:
         copy.start()
+    for copy in firsts + seconds:
+        copy.start(priority=1)
 
     width = mixture.shape[1]
     small[0].wait()

time: 19.7 us -> 18.3 us (0.929)
  Pallas kernels: 8.16 us -> 6.74 us
    pallas_call x1, Pallas kernels: 6.81 us -> 5.39 us  [single_part(): pl.pallas_call(functools.partial(single_kernel, plan), out_shape=(jax.Sha...]
where the time goes in v18:
time: 18.3 us; the launch traced here: 18.1 us
  blocking collectives  10.7 us (58%)
  Pallas kernels  6.74 us (37%)
  between operations  0.65 us (4%)
    all_to_all x1, blocking collectives, shards(): lax.all_to_all(copies, 'seq', split_axis=0, concat_axis=0, axis_index_gro...  10.7 us
    pallas_call x1, Pallas kernels, single_part(): pl.pallas_call(functools.partial(single_kernel, plan), out_shape=(jax.Sha...  5.39 us
    pallas_call x1, Pallas kernels, pair_part(): pl.pallas_call(pair_kernel, out_shape=(jax.ShapeDtypeStruct(single.shape,...  1.35 us

profile of v18, /device:TPU:0, one launch (start us, length us, event | category | flops | bytes accessed | tf_op | source)
XLA Modules:
  0.0 18.1 jit_solution(5197201600175226974)
XLA Ops:
  0.6 5.4 %single_path.1 = (bf16[16,1024]{1,0:T(8,128)(2,1)S(1)}, bf16[16,128]{1,0:T(8,128)(2,1)S(1)}, bf16[16,16,128]{2,1,0:T(8,128)(2,1)S(1)}, f32[16,256,128]{2,1,0:T(8...) custom-call(bf16[37,16,2560]{2,1,0:T(8,128)(2,1)} %hidden_hbm.1, f32[37]{0:T(128)} %mix_hbm.1, ...), custom_call_target="tpu_custom_call" | custom-call | flops 121634816 | bytes 10849044 | tf_op jit(solution)/shard_map/single_path/pallas_call | solution.py:208
  6.0 10.7 %all_to_all.5.blocks = bf16[16,16,128]{2,1,0:T(8,128)(2,1)S(1)} all-to-all(bf16[16,16,128]{2,1,0:T(8,128)(2,1)S(1)} %get-tuple-element.8), channel_id=1, replica_groups={{15,0,1,2,3,4,5,6,7,8,9,10,11,12,13,14},{31,16,17,18,19,20,21,22,23,24,..., dimensions={0} | all-to-all | bytes 131072 | tf_op jit(solution)/shard_map/all_to_all | solution.py:310
  16.7 1.4 %pair_rows.1 = (bf16[16,1024]{1,0:T(8,128)(2,1)}, bf16[16,256,128]{2,1,0:T(8,128)(2,1)}) custom-call(bf16[16,16,128]{2,1,0:T(8,128)(2,1)S(1)} %all_to_all.5.blocks, bf16[16,128]{1,0:T(8,128)(2,1)S(1)} %get-tuple-element.9.queries, f32[16,256,128]{2,1,0:T(8,128)S(1)} %get-tuple-element.10.first, bf16[128,128]{1,0:T(8,128)(2,1)S(1)} %get-tuple-element.11.right, ...), custom_call_target="tpu_custom_call" | custom-call | flops 134217728 | bytes 3145728 | tf_op jit(solution)/shard_map/pair_rows/pallas_call | solution.py:256

commit v19 on v18

--- a/solution.py
+++ b/solution.py
@@ -103,14 +103,20 @@
     states[0].start()
     for copy in small[1:] + states[1:]:
         copy.start()
-    for copy in firsts + seconds:
+    later = firsts + seconds
+    for copy in later[:3]:
         copy.start(priority=1)
+    later = later[3:]
 
     width = mixture.shape[1]
     small[0].wait()
     shift = sums = squares = None
     for at, (low, size) in enumerate(in_pieces):
         states[at].wait()
+        if at % 2 == 0:
+            for copy in later if at >= len(in_pieces) - 2 else later[:1]:
+                copy.start(priority=1)
+            later = later[1:] if at < len(in_pieces) - 2 else []
         total = None
         for state in range(hidden.shape[0]):
             term = mix[state] * hidden[state, :, low:low + size].astype(F32)
@@ -132,6 +138,8 @@
             flags = chain_flags(chain, tok_count, inner_dim)
             for row in range(tok_count):
                 residue_rows[pl.ds(row, 1), :] = residue[pl.ds(tokens[row], 1), :]
+    for copy in later:
+        copy.start(priority=1)
 
     offset = jnp.sum(sums, axis=1, keepdims=True) / width
     spread = jnp.sum(squares, axis=1, keepdims=True) / width - offset * offset

time: 18.3 us -> 18.4 us (level)
  no operation moved by 1% of the time
where the time goes in v19:
time: 18.4 us; the launch traced here: 18.2 us
  blocking collectives  10.7 us (58%)
  Pallas kernels  6.91 us (38%)
  between operations  0.65 us (4%)
    all_to_all x1, blocking collectives, shards(): lax.all_to_all(copies, 'seq', split_axis=0, concat_axis=0, axis_index_gro...  10.7 us
    pallas_call x1, Pallas kernels, single_part(): pl.pallas_call(functools.partial(single_kernel, plan), out_shape=(jax.Sha...  5.56 us
    pallas_call x1, Pallas kernels, pair_part(): pl.pallas_call(pair_kernel, out_shape=(jax.ShapeDtypeStruct(single.shape,...  1.35 us

profile of v19, /device:TPU:0, one launch (start us, length us, event | category | flops | bytes accessed | tf_op | source)
XLA Modules:
  0.0 18.2 jit_solution(6901606809289184681)
XLA Ops:
  0.6 5.6 %single_path.1 = (bf16[16,1024]{1,0:T(8,128)(2,1)S(1)}, bf16[16,128]{1,0:T(8,128)(2,1)S(1)}, bf16[16,16,128]{2,1,0:T(8,128)(2,1)S(1)}, f32[16,256,128]{2,1,0:T(8...) custom-call(bf16[37,16,2560]{2,1,0:T(8,128)(2,1)} %hidden_hbm.1, f32[37]{0:T(128)} %mix_hbm.1, ...), custom_call_target="tpu_custom_call" | custom-call | flops 121634816 | bytes 10849044 | tf_op jit(solution)/shard_map/single_path/pallas_call | solution.py:216
  6.2 10.7 %all_to_all.5.blocks = bf16[16,16,128]{2,1,0:T(8,128)(2,1)S(1)} all-to-all(bf16[16,16,128]{2,1,0:T(8,128)(2,1)S(1)} %get-tuple-element.8), channel_id=1, replica_groups={{15,0,1,2,3,4,5,6,7,8,9,10,11,12,13,14},{31,16,17,18,19,20,21,22,23,24,..., dimensions={0} | all-to-all | bytes 131072 | tf_op jit(solution)/shard_map/all_to_all | solution.py:318
  16.9 1.4 %pair_rows.1 = (bf16[16,1024]{1,0:T(8,128)(2,1)}, bf16[16,256,128]{2,1,0:T(8,128)(2,1)}) custom-call(bf16[16,16,128]{2,1,0:T(8,128)(2,1)S(1)} %all_to_all.5.blocks, bf16[16,128]{1,0:T(8,128)(2,1)S(1)} %get-tuple-element.9.queries, f32[16,256,128]{2,1,0:T(8,128)S(1)} %get-tuple-element.10.first, bf16[128,128]{1,0:T(8,128)(2,1)S(1)} %get-tuple-element.11.right, ...), custom_call_target="tpu_custom_call" | custom-call | flops 134217728 | bytes 3145728 | tf_op jit(solution)/shard_map/pair_rows/pallas_call | solution.py:264

commit v20 on v18

--- a/solution.py
+++ b/solution.py
@@ -68,13 +68,14 @@
     inner_dim = qk.shape[1] // 2
 
     small = [
-        (mix_hbm, mix), (tokens_hbm, tokens), (residue_hbm, residue),
-        (norm_gain_hbm, norm_gain), (norm_bias_hbm, norm_bias),
-        (proj_in_bias_hbm, proj_in_bias), (proj_out_bias_hbm, proj_out_bias),
-        (pair_gain_hbm, pair_gain), (pair_bias_hbm, pair_bias),
-        (qk_hbm, qk), (qk_bias_hbm, qk_bias), (chain_hbm, chain), (bins_hbm, bins),
-        (pair_weight_hbm, pair_weight), (relpos_hbm, relpos), (chain_table_hbm, chain_table),
-    ]
+        (bins_hbm, bins), (relpos_hbm, relpos), (chain_table_hbm, chain_table),
+        (pair_weight_hbm, pair_weight), (chain_hbm, chain), (mix_hbm, mix),
+        (norm_gain_hbm, norm_gain), (norm_bias_hbm, norm_bias), (tokens_hbm, tokens),
+        (residue_hbm, residue), (proj_in_bias_hbm, proj_in_bias),
+        (proj_out_bias_hbm, proj_out_bias), (pair_gain_hbm, pair_gain),
+        (pair_bias_hbm, pair_bias), (qk_hbm, qk), (qk_bias_hbm, qk_bias),
+    ]
+    first_small = 6
     small = [
         pltpu.make_async_copy(source, target, sem_small.at[at])
         for at, (source, target) in enumerate(small)
@@ -99,15 +100,24 @@
         )
         for at, (low, size) in enumerate(out_pieces)
     ]
-    small[0].start()
-    states[0].start()
-    for copy in small[1:] + states[1:]:
+    for copy in small[:first_small] + states + small[first_small:]:
         copy.start()
     for copy in firsts + seconds:
         copy.start(priority=1)
 
+    for copy in small[:first_small]:
+        copy.wait()
+    bins_col = operand_rows(
+        bins, pair_weight, relpos, chain_table, bin_rows, right, minus, tok_count
+    )
+    bin_table = bin_rows[...].astype(BF16)
+    lanes = lax.broadcasted_iota(jnp.int32, (bins_col.shape[0], bin_table.shape[0]), 1)
+    for row in range(tok_count):
+        onehot = jnp.where(bins_col[:, row:row + 1] == lanes, 1.0, 0.0).astype(BF16)
+        first[row] = jnp.dot(onehot, bin_table, preferred_element_type=F32)
+    flags = chain_flags(chain, tok_count, inner_dim)
+
     width = mixture.shape[1]
-    small[0].wait()
     shift = sums = squares = None
     for at, (low, size) in enumerate(in_pieces):
         states[at].wait()
@@ -124,12 +134,8 @@
             sums = part if sums is None else sums + part
             squares = part * part if squares is None else squares + part * part
         if at == min(1, len(in_pieces) - 1):
-            for copy in small[1:]:
+            for copy in small[first_small:]:
                 copy.wait()
-            bins_col = operand_rows(
-                bins, pair_weight, relpos, chain_table, bin_rows, right, minus, tok_count
-            )
-            flags = chain_flags(chain, tok_count, inner_dim)
             for row in range(tok_count):
                 residue_rows[pl.ds(row, 1), :] = residue[pl.ds(tokens[row], 1), :]
 
@@ -138,9 +144,6 @@
     mean = shift + offset
     scale = lax.rsqrt(jnp.maximum(spread, 0.0) + epsilon)
     gain, bias = norm_gain[...].reshape(1, width), norm_bias[...].reshape(1, width)
-    bin_table = bin_rows[...].astype(BF16)
-    lanes = lax.broadcasted_iota(jnp.int32, (bins_col.shape[0], bin_table.shape[0]), 1)
-    row_pieces = pieces(tok_count, max(1, len(in_pieces) - 1))
     total = None
     for at, (low, size) in enumerate(in_pieces):
         span = slice(low, low + size)
@@ -148,10 +151,6 @@
         firsts[at].wait()
         term = jnp.dot(normed, proj_in[pl.ds(low, size), :], preferred_element_type=F32)
         total = term if total is None else total + term
-        if at < len(row_pieces):
-            for row in range(row_pieces[at][0], sum(row_pieces[at])):
-                onehot = jnp.where(bins_col[:, row:row + 1] == lanes, 1.0, 0.0).astype(BF16)
-                first[row] = jnp.dot(onehot, bin_table, preferred_element_type=F32)
     middle = jnp.maximum(total + proj_in_bias[...], 0.0).astype(BF16)
 
     total = None

time: 18.3 us -> 18.3 us (level)
  no operation moved by 1% of the time
where the time goes in v20:
time: 18.3 us; the launch traced here: 18 us
  blocking collectives  10.7 us (58%)
  Pallas kernels  6.7 us (37%)
  between operations  0.65 us (4%)
    all_to_all x1, blocking collectives, shards(): lax.all_to_all(copies, 'seq', split_axis=0, concat_axis=0, axis_index_gro...  10.7 us
    pallas_call x1, Pallas kernels, single_part(): pl.pallas_call(functools.partial(single_kernel, plan), out_shape=(jax.Sha...  5.35 us
    pallas_call x1, Pallas kernels, pair_part(): pl.pallas_call(pair_kernel, out_shape=(jax.ShapeDtypeStruct(single.shape,...  1.35 us

profile of v20, /device:TPU:0, one launch (start us, length us, event | category | flops | bytes accessed | tf_op | source)
XLA Modules:
  0.0 18.0 jit_solution(4937970017785196666)
XLA Ops:
  0.6 5.3 %single_path.1 = (bf16[16,1024]{1,0:T(8,128)(2,1)S(1)}, bf16[16,128]{1,0:T(8,128)(2,1)S(1)}, bf16[16,16,128]{2,1,0:T(8,128)(2,1)S(1)}, f32[16,256,128]{2,1,0:T(8...) custom-call(bf16[37,16,2560]{2,1,0:T(8,128)(2,1)} %hidden_hbm.1, f32[37]{0:T(128)} %mix_hbm.1, ...), custom_call_target="tpu_custom_call" | custom-call | flops 121634816 | bytes 10849044 | tf_op jit(solution)/shard_map/single_path/pallas_call | solution.py:207
  6.0 10.7 %all_to_all.5.blocks = bf16[16,16,128]{2,1,0:T(8,128)(2,1)S(1)} all-to-all(bf16[16,16,128]{2,1,0:T(8,128)(2,1)S(1)} %get-tuple-element.8), channel_id=1, replica_groups={{15,0,1,2,3,4,5,6,7,8,9,10,11,12,13,14},{31,16,17,18,19,20,21,22,23,24,..., dimensions={0} | all-to-all | bytes 131072 | tf_op jit(solution)/shard_map/all_to_all | solution.py:309
  16.7 1.4 %pair_rows.1 = (bf16[16,1024]{1,0:T(8,128)(2,1)}, bf16[16,256,128]{2,1,0:T(8,128)(2,1)}) custom-call(bf16[16,16,128]{2,1,0:T(8,128)(2,1)S(1)} %all_to_all.5.blocks, bf16[16,128]{1,0:T(8,128)(2,1)S(1)} %get-tuple-element.9.queries, f32[16,256,128]{2,1,0:T(8,128)S(1)} %get-tuple-element.10.first, bf16[128,128]{1,0:T(8,128)(2,1)S(1)} %get-tuple-element.11.right, ...), custom_call_target="tpu_custom_call" | custom-call | flops 134217728 | bytes 3145728 | tf_op jit(solution)/shard_map/pair_rows/pallas_call | solution.py:255

commit v21 on v20

--- a/solution.py
+++ b/solution.py
@@ -137,7 +137,9 @@
             for copy in small[first_small:]:
                 copy.wait()
             for row in range(tok_count):
-                residue_rows[pl.ds(row, 1), :] = residue[pl.ds(tokens[row], 1), :]
+                residue_rows[pl.ds(row, 1), :] = (
+                    residue[pl.ds(tokens[row], 1), :] + proj_out_bias[...]
+                )
 
     offset = jnp.sum(sums, axis=1, keepdims=True) / width
     spread = jnp.sum(squares, axis=1, keepdims=True) / width - offset * offset
@@ -160,7 +162,7 @@
             middle[:, low:low + size], proj_out[pl.ds(low, size), :], preferred_element_type=F32
         )
         total = term if total is None else total + term
-    single_f = total + proj_out_bias[...] + residue_rows[...]
+    single_f = total + residue_rows[...]
     single[...] = single_f.astype(BF16)
 
     pair_in = row_norm(single_f, pair_gain[...], pair_bias[...]).astype(BF16)
@@ -182,7 +184,7 @@
     lanes = qk.shape[1]
     table_rows = -(-relpos.shape[0] // 128) * 128
     vmem = pl.BlockSpec(memory_space=pltpu.VMEM)
-    plan = (pieces(width, 5), pieces(channels, 2))
+    plan = (pieces(width, 5), pieces(channels, 4))
     args = (
         hidden, mix, norm_gain, norm_bias, proj_in, proj_in_bias[None],
         proj_out, proj_out_bias[None], tokens, residue, pair_gain[None], pair_bias[None],

time: 18.3 us -> 18.5 us (1.011)
  no operation moved by 1% of the time
where the time goes in v21:
time: 18.5 us; the launch traced here: 18.2 us
  blocking collectives  10.7 us (58%)
  Pallas kernels  6.84 us (37%)
  between operations  0.65 us (4%)
    all_to_all x1, blocking collectives, shards(): lax.all_to_all(copies, 'seq', split_axis=0, concat_axis=0, axis_index_gro...  10.7 us
    pallas_call x1, Pallas kernels, single_part(): pl.pallas_call(functools.partial(single_kernel, plan), out_shape=(jax.Sha...  5.49 us
    pallas_call x1, Pallas kernels, pair_part(): pl.pallas_call(pair_kernel, out_shape=(jax.ShapeDtypeStruct(single.shape,...  1.35 us

profile of v21, /device:TPU:0, one launch (start us, length us, event | category | flops | bytes accessed | tf_op | source)
XLA Modules:
  0.0 18.2 jit_solution(16819260619101425888)
XLA Ops:
  0.6 5.5 %single_path.1 = (bf16[16,1024]{1,0:T(8,128)(2,1)S(1)}, bf16[16,128]{1,0:T(8,128)(2,1)S(1)}, bf16[16,16,128]{2,1,0:T(8,128)(2,1)S(1)}, f32[16,256,128]{2,1,0:T(8...) custom-call(bf16[37,16,2560]{2,1,0:T(8,128)(2,1)} %hidden_hbm.1, f32[37]{0:T(128)} %mix_hbm.1, ...), custom_call_target="tpu_custom_call" | custom-call | flops 121634816 | bytes 10849044 | tf_op jit(solution)/shard_map/single_path/pallas_call | solution.py:209
  6.1 10.7 %all_to_all.5.blocks = bf16[16,16,128]{2,1,0:T(8,128)(2,1)S(1)} all-to-all(bf16[16,16,128]{2,1,0:T(8,128)(2,1)S(1)} %get-tuple-element.8), channel_id=1, replica_groups={{15,0,1,2,3,4,5,6,7,8,9,10,11,12,13,14},{31,16,17,18,19,20,21,22,23,24,..., dimensions={0} | all-to-all | bytes 131072 | tf_op jit(solution)/shard_map/all_to_all | solution.py:311
  16.8 1.4 %pair_rows.1 = (bf16[16,1024]{1,0:T(8,128)(2,1)}, bf16[16,256,128]{2,1,0:T(8,128)(2,1)}) custom-call(bf16[16,16,128]{2,1,0:T(8,128)(2,1)S(1)} %all_to_all.5.blocks, bf16[16,128]{1,0:T(8,128)(2,1)S(1)} %get-tuple-element.9.queries, f32[16,256,128]{2,1,0:T(8,128)S(1)} %get-tuple-element.10.first, bf16[128,128]{1,0:T(8,128)(2,1)S(1)} %get-tuple-element.11.right, ...), custom_call_target="tpu_custom_call" | custom-call | flops 134217728 | bytes 3145728 | tf_op jit(solution)/shard_map/pair_rows/pallas_call | solution.py:257

commit v22 on v20

--- a/solution.py
+++ b/solution.py
@@ -145,10 +145,14 @@
     scale = lax.rsqrt(jnp.maximum(spread, 0.0) + epsilon)
     gain, bias = norm_gain[...].reshape(1, width), norm_bias[...].reshape(1, width)
     total = None
-    for at, (low, size) in enumerate(in_pieces):
+    half = -(-len(in_pieces) // 2)
+    for group in (range(0, half), range(half, len(in_pieces))):
+        low = in_pieces[group[0]][0]
+        size = sum(in_pieces[group[-1]]) - low
         span = slice(low, low + size)
         normed = ((mixture[:, span] - mean) * scale * gain[:, span] + bias[:, span]).astype(BF16)
-        firsts[at].wait()
+        for at in group:
+            firsts[at].wait()
         term = jnp.dot(normed, proj_in[pl.ds(low, size), :], preferred_element_type=F32)
         total = term if total is None else total + term
     middle = jnp.maximum(total + proj_in_bias[...], 0.0).astype(BF16)
@@ -182,7 +186,7 @@
     lanes = qk.shape[1]
     table_rows = -(-relpos.shape[0] // 128) * 128
     vmem = pl.BlockSpec(memory_space=pltpu.VMEM)
-    plan = (pieces(width, 5), pieces(channels, 2))
+    plan = (pieces(width, 5), pieces(channels, 1))
     args = (
         hidden, mix, norm_gain, norm_bias, proj_in, proj_in_bias[None],
         proj_out, proj_out_bias[None], tokens, residue, pair_gain[None], pair_bias[None],

time: 18.3 us -> 18.4 us (level)
  no operation moved by 1% of the time
where the time goes in v22:
time: 18.4 us; the launch traced here: 18.2 us
  blocking collectives  10.7 us (58%)
  Pallas kernels  6.85 us (37%)
  between operations  0.65 us (4%)
    all_to_all x1, blocking collectives, shards(): lax.all_to_all(copies, 'seq', split_axis=0, concat_axis=0, axis_index_gro...  10.7 us
    pallas_call x1, Pallas kernels, single_part(): pl.pallas_call(functools.partial(single_kernel, plan), out_shape=(jax.Sha...  5.5 us
    pallas_call x1, Pallas kernels, pair_part(): pl.pallas_call(pair_kernel, out_shape=(jax.ShapeDtypeStruct(single.shape,...  1.35 us

profile of v22, /device:TPU:0, one launch (start us, length us, event | category | flops | bytes accessed | tf_op | source)
XLA Modules:
  0.0 18.2 jit_solution(17193042472698766123)
XLA Ops:
  0.6 5.5 %single_path.1 = (bf16[16,1024]{1,0:T(8,128)(2,1)S(1)}, bf16[16,128]{1,0:T(8,128)(2,1)S(1)}, bf16[16,16,128]{2,1,0:T(8,128)(2,1)S(1)}, f32[16,256,128]{2,1,0:T(8...) custom-call(bf16[37,16,2560]{2,1,0:T(8,128)(2,1)} %hidden_hbm.1, f32[37]{0:T(128)} %mix_hbm.1, ...), custom_call_target="tpu_custom_call" | custom-call | flops 121634816 | bytes 10849044 | tf_op jit(solution)/shard_map/single_path/pallas_call | solution.py:211
  6.1 10.7 %all_to_all.5.blocks = bf16[16,16,128]{2,1,0:T(8,128)(2,1)S(1)} all-to-all(bf16[16,16,128]{2,1,0:T(8,128)(2,1)S(1)} %get-tuple-element.8), channel_id=1, replica_groups={{15,0,1,2,3,4,5,6,7,8,9,10,11,12,13,14},{31,16,17,18,19,20,21,22,23,24,..., dimensions={0} | all-to-all | bytes 131072 | tf_op jit(solution)/shard_map/all_to_all | solution.py:313
  16.8 1.4 %pair_rows.1 = (bf16[16,1024]{1,0:T(8,128)(2,1)}, bf16[16,256,128]{2,1,0:T(8,128)(2,1)}) custom-call(bf16[16,16,128]{2,1,0:T(8,128)(2,1)S(1)} %all_to_all.5.blocks, bf16[16,128]{1,0:T(8,128)(2,1)S(1)} %get-tuple-element.9.queries, f32[16,256,128]{2,1,0:T(8,128)S(1)} %get-tuple-element.10.first, bf16[128,128]{1,0:T(8,128)(2,1)S(1)} %get-tuple-element.11.right, ...), custom_call_target="tpu_custom_call" | custom-call | flops 134217728 | bytes 3145728 | tf_op jit(solution)/shard_map/pair_rows/pallas_call | solution.py:259

commit v23 on v20

--- a/solution.py
+++ b/solution.py
@@ -61,7 +61,7 @@
     single, query_ref, copies_ref, first, right, minus,
     hidden, mix, norm_gain, norm_bias, proj_in, proj_in_bias, proj_out, proj_out_bias, tokens,
     residue, pair_gain, pair_bias, qk, qk_bias, chain, bins, pair_weight, relpos, chain_table,
-    mixture, residue_rows, bin_rows, sem_hidden, sem_in, sem_out, sem_small,
+    mixture, normed, residue_rows, bin_rows, sem_hidden, sem_in, sem_out, sem_small,
 ):
     in_pieces, out_pieces = plan
     tok_count = mixture.shape[0]
@@ -118,39 +118,55 @@
     flags = chain_flags(chain, tok_count, inner_dim)
 
     width = mixture.shape[1]
-    shift = sums = squares = None
-    for at, (low, size) in enumerate(in_pieces):
-        states[at].wait()
+    count, size = len(in_pieces), in_pieces[0][1]
+
+    def mixed(low):
         total = None
         for state in range(hidden.shape[0]):
-            term = mix[state] * hidden[state, :, low:low + size].astype(F32)
+            term = mix[state] * hidden[state, :, pl.ds(low, size)].astype(F32)
             total = term if total is None else total + term
-        mixture[:, low:low + size] = total
-        if shift is None:
-            shift = jnp.mean(total, axis=1, keepdims=True)
-        total = total - shift
-        for lane in range(0, size, 128):
-            part = total[:, lane:lane + 128]
-            sums = part if sums is None else sums + part
-            squares = part * part if squares is None else squares + part * part
-        if at == min(1, len(in_pieces) - 1):
-            for copy in small[first_small:]:
-                copy.wait()
-            for row in range(tok_count):
-                residue_rows[pl.ds(row, 1), :] = residue[pl.ds(tokens[row], 1), :]
-
+        mixture[:, pl.ds(low, size)] = total
+        return total
+
+    def sums_of(values):
+        parts = [values[:, lane:lane + 128] for lane in range(0, size, 128)]
+        return sum(parts[1:], parts[0]), sum([part * part for part in parts[1:]], parts[0] ** 2)
+
+    states[0].wait()
+    total = mixed(0)
+    shift = jnp.mean(total, axis=1, keepdims=True)
+    first_sums = sums_of(total - shift)
+    for copy in small[first_small:]:
+        copy.wait()
+    for row in range(tok_count):
+        residue_rows[pl.ds(row, 1), :] = residue[pl.ds(tokens[row], 1), :]
+
+    def mixture_step(at, carry):
+        low = pl.multiple_of(at * size, size)
+        columns = pl.ds(low, size)
+        pltpu.make_async_copy(
+            hidden_hbm.at[:, :, columns], hidden.at[:, :, columns], sem_hidden.at[at]
+        ).wait()
+        sums, squares = sums_of(mixed(low) - shift)
+        return carry[0] + sums, carry[1] + squares
+
+    sums, squares = lax.fori_loop(1, count, mixture_step, first_sums)
     offset = jnp.sum(sums, axis=1, keepdims=True) / width
     spread = jnp.sum(squares, axis=1, keepdims=True) / width - offset * offset
     mean = shift + offset
     scale = lax.rsqrt(jnp.maximum(spread, 0.0) + epsilon)
     gain, bias = norm_gain[...].reshape(1, width), norm_bias[...].reshape(1, width)
-    total = None
-    for at, (low, size) in enumerate(in_pieces):
-        span = slice(low, low + size)
-        normed = ((mixture[:, span] - mean) * scale * gain[:, span] + bias[:, span]).astype(BF16)
-        firsts[at].wait()
-        term = jnp.dot(normed, proj_in[pl.ds(low, size), :], preferred_element_type=F32)
-        total = term if total is None else total + term
+    normed[...] = ((mixture[...] - mean) * scale * gain + bias).astype(BF16)
+
+    def product_step(at, total):
+        low = pl.multiple_of(at * size, size)
+        rows = pl.ds(low, size)
+        pltpu.make_async_copy(proj_in_hbm.at[rows], proj_in.at[rows], sem_in.at[at]).wait()
+        return total + jnp.dot(normed[:, rows], proj_in[rows, :], preferred_element_type=F32)
+
+    total = lax.fori_loop(
+        0, count, product_step, jnp.zeros((tok_count, proj_in.shape[1]), F32)
+    )
     middle = jnp.maximum(total + proj_in_bias[...], 0.0).astype(BF16)
 
     total = None
@@ -182,7 +198,7 @@
     lanes = qk.shape[1]
     table_rows = -(-relpos.shape[0] // 128) * 128
     vmem = pl.BlockSpec(memory_space=pltpu.VMEM)
-    plan = (pieces(width, 5), pieces(channels, 2))
+    plan = (pieces(width, 5 if width % (5 * 128) == 0 else 1), pieces(channels, 2))
     args = (
         hidden, mix, norm_gain, norm_bias, proj_in, proj_in_bias[None],
         proj_out, proj_out_bias[None], tokens, residue, pair_gain[None], pair_bias[None],
@@ -196,6 +212,7 @@
     ]
     scratch += [
         pltpu.VMEM((tok_count, width), F32),
+        pltpu.VMEM((tok_count, width), BF16),
         pltpu.VMEM((tok_count, channels), F32),
         pltpu.VMEM((table_rows, pair_weight.shape[1]), F32),
         pltpu.SemaphoreType.DMA((len(plan[0]),)),

time: 18.3 us -> 18.3 us (level)
  no operation moved by 1% of the time
where the time goes in v23:
time: 18.3 us; the launch traced here: 18 us
  blocking collectives  10.7 us (58%)
  Pallas kernels  6.7 us (37%)
  between operations  0.65 us (4%)
    all_to_all x1, blocking collectives, shards(): lax.all_to_all(copies, 'seq', split_axis=0, concat_axis=0, axis_index_gro...  10.7 us
    pallas_call x1, Pallas kernels, single_part(): pl.pallas_call(functools.partial(single_kernel, plan), out_shape=(jax.Sha...  5.34 us
    pallas_call x1, Pallas kernels, pair_part(): pl.pallas_call(pair_kernel, out_shape=(jax.ShapeDtypeStruct(single.shape,...  1.35 us

profile of v23, /device:TPU:0, one launch (start us, length us, event | category | flops | bytes accessed | tf_op | source)
XLA Modules:
  0.0 18.0 jit_solution(13619392105132427653)
XLA Ops:
  0.6 5.3 %single_path.1 = (bf16[16,1024]{1,0:T(8,128)(2,1)S(1)}, bf16[16,128]{1,0:T(8,128)(2,1)S(1)}, bf16[16,16,128]{2,1,0:T(8,128)(2,1)S(1)}, f32[16,256,128]{2,1,0:T(8...) custom-call(bf16[37,16,2560]{2,1,0:T(8,128)(2,1)} %hidden_hbm.1, f32[37]{0:T(128)} %mix_hbm.1, ...), custom_call_target="tpu_custom_call" | custom-call | flops 121634816 | bytes 10849044 | tf_op jit(solution)/shard_map/single_path/pallas_call | solution.py:224
  6.0 10.7 %all_to_all.5.blocks = bf16[16,16,128]{2,1,0:T(8,128)(2,1)S(1)} all-to-all(bf16[16,16,128]{2,1,0:T(8,128)(2,1)S(1)} %get-tuple-element.8), channel_id=1, replica_groups={{15,0,1,2,3,4,5,6,7,8,9,10,11,12,13,14},{31,16,17,18,19,20,21,22,23,24,..., dimensions={0} | all-to-all | bytes 131072 | tf_op jit(solution)/shard_map/all_to_all | solution.py:326
  16.7 1.4 %pair_rows.1 = (bf16[16,1024]{1,0:T(8,128)(2,1)}, bf16[16,256,128]{2,1,0:T(8,128)(2,1)}) custom-call(bf16[16,16,128]{2,1,0:T(8,128)(2,1)S(1)} %all_to_all.5.blocks, bf16[16,128]{1,0:T(8,128)(2,1)S(1)} %get-tuple-element.9.queries, f32[16,256,128]{2,1,0:T(8,128)S(1)} %get-tuple-element.10.first, bf16[128,128]{1,0:T(8,128)(2,1)S(1)} %get-tuple-element.11.right, ...), custom_call_target="tpu_custom_call" | custom-call | flops 134217728 | bytes 3145728 | tf_op jit(solution)/shard_map/pair_rows/pallas_call | solution.py:272

commit v24 on v20

--- a/solution.py
+++ b/solution.py
@@ -232,7 +232,10 @@
 ):
     single_copy = pltpu.make_async_copy(single, single_hbm, sem_single)
     single_copy.start()
-    keys = jnp.concatenate([blocks[1:].reshape(-1, blocks.shape[2]), blocks[0]], axis=0)
+    last = blocks.shape[0] - 1
+    keys = jnp.concatenate(
+        [blocks[1:last].reshape(-1, blocks.shape[2]), blocks[0], blocks[last]], axis=0
+    )
     row_diff = jnp.dot(queries[...], minus[...], preferred_element_type=F32)
     col_diff = jnp.dot(keys, minus[...], preferred_element_type=F32)
     copies = []
@@ -305,7 +308,7 @@
             qk_weight, qk_bias, chain_ids, relpos_bins, pair_weight, relpos_table, chain_table,
         ),
     )
-    order = [device_count - 1] + list(range(device_count - 1))
+    order = [device_count - 2] + list(range(device_count - 2)) + [device_count - 1]
     blocks = lax.all_to_all(
         copies, "seq", split_axis=0, concat_axis=0, axis_index_groups=[order]
     )

time: 18.3 us -> 18.7 us (1.022)
  blocking collectives: 10.7 us -> 11 us
    all_to_all x1, blocking collectives: 10.7 us -> 11 us  [shards(): lax.all_to_all(copies, 'seq', split_axis=0, concat_axis=0, axis_index_gro...]
where the time goes in v24:
time: 18.7 us; the launch traced here: 18.4 us
  blocking collectives  11 us (59%)
  Pallas kernels  6.7 us (36%)
  between operations  0.65 us (3%)
    all_to_all x1, blocking collectives, shards(): lax.all_to_all(copies, 'seq', split_axis=0, concat_axis=0, axis_index_gro...  11 us
    pallas_call x1, Pallas kernels, single_part(): pl.pallas_call(functools.partial(single_kernel, plan), out_shape=(jax.Sha...  5.35 us
    pallas_call x1, Pallas kernels, pair_part(): pl.pallas_call(pair_kernel, out_shape=(jax.ShapeDtypeStruct(single.shape,...  1.35 us

profile of v24, /device:TPU:0, one launch (start us, length us, event | category | flops | bytes accessed | tf_op | source)
XLA Modules:
  0.0 18.4 jit_solution(5852908304460351784)
XLA Ops:
  0.6 5.3 %single_path.1 = (bf16[16,1024]{1,0:T(8,128)(2,1)S(1)}, bf16[16,128]{1,0:T(8,128)(2,1)S(1)}, bf16[16,16,128]{2,1,0:T(8,128)(2,1)S(1)}, f32[16,256,128]{2,1,0:T(8...) custom-call(bf16[37,16,2560]{2,1,0:T(8,128)(2,1)} %hidden_hbm.1, f32[37]{0:T(128)} %mix_hbm.1, ...), custom_call_target="tpu_custom_call" | custom-call | flops 121634816 | bytes 10849044 | tf_op jit(solution)/shard_map/single_path/pallas_call | solution.py:207
  6.0 11.0 %all_to_all.5.blocks = bf16[16,16,128]{2,1,0:T(8,128)(2,1)S(1)} all-to-all(bf16[16,16,128]{2,1,0:T(8,128)(2,1)S(1)} %get-tuple-element.8), channel_id=1, replica_groups={{14,0,1,2,3,4,5,6,7,8,9,10,11,12,13,15},{30,16,17,18,19,20,21,22,23,24,..., dimensions={0} | all-to-all | bytes 131072 | tf_op jit(solution)/shard_map/all_to_all | solution.py:312
  17.0 1.4 %pair_rows.1 = (bf16[16,1024]{1,0:T(8,128)(2,1)}, bf16[16,256,128]{2,1,0:T(8,128)(2,1)}) custom-call(bf16[16,16,128]{2,1,0:T(8,128)(2,1)S(1)} %all_to_all.5.blocks, bf16[16,128]{1,0:T(8,128)(2,1)S(1)} %get-tuple-element.9.queries, f32[16,256,128]{2,1,0:T(8,128)S(1)} %get-tuple-element.10.first, bf16[128,128]{1,0:T(8,128)(2,1)S(1)} %get-tuple-element.11.right, ...), custom_call_target="tpu_custom_call" | custom-call | flops 134217728 | bytes 3145728 | tf_op jit(solution)/shard_map/pair_rows/pallas_call | solution.py:258

commit v25 on v20

--- a/solution.py
+++ b/solution.py
@@ -236,12 +236,17 @@
     row_diff = jnp.dot(queries[...], minus[...], preferred_element_type=F32)
     col_diff = jnp.dot(keys, minus[...], preferred_element_type=F32)
     copies = []
-    for row in range(first.shape[0]):
-        products = keys * queries[row:row + 1, :]
-        value = jnp.dot(products, right[...], preferred_element_type=F32)
-        value = value + first[row] + (row_diff[row:row + 1, :] - col_diff)
-        pair[row] = value.astype(BF16)
-        copy = pltpu.make_async_copy(pair.at[row], pair_hbm.at[row], sem.at[row])
+    tok_count, col_count, channels = first.shape
+    for at, (low, size) in enumerate(pieces(tok_count, tok_count // 2)):
+        products = [keys * queries[row:row + 1, :] for row in range(low, low + size)]
+        value = jnp.dot(
+            jnp.concatenate(products, axis=0), right[...], preferred_element_type=F32
+        ).reshape(size, col_count, channels)
+        for row in range(low, low + size):
+            rest = first[row] + (row_diff[row:row + 1, :] - col_diff)
+            pair[row] = (value[row - low] + rest).astype(BF16)
+        rows = pl.ds(low, size)
+        copy = pltpu.make_async_copy(pair.at[rows], pair_hbm.at[rows], sem.at[at])
         copy.start()
         copies.append(copy)
     for copy in copies:

time: 18.3 us -> 18.4 us (level)
  no operation moved by 1% of the time
where the time goes in v25:
time: 18.4 us; the launch traced here: 18.1 us
  blocking collectives  10.7 us (58%)
  Pallas kernels  6.78 us (37%)
  between operations  0.65 us (4%)
    all_to_all x1, blocking collectives, shards(): lax.all_to_all(copies, 'seq', split_axis=0, concat_axis=0, axis_index_gro...  10.7 us
    pallas_call x1, Pallas kernels, single_part(): pl.pallas_call(functools.partial(single_kernel, plan), out_shape=(jax.Sha...  5.35 us
    pallas_call x1, Pallas kernels, pair_part(): pl.pallas_call(pair_kernel, out_shape=(jax.ShapeDtypeStruct(single.shape,...  1.43 us

profile of v25, /device:TPU:0, one launch (start us, length us, event | category | flops | bytes accessed | tf_op | source)
XLA Modules:
  0.0 18.1 jit_solution(16600551798122380517)
XLA Ops:
  0.6 5.3 %single_path.1 = (bf16[16,1024]{1,0:T(8,128)(2,1)S(1)}, bf16[16,128]{1,0:T(8,128)(2,1)S(1)}, bf16[16,16,128]{2,1,0:T(8,128)(2,1)S(1)}, f32[16,256,128]{2,1,0:T(8...) custom-call(bf16[37,16,2560]{2,1,0:T(8,128)(2,1)} %hidden_hbm.1, f32[37]{0:T(128)} %mix_hbm.1, ...), custom_call_target="tpu_custom_call" | custom-call | flops 121634816 | bytes 10849044 | tf_op jit(solution)/shard_map/single_path/pallas_call | solution.py:207
  6.0 10.7 %all_to_all.5.blocks = bf16[16,16,128]{2,1,0:T(8,128)(2,1)S(1)} all-to-all(bf16[16,16,128]{2,1,0:T(8,128)(2,1)S(1)} %get-tuple-element.8), channel_id=1, replica_groups={{15,0,1,2,3,4,5,6,7,8,9,10,11,12,13,14},{31,16,17,18,19,20,21,22,23,24,..., dimensions={0} | all-to-all | bytes 131072 | tf_op jit(solution)/shard_map/all_to_all | solution.py:314
  16.7 1.4 %pair_rows.1 = (bf16[16,1024]{1,0:T(8,128)(2,1)}, bf16[16,256,128]{2,1,0:T(8,128)(2,1)}) custom-call(bf16[16,16,128]{2,1,0:T(8,128)(2,1)S(1)} %all_to_all.5.blocks, bf16[16,128]{1,0:T(8,128)(2,1)S(1)} %get-tuple-element.9.queries, f32[16,256,128]{2,1,0:T(8,128)S(1)} %get-tuple-element.10.first, bf16[128,128]{1,0:T(8,128)(2,1)S(1)} %get-tuple-element.11.right, ...), custom_call_target="tpu_custom_call" | custom-call | flops 134217728 | bytes 3145728 | tf_op jit(solution)/shard_map/pair_rows/pallas_call | solution.py:260

commit v26 on v20

--- a/solution.py
+++ b/solution.py
@@ -233,13 +233,14 @@
     single_copy = pltpu.make_async_copy(single, single_hbm, sem_single)
     single_copy.start()
     keys = jnp.concatenate([blocks[1:].reshape(-1, blocks.shape[2]), blocks[0]], axis=0)
-    row_diff = jnp.dot(queries[...], minus[...], preferred_element_type=F32)
-    col_diff = jnp.dot(keys, minus[...], preferred_element_type=F32)
+    query_rows = queries[...]
+    row_diff = jnp.dot(query_rows, minus[...], preferred_element_type=F32)
+    both = jnp.concatenate([right[...], -minus[...]], axis=0)
     copies = []
     for row in range(first.shape[0]):
-        products = keys * queries[row:row + 1, :]
-        value = jnp.dot(products, right[...], preferred_element_type=F32)
-        value = value + first[row] + (row_diff[row:row + 1, :] - col_diff)
+        products = jnp.concatenate([keys * query_rows[row:row + 1, :], keys], axis=1)
+        value = jnp.dot(products, both, preferred_element_type=F32)
+        value = value + first[row] + row_diff[row:row + 1, :]
         pair[row] = value.astype(BF16)
         copy = pltpu.make_async_copy(pair.at[row], pair_hbm.at[row], sem.at[row])
         copy.start()

time: 18.3 us -> 18.4 us (level)
  no operation moved by 1% of the time
where the time goes in v26:
time: 18.4 us; the launch traced here: 18.2 us
  blocking collectives  10.7 us (58%)
  Pallas kernels  6.84 us (37%)
  between operations  0.65 us (4%)
    all_to_all x1, blocking collectives, shards(): lax.all_to_all(copies, 'seq', split_axis=0, concat_axis=0, axis_index_gro...  10.7 us
    pallas_call x1, Pallas kernels, single_part(): pl.pallas_call(functools.partial(single_kernel, plan), out_shape=(jax.Sha...  5.35 us
    pallas_call x1, Pallas kernels, pair_part(): pl.pallas_call(pair_kernel, out_shape=(jax.ShapeDtypeStruct(single.shape,...  1.49 us

profile of v26, /device:TPU:0, one launch (start us, length us, event | category | flops | bytes accessed | tf_op | source)
XLA Modules:
  0.0 18.2 jit_solution(2853076613605129312)
XLA Ops:
  0.6 5.3 %single_path.1 = (bf16[16,1024]{1,0:T(8,128)(2,1)S(1)}, bf16[16,128]{1,0:T(8,128)(2,1)S(1)}, bf16[16,16,128]{2,1,0:T(8,128)(2,1)S(1)}, f32[16,256,128]{2,1,0:T(8...) custom-call(bf16[37,16,2560]{2,1,0:T(8,128)(2,1)} %hidden_hbm.1, f32[37]{0:T(128)} %mix_hbm.1, ...), custom_call_target="tpu_custom_call" | custom-call | flops 121634816 | bytes 10849044 | tf_op jit(solution)/shard_map/single_path/pallas_call | solution.py:207
  6.0 10.7 %all_to_all.5.blocks = bf16[16,16,128]{2,1,0:T(8,128)(2,1)S(1)} all-to-all(bf16[16,16,128]{2,1,0:T(8,128)(2,1)S(1)} %get-tuple-element.8), channel_id=1, replica_groups={{15,0,1,2,3,4,5,6,7,8,9,10,11,12,13,14},{31,16,17,18,19,20,21,22,23,24,..., dimensions={0} | all-to-all | bytes 131072 | tf_op jit(solution)/shard_map/all_to_all | solution.py:310
  16.7 1.5 %pair_rows.1 = (bf16[16,1024]{1,0:T(8,128)(2,1)}, bf16[16,256,128]{2,1,0:T(8,128)(2,1)}) custom-call(bf16[16,16,128]{2,1,0:T(8,128)(2,1)S(1)} %all_to_all.5.blocks, bf16[16,128]{1,0:T(8,128)(2,1)S(1)} %get-tuple-element.9.queries, f32[16,256,128]{2,1,0:T(8,128)S(1)} %get-tuple-element.10.first, bf16[128,128]{1,0:T(8,128)(2,1)S(1)} %get-tuple-element.11.right, ...), custom_call_target="tpu_custom_call" | custom-call | flops 134217728 | bytes 3145728 | tf_op jit(solution)/shard_map/pair_rows/pallas_call | solution.py:256
